TPU v7x, 512 devices: a whole 4x8x8 slice. The times are simulated.
512 devices in a mesh: blk: 32 (over x, z_lo, core), narrow: 16 (over z_hi, y).
Axes of the slice: x: 4, y: 8, z: 8 (z_hi: 2, z_lo: 4; z = z_hi * 4 + z_lo), core: 2. Of those that a mesh axis runs over, the one named last changes fastest.
Arguments:
- user_factors: float32 [131072, 128], P(('blk', 'narrow')), may hold values from -2 to 2
- user_m: float32 [131072, 128], P(('blk', 'narrow')), may hold values from -1.75 to 1.75
- user_v: float32 [131072, 128], P(('blk', 'narrow')), may hold values from 0.05 to 1
- item_factors: float32 [131072, 128], P(('blk', 'narrow')), may hold values from -2 to 2
- item_m: float32 [131072, 128], P(('blk', 'narrow')), may hold values from -1.75 to 1.75
- item_v: float32 [131072, 128], P(('blk', 'narrow')), may hold values from 0.05 to 1
- ratings: bfloat16 [32, 16, 3, 36, 128, 128], P('blk', 'narrow'), may hold values from -6 to 6
- user_tiles: int32 [32, 16, 3, 36], P('blk', 'narrow'), may hold values from 0 to 1, as said below
- item_tiles: int32 [32, 16, 3, 36], P('blk', 'narrow'), may hold values from 0 to 31
- tile_counts: int32 [32, 16, 3], P('blk', 'narrow'), may hold values from 4 to 36, as said below
Outputs:
- new_user_factors: float32 [131072, 128], P(('blk', 'narrow'))
- new_user_m: float32 [131072, 128], P(('blk', 'narrow'))
- new_user_v: float32 [131072, 128], P(('blk', 'narrow'))
- new_item_factors: float32 [131072, 128], P(('blk', 'narrow'))
- new_item_m: float32 [131072, 128], P(('blk', 'narrow'))
- new_item_v: float32 [131072, 128], P(('blk', 'narrow'))
Inputs may be any that keep to these rules, and one draw needn't show every extreme that they name: Slots may name the same pair (user_tiles, item_tiles) more than once. Only the first tile_counts slots are live; in every sub-step some device has all 36 slots live.
All inputs are finite; a program needn't handle non-finite values.
Results may differ from a plain program's by a relative error of at most 0.02.
Values may be sent and summed in bfloat16 or wider, within the bound.
No kernel may reach another device: no remote copies, remote signals or barrier semaphores. Data moves between devices by JAX's collectives and lax.ppermute only.
A program may use at most 64 MiB of HBM per device.

v0:
```python
import jax
import jax.numpy as jnp
from jax import lax
from jax.sharding import PartitionSpec as P

K = 128
TILE = 128
MAXT = 36
STEPS = 3


LEARN_RATE = 0.01
BETA_ONE = 0.8
BETA_TWO = 0.95
ADAM_EPS = 1e-08
DECAY_REG = 0.05
GRAD_SCALE = 0.03125


def shifted(block, axis, distance):
    devices = range(lax.axis_size(axis))
    route = [((i - distance) % len(devices), i) for i in devices]
    return lax.ppermute(block, axis, route)


def adam_update(param, first, second, grad):
    first = BETA_ONE * first + (1.0 - BETA_ONE) * grad
    second = BETA_TWO * second + (1.0 - BETA_TWO) * grad * grad
    return (param - LEARN_RATE * first / (jnp.sqrt(second) + ADAM_EPS), first, second)


def slot_terms(user_bf, item_bf, rating_tiles, user_idx, item_idx, count):
    user_tiles_all = user_bf.shape[0] // TILE
    item_tiles_all = item_bf.shape[0] // TILE
    user_rows = user_bf.reshape(user_tiles_all, TILE, K)[user_idx]
    item_rows = item_bf.reshape(item_tiles_all, TILE, K)[item_idx]
    predicted = jnp.einsum("tak,tbk->tab", user_rows, item_rows, preferred_element_type=jnp.float32)
    live = (jnp.arange(MAXT) < count).astype(jnp.float32)
    errors = ((predicted - rating_tiles.astype(jnp.float32)) * live[:, None, None]).astype(
        jnp.bfloat16
    )
    user_part = jnp.einsum("tab,tbk->tak", errors, item_rows, preferred_element_type=jnp.float32)
    item_part = jnp.einsum("tab,tak->tbk", errors, user_rows, preferred_element_type=jnp.float32)
    user_select = (jnp.arange(user_tiles_all)[:, None] == user_idx[None, :]).astype(jnp.float32)
    user_grad = jnp.dot(
        user_select, user_part.reshape(MAXT, TILE * K), precision=lax.Precision.HIGHEST
    )
    return (user_grad.reshape(user_bf.shape[0], K), item_part.reshape(MAXT, TILE * K))


def select_rows(item_part, item_idx, start, count):
    tiles = count // TILE
    wanted = start // TILE + jnp.arange(tiles, dtype=jnp.int32)
    selector = (wanted[:, None] == item_idx[None, :]).astype(jnp.float32)
    return jnp.dot(selector, item_part, precision=lax.Precision.HIGHEST).reshape(count, K)


def per_device(
    user_factors,
    user_m,
    user_v,
    item_factors,
    item_m,
    item_v,
    ratings,
    user_tiles,
    item_tiles,
    tile_counts,
):
    user_fac, user_first, user_second = (user_factors, user_m, user_v)
    item_fac, item_first, item_second = (item_factors, item_m, item_v)
    for substep in range(STEPS):
        current_rows = lax.all_gather(item_fac.astype(jnp.bfloat16), "narrow", axis=0, tiled=True)
        block_rows = current_rows.shape[0]
        item_idx = item_tiles[0, 0, substep]
        user_grad, item_part = slot_terms(
            user_fac.astype(jnp.bfloat16),
            current_rows,
            ratings[0, 0, substep],
            user_tiles[0, 0, substep],
            item_idx,
            tile_counts[0, 0, substep],
        )
        user_fac, user_first, user_second = adam_update(
            user_fac, user_first, user_second, GRAD_SCALE * user_grad + DECAY_REG * user_fac
        )
        dense_part = select_rows(item_part, item_idx, 0, block_rows)
        item_total = lax.psum_scatter(
            dense_part.astype(jnp.bfloat16), "narrow", scatter_dimension=0, tiled=True
        ).astype(jnp.float32)
        item_fac, item_first, item_second = adam_update(
            item_fac, item_first, item_second, GRAD_SCALE * item_total + DECAY_REG * item_fac
        )
        if substep + 1 < STEPS:
            item_fac, item_first, item_second = shifted(
                (item_fac, item_first, item_second), "blk", -1
            )
    return (user_fac, user_first, user_second, item_fac, item_first, item_second)


def solution(mesh):
    return jax.shard_map(
        per_device,
        mesh=mesh,
        in_specs=(
            P(("blk", "narrow"), None),
            P(("blk", "narrow"), None),
            P(("blk", "narrow"), None),
            P(("blk", "narrow"), None),
            P(("blk", "narrow"), None),
            P(("blk", "narrow"), None),
            P("blk", "narrow", None, None, None, None),
            P("blk", "narrow", None, None),
            P("blk", "narrow", None, None),
            P("blk", "narrow", None),
        ),
        out_specs=(
            P(("blk", "narrow"), None),
            P(("blk", "narrow"), None),
            P(("blk", "narrow"), None),
            P(("blk", "narrow"), None),
            P(("blk", "narrow"), None),
            P(("blk", "narrow"), None),
        ),
        check_vma=False,
    )
```

profile of v0, /device:TPU:6, one launch (start us, length us, event | category | flops | bytes accessed | tf_op | source)
XLA Modules:
  0.0 990.9 jit_solution(6336794547997010671)
XLA Ops:
  7.2 1.5 convert_element_type.100
  8.8 0.9 convert_element_type.99
  9.7 1.2 fusion.25
  11.0 0.8 gather_fusion
  11.8 0.6 fusion.36
  12.4 0.6 compare_convert_fusion.2
  13.0 0.5 fusion.26
  13.5 0.5 slice_bitcast_fusion
  14.1 95.7 %all-gather.4.cloned.1.call-done = bf16[4096,128]{1,0:T(8,128)(2,1)} async-done(((bf16[256,128]{1,0:T(8,128)(2,1)}), bf16[4096,128]{1,0:T(8,128)(2,1)}) %all-gather.4.cloned.1.call-update) | async-done | bytes 1048592 | tf_op jit(solution)/shard_map/all_gather | solution.py:73
  109.8 2.0 gather_fusion.1
  111.8 2.2 fusion.5
  114.0 0.6 fusion.38
  114.6 0.3 pad.7
  114.8 1.5 copy.23
  116.3 1.2 convolution_convert_fusion.2
  117.6 1.3 convert_element_type.107
  119.0 215.4 %reduce-scatter.4.cloned.1.call-done = bf16[256,128]{1,0:T(8,128)(2,1)} async-done(((bf16[4096,128]{1,0:T(8,128)(2,1)}), bf16[256,128]{1,0:T(8,128)(2,1)}) %reduce-scatter.4.cloned.1.call-update) | async-done | bytes 65552 | tf_op jit(solution)/shard_map/reduce_scatter | solution.py:88
  334.4 1.8 divide_subtract_fusion.4
  336.2 1.9 collective-permute-start
  338.1 2.5 collective-permute-done
  340.6 0.7 copy-done.18
  341.2 0.6 convert_element_type.109
  342.1 1.2 compare_convert_fusion.1
  343.3 0.5 fusion.37
  344.1 1.5 copy.22
  345.6 1.0 convolution_multiply_fusion.2
  346.9 0.8 gather_fusion.2
  347.7 86.2 %all-gather.6.cloned.1.call-done = bf16[4096,128]{1,0:T(8,128)(2,1)} async-done(((bf16[256,128]{1,0:T(8,128)(2,1)}), bf16[4096,128]{1,0:T(8,128)(2,1)}) %all-gather.6.cloned.1.call-update) | async-done | bytes 1048592 | tf_op jit(solution)/shard_map/all_gather | solution.py:73
  433.9 2.0 gather_fusion.3
  435.9 2.2 fusion.3
  438.1 0.6 fusion.40
  439.0 1.5 copy.25
  440.5 1.2 convolution_convert_fusion.1
  441.8 1.3 convert_element_type.116
  443.1 1.9 collective-permute-start.1
  445.1 3.3 collective-permute-start.2
  448.4 2.8 collective-permute-done.2
  451.2 207.2 %reduce-scatter.6.cloned.1.call-done = bf16[256,128]{1,0:T(8,128)(2,1)} async-done(((bf16[4096,128]{1,0:T(8,128)(2,1)}), bf16[256,128]{1,0:T(8,128)(2,1)}) %reduce-scatter.6.cloned.1.call-update) | async-done | bytes 65552 | tf_op jit(solution)/shard_map/reduce_scatter | solution.py:88
  658.4 1.6 divide_subtract_fusion.2
  660.1 1.9 collective-permute-start.3
  662.0 2.5 collective-permute-done.3
  664.5 0.7 copy-done.16
  665.1 0.6 convert_element_type.118
  666.1 1.1 compare_convert_fusion
  667.2 0.5 fusion.39
  668.0 1.5 copy.24
  669.5 1.0 convolution_multiply_fusion.1
  670.7 0.9 fusion.34
  671.6 0.8 gather_fusion.4
  672.3 85.5 %all-gather.8.cloned.1.call-done = bf16[4096,128]{1,0:T(8,128)(2,1)} async-done(((bf16[256,128]{1,0:T(8,128)(2,1)}), bf16[4096,128]{1,0:T(8,128)(2,1)}) %all-gather.8.cloned.1.call-update) | async-done | bytes 1048592 | tf_op jit(solution)/shard_map/all_gather | solution.py:73
  757.9 2.0 gather_fusion.5
  759.9 2.2 fusion.1
  762.1 0.6 fusion.42
  763.0 1.5 copy.27
  764.5 1.2 convolution_convert_fusion
  765.7 1.3 convert_element_type.124
  767.1 1.9 collective-permute-start.4
  769.0 3.6 collective-permute-start.5
  772.6 0.5 fusion.41
  773.4 1.5 copy.26
  774.9 1.0 convolution_multiply_fusion
  776.1 0.9 divide_subtract_fusion.1
  777.0 205.4 %reduce-scatter.8.cloned.1.call-done = bf16[256,128]{1,0:T(8,128)(2,1)} async-done(((bf16[4096,128]{1,0:T(8,128)(2,1)}), bf16[256,128]{1,0:T(8,128)(2,1)}) %reduce-scatter.8.cloned.1.call-update) | async-done | bytes 65552 | tf_op jit(solution)/shard_map/reduce_scatter | solution.py:88
  982.5 1.6 divide_subtract_fusion
  (89 shorter events, 2.8 us)
Async XLA Ops:
  7.2 102.6 %all-gather.4.cloned.1.call-start = ((), (), s32[]{:S(2)}) async-start(), calls=%async_computation.3 | async-start | bytes 1114112 | tf_op jit(solution)/shard_map/all_gather | solution.py:73
  8.8 325.6 %reduce-scatter.4.cloned.1.call-start = ((), (), s32[]{:S(2)}) async-start(), calls=%async_computation.4 | async-start | bytes 1114112 | tf_op jit(solution)/shard_map/reduce_scatter | solution.py:88
  11.0 0.8 copy-start.23
  11.0 2.0 copy-start.21
  117.6 216.8 %copy-start.15 = (f32[256,128]{1,0:T(8,128)S(1)}, f32[256,128]{1,0:T(8,128)}, u32[]{:S(2)}) copy-start(f32[256,128]{1,0:T(8,128)} %param.13) | copy-start | bytes 393220
  118.9 224.4 %copy-start.22 = (s32[1,1,3,36]{3,1,2,0:T(1,128)S(1)}, s32[1,1,3,36]{3,1,2,0:T(1,128)}, u32[]{:S(2)}) copy-start(s32[1,1,3,36]{3,1,2,0:T(1,128)} %param.17) | copy-start | bytes 1300
  118.9 314.9 %all-gather.6.cloned.1.call-start = ((), (), s32[]{:S(2)}) async-start(), calls=%async_computation.5 | async-start | bytes 1114112 | tf_op jit(solution)/shard_map/all_gather | solution.py:73
  336.2 4.4 collective-permute-start
  340.6 0.7 copy-start.18
  341.9 316.6 %reduce-scatter.6.cloned.1.call-start = ((), (), s32[]{:S(2)}) async-start(), calls=%async_computation.6 | async-start | bytes 1114112 | tf_op jit(solution)/shard_map/reduce_scatter | solution.py:88
  345.6 1.2 copy-start
  345.6 1.2 copy-start.8
  345.6 1.2 copy-start.11
  346.8 0.9 copy-start.3
  433.9 2.0 copy-start.28
  439.0 1.5 copy-start.27
  441.7 216.7 %copy-start.19 = (f32[256,128]{1,0:T(8,128)S(1)}, f32[256,128]{1,0:T(8,128)}, u32[]{:S(2)}) copy-start(f32[256,128]{1,0:T(8,128)} %copy-done.18) | copy-start | bytes 393220
  443.1 224.1 %copy-start.25 = (s32[36]{0:T(128)S(1)}, s32[36]{0:T(128)}, u32[]{:S(2)}) copy-start(s32[36]{0:T(128)} %get-tuple-element.26) | copy-start | bytes 436
  443.1 224.1 %copy-start.24 = (s32[36]{0:T(128)S(1)}, s32[36]{0:T(128)}, u32[]{:S(2)}) copy-start(s32[36]{0:T(128)} %get-tuple-element.29) | copy-start | bytes 436
  443.1 314.7 %all-gather.8.cloned.1.call-start = ((), (), s32[]{:S(2)}) async-start(), calls=%async_computation.7 | async-start | bytes 1114112 | tf_op jit(solution)/shard_map/all_gather | solution.py:73
  443.1 5.3 collective-permute-start.1
  445.1 6.2 collective-permute-start.2
  660.1 4.4 collective-permute-start.3
  664.5 0.7 copy-start.16
  665.8 316.6 %reduce-scatter.8.cloned.1.call-start = ((), (), s32[]{:S(2)}) async-start(), calls=%async_computation.8 | async-start | bytes 1114112 | tf_op jit(solution)/shard_map/reduce_scatter | solution.py:88
  669.5 1.2 copy-start.1
  669.5 1.2 copy-start.4
  669.5 1.2 copy-start.9
  669.5 1.2 copy-start.12
  670.7 1.7 copy-start.6
  757.9 2.0 copy-start.29
  762.9 1.5 copy-start.26
  765.7 3.3 copy-start.20
  767.1 10.0 %collective-permute-start.4 = (f32[256,128]{1,0:T(8,128)}, f32[256,128]{1,0:T(8,128)S(1)}, u32[]{:S(2)}, u32[]{:S(2)}) collective-permute-start(f32[256,128]{1,0:T(8,128)} %get-tuple-element.13), channel_id=1, source_target_pairs={{16,0},{32,16},{48,32},{64,48},{80,64},{96,80},{112,96},{128,112},... | collective-permute-start | bytes 393224 | tf_op jit(solution)/shard_map/ppermute | solution.py:23
  769.0 8.0 collective-permute-start.5
  774.9 1.2 copy-start.2
  774.9 1.2 copy-start.5
  774.9 1.2 copy-start.7
  774.9 1.2 copy-start.10
  774.9 1.2 copy-start.13
  774.9 1.2 copy-start.14
  775.9 206.5 %copy-start.17 = (f32[256,128]{1,0:T(8,128)S(1)}, f32[256,128]{1,0:T(8,128)}, u32[]{:S(2)}) copy-start(f32[256,128]{1,0:T(8,128)} %copy-done.16) | copy-start | bytes 393220
Sparse Core Ops, SparseCore 0:
  11.8 97.9 all-gather.3
  119.1 215.2 reduce-scatter.3
  342.0 91.8 all-gather.5
  443.2 215.1 reduce-scatter.5
  665.9 91.8 all-gather.7
  767.2 215.2 reduce-scatter.7
where the time goes:
time: 992 us; the launch traced here: 991 us
  waiting for transfers between devices  903 us (91%)
  local copies, waits for them, and re-layouts  25.8 us (3%)
  matrix products  16.4 us (2%)
  other arithmetic  15.4 us (2%)
  starting transfers between devices  15.2 us (2%)
  between operations  14.8 us (1%)
    reduce_scatter x3, waiting for transfers between devices, per_device(): lax.psum_scatter(dense_part.astype(jnp.bfloat16), 'narrow', scatter_dimen...  628 us
    all_gather x3, waiting for transfers between devices, per_device(): lax.all_gather(item_fac.astype(jnp.bfloat16), 'narrow', axis=0, tiled=True)  267 us
  transfers between devices with their start and end apart: 12, of which 9 were waited for; matrix products, arithmetic and copies ran while one was open for 2% of the time, Pallas kernels for 0%

commit v1 on v0

--- a/solution.py
+++ b/solution.py
@@ -21,6 +21,19 @@
     devices = range(lax.axis_size(axis))
     route = [((i - distance) % len(devices), i) for i in devices]
     return lax.ppermute(block, axis, route)
+
+
+def gathered(rows):
+    members = lax.axis_size("narrow")
+    copies = jnp.broadcast_to(rows[None], (members,) + rows.shape)
+    return lax.all_to_all(copies, "narrow", 0, 0).reshape(members * rows.shape[0], K)
+
+
+def summed(partial):
+    members = lax.axis_size("narrow")
+    parts = partial.reshape(members, partial.shape[0] // members, K)
+    arrived = lax.all_to_all(parts, "narrow", 0, 0)
+    return jnp.sum(arrived.astype(jnp.float32), axis=0)
 
 
 def adam_update(param, first, second, grad):
@@ -70,7 +83,7 @@
     user_fac, user_first, user_second = (user_factors, user_m, user_v)
     item_fac, item_first, item_second = (item_factors, item_m, item_v)
     for substep in range(STEPS):
-        current_rows = lax.all_gather(item_fac.astype(jnp.bfloat16), "narrow", axis=0, tiled=True)
+        current_rows = gathered(item_fac.astype(jnp.bfloat16))
         block_rows = current_rows.shape[0]
         item_idx = item_tiles[0, 0, substep]
         user_grad, item_part = slot_terms(
@@ -85,9 +98,7 @@
             user_fac, user_first, user_second, GRAD_SCALE * user_grad + DECAY_REG * user_fac
         )
         dense_part = select_rows(item_part, item_idx, 0, block_rows)
-        item_total = lax.psum_scatter(
-            dense_part.astype(jnp.bfloat16), "narrow", scatter_dimension=0, tiled=True
-        ).astype(jnp.float32)
+        item_total = summed(dense_part.astype(jnp.bfloat16))
         item_fac, item_first, item_second = adam_update(
             item_fac, item_first, item_second, GRAD_SCALE * item_total + DECAY_REG * item_fac
         )

time: 992 us -> 290 us (0.29)
  waiting for transfers between devices: 903 us -> 131 us
  starting transfers between devices: 15.2 us -> 58.2 us
  blocking collectives: 0 us -> 37.8 us
  between operations: 14.8 us -> 1.45 us
    reduce_scatter x3 -> x0, waiting for transfers between devices: 628 us -> none  [per_device(): lax.psum_scatter(dense_part.astype(jnp.bfloat16), 'narrow', scatter_dimen...]
    all_gather x3 -> x0, waiting for transfers between devices: 267 us -> none  [per_device(): lax.all_gather(item_fac.astype(jnp.bfloat16), 'narrow', axis=0, tiled=True)]
    all_to_all x0 -> x5, waiting for transfers between devices: none -> 126 us  [the longest x3 78.4 us: gathered(): lax.all_to_all(copies, 'narrow', 0, 0).reshape(members * rows.shape[0], K)]
    all_to_all x0 -> x5, starting transfers between devices: none -> 46.4 us  [the longest x3 28.5 us: gathered(): lax.all_to_all(copies, 'narrow', 0, 0).reshape(members * rows.shape[0], K)]
    all_to_all x0 -> x1, blocking collectives: none -> 37.8 us  [summed(): arrived = lax.all_to_all(parts, 'narrow', 0, 0)]
  transfers between devices with their start and end apart: 12 -> 11, of which waited for: 9 -> 7; matrix products, arithmetic and copies ran while one was open for 2% -> 7% of each run, Pallas kernels for 0% -> 0%
where the time goes in v1:
time: 290 us; the launch traced here: 288 us
  waiting for transfers between devices  131 us (45%)
  starting transfers between devices  58.2 us (20%)
  blocking collectives  37.8 us (13%)
  local copies, waits for them, and re-layouts  29.1 us (10%)
  matrix products  17.4 us (6%)
  other arithmetic  12.2 us (4%)
    all_to_all x3, waiting for transfers between devices, gathered(): lax.all_to_all(copies, 'narrow', 0, 0).reshape(members * rows.shape[0], K)  78.4 us
    all_to_all x2, waiting for transfers between devices, summed(): arrived = lax.all_to_all(parts, 'narrow', 0, 0)  47.9 us
    all_to_all x1, blocking collectives, summed(): arrived = lax.all_to_all(parts, 'narrow', 0, 0)  37.8 us
    all_to_all x3, starting transfers between devices, gathered(): lax.all_to_all(copies, 'narrow', 0, 0).reshape(members * rows.shape[0], K)  28.5 us
    all_to_all x2, starting transfers between devices, summed(): arrived = lax.all_to_all(parts, 'narrow', 0, 0)  17.9 us
    unnamed x80, local copies, waits for them, and re-layouts  12.1 us
    ppermute x6, starting transfers between devices, shifted(): return lax.ppermute(block, axis, route)  11.8 us
    dot_general x3, matrix products, slot_terms(): jnp.einsum('tak,tbk->tab', user_rows, item_rows, preferred_element_type=j...  6.66 us
  transfers between devices with their start and end apart: 11, of which 7 were waited for; matrix products, arithmetic and copies ran while one was open for 7% of the time, Pallas kernels for 0%

profile of v1, /device:TPU:6, one launch (start us, length us, event | category | flops | bytes accessed | tf_op | source)
XLA Modules:
  0.0 287.5 jit_solution(16729043302429306460)
XLA Ops:
  0.6 0.9 convert_element_type.103
  1.5 1.2 broadcast_in_dim.6
  2.7 15.8 %all-to-all-start = ((bf16[16,256,128]{2,1,0:T(8,128)(2,1)}), bf16[16,256,128]{2,1,0:T(8,128)(2,1)S(1)}, u32[]{:S(2)}, u32[]{:S(2)}) async-start(bf16[16,256,128]{2,1,0:T(8,128)(2,1)} %broadcast_in_dim.6), calls=%async_computation | async-start | bytes 2097152 | tf_op jit(solution)/shard_map/all_to_all | solution.py:29
  18.6 0.5 fusion.25
  19.1 0.8 gather_fusion
  19.9 0.7 fusion.36
  20.5 1.2 compare_convert_fusion.2
  22.2 0.5 slice_bitcast_fusion
  22.7 27.1 %all-to-all-done = bf16[16,256,128]{2,1,0:T(8,128)(2,1)S(1)} async-done(((bf16[16,256,128]{2,1,0:T(8,128)(2,1)}), bf16[16,256,128]{2,1,0:T(8,128)(2,1)S(1)}, u32[]{:S(2)}, u32[]{:S(2)}) %all-to-all-start) | async-done | bytes 1048608 | tf_op jit(solution)/shard_map/all_to_all | solution.py:29
  49.9 0.8 gather_fusion.1
  50.7 2.2 fusion.5
  52.9 0.6 fusion.38
  53.8 1.5 copy.23
  55.2 2.2 convolution_convert_fusion.2
  57.5 1.6 convert_element_type.110
  59.1 37.8 %all_to_all.30 = bf16[16,256,128]{2,1,0:T(8,128)(2,1)S(1)} all-to-all(bf16[16,256,128]{2,1,0:T(8,128)(2,1)S(1)} %convert_element_type.110), channel_id=1, replica_groups=mesh['blk'=32,'narrow'=16] {'narrow'}, dimensions={0} | all-to-all | bytes 2097152 | tf_op jit(solution)/shard_map/all_to_all | solution.py:35
  97.1 0.8 divide_subtract_fusion.4
  97.8 1.9 collective-permute-start
  99.8 2.5 collective-permute-done
  102.3 0.7 copy-done.18
  102.9 1.2 broadcast_in_dim.7
  104.1 4.7 %all-to-all-start.2 = ((bf16[16,256,128]{2,1,0:T(8,128)(2,1)}), bf16[16,256,128]{2,1,0:T(8,128)(2,1)}, u32[]{:S(2)}, u32[]{:S(2)}) async-start(bf16[16,256,128]{2,1,0:T(8,128)(2,1)} %broadcast_in_dim.7), calls=%async_computation.2 | async-start | bytes 2097152 | tf_op jit(solution)/shard_map/all_to_all | solution.py:29
  108.8 1.2 compare_convert_fusion.1
  110.0 0.6 slice_bitcast_fusion.1
  111.4 1.5 copy.22
  112.9 1.0 convolution_multiply_fusion.2
  114.2 0.8 gather_fusion.2
  115.0 28.0 %all-to-all-done.2 = bf16[16,256,128]{2,1,0:T(8,128)(2,1)} async-done(((bf16[16,256,128]{2,1,0:T(8,128)(2,1)}), bf16[16,256,128]{2,1,0:T(8,128)(2,1)}, u32[]{:S(2)}, u32[]{:S(2)}) %all-to-all-start.2) | async-done | bytes 1048608 | tf_op jit(solution)/shard_map/all_to_all | solution.py:29
  143.0 2.0 gather_fusion.3
  145.0 2.2 fusion.3
  147.2 0.6 fusion.40
  148.1 1.5 copy.25
  149.6 1.2 convolution_convert_fusion.1
  150.8 1.3 convert_element_type.119
  152.2 12.5 %all-to-all-start.3 = ((bf16[16,256,128]{2,1,0:T(8,128)(2,1)}), bf16[16,256,128]{2,1,0:T(8,128)(2,1)S(1)}, u32[]{:S(2)}, u32[]{:S(2)}) async-start(bf16[16,256,128]{2,1,0:T(8,128)(2,1)} %convert_element_type.119), calls=%async_computation.3 | async-start | bytes 2097152 | tf_op jit(solution)/shard_map/all_to_all | solution.py:35
  164.7 1.9 collective-permute-start.1
  166.6 1.9 collective-permute-start.2
  168.5 27.3 %all-to-all-done.3 = bf16[16,256,128]{2,1,0:T(8,128)(2,1)S(1)} async-done(((bf16[16,256,128]{2,1,0:T(8,128)(2,1)}), bf16[16,256,128]{2,1,0:T(8,128)(2,1)S(1)}, u32[]{:S(2)}, u32[]{:S(2)}) %all-to-all-start.3) | async-done | bytes 1048608 | tf_op jit(solution)/shard_map/all_to_all | solution.py:35
  196.0 1.8 divide_subtract_fusion.2
  197.8 1.9 collective-permute-start.3
  199.7 2.5 collective-permute-done.3
  202.2 0.7 copy-done.16
  202.9 1.2 broadcast_in_dim.8
  204.1 8.0 %all-to-all-start.4 = ((bf16[16,256,128]{2,1,0:T(8,128)(2,1)}), bf16[16,256,128]{2,1,0:T(8,128)(2,1)}, u32[]{:S(2)}, u32[]{:S(2)}) async-start(bf16[16,256,128]{2,1,0:T(8,128)(2,1)} %broadcast_in_dim.8), calls=%async_computation.4 | async-start | bytes 2097152 | tf_op jit(solution)/shard_map/all_to_all | solution.py:29
  212.1 1.3 compare_convert_fusion
  214.1 1.5 copy.24
  215.7 1.0 convolution_multiply_fusion.1
  216.9 0.9 fusion.34
  217.7 0.8 gather_fusion.4
  218.5 23.2 %all-to-all-done.4 = bf16[16,256,128]{2,1,0:T(8,128)(2,1)} async-done(((bf16[16,256,128]{2,1,0:T(8,128)(2,1)}), bf16[16,256,128]{2,1,0:T(8,128)(2,1)}, u32[]{:S(2)}, u32[]{:S(2)}) %all-to-all-start.4) | async-done | bytes 1048608 | tf_op jit(solution)/shard_map/all_to_all | solution.py:29
  241.8 2.0 gather_fusion.5
  243.8 2.2 fusion.1
  246.0 0.6 fusion.42
  246.9 1.5 copy.27
  248.4 1.2 convolution_convert_fusion
  249.6 1.3 convert_element_type.127
  251.0 5.4 %all-to-all-start.5 = ((bf16[16,256,128]{2,1,0:T(8,128)(2,1)}), bf16[16,256,128]{2,1,0:T(8,128)(2,1)S(1)}, u32[]{:S(2)}, u32[]{:S(2)}) async-start(bf16[16,256,128]{2,1,0:T(8,128)(2,1)} %convert_element_type.127), calls=%async_computation.5 | async-start | bytes 2097152 | tf_op jit(solution)/shard_map/all_to_all | solution.py:35
  256.4 1.9 collective-permute-start.4
  258.3 2.2 collective-permute-start.5
  261.3 1.5 copy.26
  262.9 1.0 convolution_multiply_fusion
  264.0 0.9 divide_subtract_fusion.1
  265.0 20.6 %all-to-all-done.5 = bf16[16,256,128]{2,1,0:T(8,128)(2,1)S(1)} async-done(((bf16[16,256,128]{2,1,0:T(8,128)(2,1)}), bf16[16,256,128]{2,1,0:T(8,128)(2,1)S(1)}, u32[]{:S(2)}, u32[]{:S(2)}) %all-to-all-start.5) | async-done | bytes 1048608 | tf_op jit(solution)/shard_map/all_to_all | solution.py:35
  285.7 1.8 divide_subtract_fusion
  (96 shorter events, 4.7 us)
Async XLA Ops:
  2.7 15.8 %copy-start = (f32[256,128]{1,0:T(8,128)S(1)}, f32[256,128]{1,0:T(8,128)}, u32[]{:S(2)}) copy-start(f32[256,128]{1,0:T(8,128)} %param.10) | copy-start | bytes 393220
  2.7 15.8 %copy-start.25 = (s32[1,1,3,36]{3,1,2,0:T(1,128)S(1)}, s32[1,1,3,36]{3,1,2,0:T(1,128)}, u32[]{:S(2)}) copy-start(s32[1,1,3,36]{3,1,2,0:T(1,128)} %param.17) | copy-start | bytes 1300
  2.7 47.1 %all-to-all-start = ((bf16[16,256,128]{2,1,0:T(8,128)(2,1)}), bf16[16,256,128]{2,1,0:T(8,128)(2,1)S(1)}, u32[]{:S(2)}, u32[]{:S(2)}) async-start(bf16[16,256,128]{2,1,0:T(8,128)(2,1)} %broadcast_in_dim.6), calls=%async_computation | async-start | bytes 2097152 | tf_op jit(solution)/shard_map/all_to_all | solution.py:29
  19.1 0.8 copy-start.26
  19.1 2.6 copy-start.24
  59.0 38.0 %copy-start.15 = (f32[256,128]{1,0:T(8,128)S(1)}, f32[256,128]{1,0:T(8,128)}, u32[]{:S(2)}) copy-start(f32[256,128]{1,0:T(8,128)} %param.13) | copy-start | bytes 393220
  59.0 38.0 %copy-start.21 = (f32[256,128]{1,0:T(8,128)S(1)}, f32[256,128]{1,0:T(8,128)}, u32[]{:S(2)}) copy-start(f32[256,128]{1,0:T(8,128)} %param.14) | copy-start | bytes 393220
  59.1 38.0 %copy-start.22 = (f32[256,128]{1,0:T(8,128)S(1)}, f32[256,128]{1,0:T(8,128)}, u32[]{:S(2)}) copy-start(f32[256,128]{1,0:T(8,128)} %param.15) | copy-start | bytes 393220
  97.8 4.4 %collective-permute-start = (f32[256,128]{1,0:T(8,128)S(1)}, f32[256,128]{1,0:T(8,128)S(1)}, u32[]{:S(2)}, u32[]{:S(2)}) collective-permute-start(f32[256,128]{1,0:T(8,128)S(1)} %get-tuple-element.17), channel_id=1, source_target_pairs={{16,0},{32,16},{48,32},{64,48},{80,64},{96,80},{112,96},{128,112},... | collective-permute-start | bytes 393224 | tf_op jit(solution)/shard_map/ppermute | solution.py:23
  102.3 0.7 copy-start.18
  104.1 38.9 %all-to-all-start.2 = ((bf16[16,256,128]{2,1,0:T(8,128)(2,1)}), bf16[16,256,128]{2,1,0:T(8,128)(2,1)}, u32[]{:S(2)}, u32[]{:S(2)}) async-start(bf16[16,256,128]{2,1,0:T(8,128)(2,1)} %broadcast_in_dim.7), calls=%async_computation.2 | async-start | bytes 2097152 | tf_op jit(solution)/shard_map/all_to_all | solution.py:29
  112.9 1.2 copy-start.1
  112.9 1.2 copy-start.9
  112.9 1.2 copy-start.12
  114.0 0.9 copy-start.4
  143.0 2.0 copy-start.32
  148.1 1.5 copy-start.31
  152.2 43.8 %copy-start.19 = (f32[256,128]{1,0:T(8,128)S(1)}, f32[256,128]{1,0:T(8,128)}, u32[]{:S(2)}) copy-start(f32[256,128]{1,0:T(8,128)} %copy-done.18) | copy-start | bytes 393220
  152.2 43.7 %all-to-all-start.3 = ((bf16[16,256,128]{2,1,0:T(8,128)(2,1)}), bf16[16,256,128]{2,1,0:T(8,128)(2,1)S(1)}, u32[]{:S(2)}, u32[]{:S(2)}) async-start(bf16[16,256,128]{2,1,0:T(8,128)(2,1)} %convert_element_type.119), calls=%async_computation.3 | async-start | bytes 2097152 | tf_op jit(solution)/shard_map/all_to_all | solution.py:35
  164.7 31.3 %collective-permute-start.1 = (f32[256,128]{1,0:T(8,128)}, f32[256,128]{1,0:T(8,128)}, u32[]{:S(2)}, u32[]{:S(2)}) collective-permute-start(f32[256,128]{1,0:T(8,128)} %get-tuple-element.18), channel_id=1, source_target_pairs={{16,0},{32,16},{48,32},{64,48},{80,64},{96,80},{112,96},{128,112},... | collective-permute-start | bytes 393224 | tf_op jit(solution)/shard_map/ppermute | solution.py:23
  166.6 29.4 %collective-permute-start.2 = (f32[256,128]{1,0:T(8,128)}, f32[256,128]{1,0:T(8,128)}, u32[]{:S(2)}, u32[]{:S(2)}) collective-permute-start(f32[256,128]{1,0:T(8,128)} %get-tuple-element.19), channel_id=1, source_target_pairs={{16,0},{32,16},{48,32},{64,48},{80,64},{96,80},{112,96},{128,112},... | collective-permute-start | bytes 393224 | tf_op jit(solution)/shard_map/ppermute | solution.py:23
  197.8 4.4 %collective-permute-start.3 = (f32[256,128]{1,0:T(8,128)S(1)}, f32[256,128]{1,0:T(8,128)S(1)}, u32[]{:S(2)}, u32[]{:S(2)}) collective-permute-start(f32[256,128]{1,0:T(8,128)S(1)} %get-tuple-element.12), channel_id=1, source_target_pairs={{16,0},{32,16},{48,32},{64,48},{80,64},{96,80},{112,96},{128,112},... | collective-permute-start | bytes 393224 | tf_op jit(solution)/shard_map/ppermute | solution.py:23
  202.2 0.7 copy-start.16
  204.1 9.3 %copy-start.29 = (s32[36]{0:T(128)S(1)}, s32[36]{0:T(128)}, u32[]{:S(2)}) copy-start(s32[36]{0:T(128)} %get-tuple-element.26) | copy-start | bytes 436
  204.1 9.3 %copy-start.28 = (s32[36]{0:T(128)S(1)}, s32[36]{0:T(128)}, u32[]{:S(2)}) copy-start(s32[36]{0:T(128)} %get-tuple-element.29) | copy-start | bytes 436
  204.1 37.7 %all-to-all-start.4 = ((bf16[16,256,128]{2,1,0:T(8,128)(2,1)}), bf16[16,256,128]{2,1,0:T(8,128)(2,1)}, u32[]{:S(2)}, u32[]{:S(2)}) async-start(bf16[16,256,128]{2,1,0:T(8,128)(2,1)} %broadcast_in_dim.8), calls=%async_computation.4 | async-start | bytes 2097152 | tf_op jit(solution)/shard_map/all_to_all | solution.py:29
  214.1 1.5 copy-start.27
  215.7 1.2 copy-start.2
  215.7 1.2 copy-start.5
  215.7 1.2 copy-start.10
  215.7 1.2 copy-start.13
  216.9 1.7 copy-start.7
  241.8 2.0 copy-start.33
  246.9 1.5 copy-start.30
  251.0 7.4 %copy-start.23 = (f32[256,128]{1,0:T(8,128)S(1)}, f32[256,128]{1,0:T(8,128)}, u32[]{:S(2)}) copy-start(f32[256,128]{1,0:T(8,128)} %get-tuple-element.14) | copy-start | bytes 393220
  251.0 34.6 %all-to-all-start.5 = ((bf16[16,256,128]{2,1,0:T(8,128)(2,1)}), bf16[16,256,128]{2,1,0:T(8,128)(2,1)S(1)}, u32[]{:S(2)}, u32[]{:S(2)}) async-start(bf16[16,256,128]{2,1,0:T(8,128)(2,1)} %convert_element_type.127), calls=%async_computation.5 | async-start | bytes 2097152 | tf_op jit(solution)/shard_map/all_to_all | solution.py:35
  256.4 29.3 %collective-permute-start.4 = (f32[256,128]{1,0:T(8,128)}, f32[256,128]{1,0:T(8,128)}, u32[]{:S(2)}, u32[]{:S(2)}) collective-permute-start(f32[256,128]{1,0:T(8,128)} %get-tuple-element.13), channel_id=1, source_target_pairs={{16,0},{32,16},{48,32},{64,48},{80,64},{96,80},{112,96},{128,112},... | collective-permute-start | bytes 393224 | tf_op jit(solution)/shard_map/ppermute | solution.py:23
  258.3 27.4 %collective-permute-start.5 = (f32[256,128]{1,0:T(8,128)S(1)}, f32[256,128]{1,0:T(8,128)}, u32[]{:S(2)}, u32[]{:S(2)}) collective-permute-start(f32[256,128]{1,0:T(8,128)S(1)} %copy-done.23), channel_id=1, source_target_pairs={{16,0},{32,16},{48,32},{64,48},{80,64},{96,80},{112,96},{128,112},... | collective-permute-start | bytes 393224 | tf_op jit(solution)/shard_map/ppermute | solution.py:23
  262.8 1.2 copy-start.3
  262.8 1.2 copy-start.6
  262.8 1.2 copy-start.8
  262.8 1.2 copy-start.11
  262.8 1.2 copy-start.14
  262.9 1.2 copy-start.20
  264.0 21.7 %copy-start.17 = (f32[256,128]{1,0:T(8,128)S(1)}, f32[256,128]{1,0:T(8,128)}, u32[]{:S(2)}) copy-start(f32[256,128]{1,0:T(8,128)} %copy-done.16) | copy-start | bytes 393220

commit v2 on v0

v2 whole, which is shorter than its diff:
```python
import jax
import jax.numpy as jnp
from jax import lax
from jax.experimental import pallas as pl
from jax.experimental.pallas import tpu as pltpu
from jax.sharding import PartitionSpec as P

K = 128
TILE = 128
MAXT = 36
STEPS = 3
RING = 8
USER_ROWS = 256
ITEM_ROWS = 256
USER_TILES = 2
ITEM_TILES = 32
COUNT_ROWS = 16
PART = USER_ROWS + COUNT_ROWS


LEARN_RATE = 0.01
BETA_ONE = 0.8
BETA_TWO = 0.95
ADAM_EPS = 1e-08
DECAY_REG = 0.05
GRAD_SCALE = 0.03125

VMEM = pl.BlockSpec(memory_space=pltpu.VMEM)
SMEM = pl.BlockSpec(memory_space=pltpu.SMEM)
F32 = jnp.float32
BF16 = jnp.bfloat16


def adam_update(param, first, second, grad):
    first = BETA_ONE * first + (1.0 - BETA_ONE) * grad
    second = BETA_TWO * second + (1.0 - BETA_TWO) * grad * grad
    return (param - LEARN_RATE * first / (jnp.sqrt(second) + ADAM_EPS), first, second)


def kernel_call(body, outs, in_specs, scratch=(), flops=0, moved=1 << 20):
    return pl.pallas_call(
        body,
        out_shape=outs,
        in_specs=in_specs,
        out_specs=jax.tree.map(lambda _: VMEM, outs),
        scratch_shapes=list(scratch),
        cost_estimate=pl.CostEstimate(flops=flops, bytes_accessed=moved, transcendentals=0),
        compiler_params=pltpu.CompilerParams(vmem_limit_bytes=40 << 20),
    )


def dense_body(slots_ref, live_ref, ratings_ref, out_ref, total):
    total[...] = jnp.zeros_like(total)

    def add(t, carry):
        row = pl.multiple_of(slots_ref[t] * TILE, TILE)
        total[pl.ds(row, TILE), :] += ratings_ref[t].astype(F32)
        return carry

    lax.fori_loop(0, live_ref[0], add, 0)
    out_ref[...] = total[...].astype(BF16)


def dense_ratings(slots, live, ratings):
    rows = ITEM_TILES * USER_ROWS
    return kernel_call(
        dense_body,
        jax.ShapeDtypeStruct((rows, TILE), BF16),
        [SMEM, SMEM, VMEM],
        [pltpu.VMEM((rows, TILE), F32)],
        moved=10 << 20,
    )(slots, live, ratings)


def rating_part_body(order_ref, users_ref, dense_ref, out_ref):
    users = users_ref[: USER_ROWS]
    for k in range(ITEM_TILES):
        row = pl.multiple_of(order_ref[k] * USER_ROWS, USER_ROWS)
        part = lax.dot_general(
            dense_ref[pl.ds(row, USER_ROWS), :],
            users,
            (((0,), (0,)), ((), ())),
            preferred_element_type=F32,
        )
        out_ref[k * TILE : (k + 1) * TILE] = part.astype(BF16)


def rating_part(order, users, dense):
    return kernel_call(
        rating_part_body,
        jax.ShapeDtypeStruct((ITEM_TILES * TILE, K), BF16),
        [SMEM, VMEM, VMEM],
        flops=2 * ITEM_TILES * USER_ROWS * TILE * K,
        moved=3 << 20,
    )(order, users, dense)


def user_body(order_ref, counts_ref, dense_ref, fac_ref, first_ref, second_ref, *rest):
    pieces, (fac_out, first_out, second_out, bf_out) = rest[:-4], rest[-4:]
    fac = fac_ref[...]
    users = fac.astype(BF16)
    total = jnp.zeros((USER_ROWS, K), F32)
    upper = lax.broadcasted_iota(jnp.int32, (USER_ROWS, TILE), 0) < TILE
    k = 0
    for piece in pieces:
        for pair in range(2):
            rows = piece[pair * ITEM_ROWS : (pair + 1) * ITEM_ROWS]
            predicted = lax.dot_general(
                users, rows, (((1,), (1,)), ((), ())), preferred_element_type=F32
            )
            errors = []
            for h in range(2):
                tile = order_ref[k]
                k += 1
                row = pl.multiple_of(tile * USER_ROWS, USER_ROWS)
                many = jnp.where(upper, counts_ref[tile], counts_ref[ITEM_TILES + tile])
                ratings = dense_ref[pl.ds(row, USER_ROWS), :].astype(F32)
                errors.append(
                    (predicted[:, h * TILE : (h + 1) * TILE] * many - ratings).astype(BF16)
                )
            total += jnp.dot(
                jnp.concatenate(errors, axis=1), rows, preferred_element_type=F32
            )
    grad = GRAD_SCALE * total + DECAY_REG * fac
    fac, first, second = adam_update(fac, first_ref[...], second_ref[...], grad)
    fac_out[...] = fac
    first_out[...] = first
    second_out[...] = second
    bf_out[...] = fac.astype(BF16)


def user_step(order, counts, dense, state, pieces):
    like = jax.ShapeDtypeStruct((USER_ROWS, K), F32)
    return kernel_call(
        user_body,
        (like, like, like, jax.ShapeDtypeStruct((USER_ROWS, K), BF16)),
        [SMEM, SMEM] + [VMEM] * (4 + len(pieces)),
        flops=4 * ITEM_TILES * USER_ROWS * TILE * K,
        moved=5 << 20,
    )(order, counts, dense, *state, *pieces)


def item_body(lanes_ref, own_ref, other_ref, fac_ref, first_ref, second_ref, *rest):
    pieces, (fac_out, first_out, second_out, bf_out) = rest[:-4], rest[-4:]
    lane = lax.broadcasted_iota(jnp.int32, (COUNT_ROWS, K), 1)
    weighted = [jnp.zeros((K, K), F32) for _ in range(2)]
    for piece, offset in pieces_at(pieces):
        for plane in range(2):
            top = offset + plane * PART
            counts = piece[top + USER_ROWS : top + PART].astype(F32)
            for u in range(USER_TILES):
                users = piece[top + u * TILE : top + (u + 1) * TILE]
                gram = lax.dot_general(
                    users, users, (((0,), (0,)), ((), ())), preferred_element_type=F32
                )
                for h in range(2):
                    at = u * ITEM_TILES + lanes_ref[0] + h
                    many = jnp.sum(jnp.where(lane == at, counts, 0.0), axis=1, keepdims=True)
                    weighted[h] = weighted[h] + many[0:1] * gram
    fac = fac_ref[...]
    rows = fac.astype(BF16)
    parts = []
    for h in range(2):
        high = weighted[h].astype(BF16)
        low = (weighted[h] - high.astype(F32)).astype(BF16)
        mine = rows[h * TILE : (h + 1) * TILE]
        parts.append(
            jnp.dot(mine, high, preferred_element_type=F32)
            + jnp.dot(mine, low, preferred_element_type=F32)
        )
    total = jnp.concatenate(parts, axis=0) - (
        own_ref[...].astype(F32) + other_ref[...].astype(F32)
    )
    grad = GRAD_SCALE * total + DECAY_REG * fac
    fac, first, second = adam_update(fac, first_ref[...], second_ref[...], grad)
    fac_out[...] = fac
    first_out[...] = first
    second_out[...] = second
    bf_out[...] = fac.astype(BF16)


def pieces_at(pieces):
    return [(p, 2 * ITEM_ROWS) for p in pieces[:-1]] + [(pieces[-1], 0)]


def item_step(lanes, own, other, state, pieces):
    like = jax.ShapeDtypeStruct((ITEM_ROWS, K), F32)
    return kernel_call(
        item_body,
        (like, like, like, jax.ShapeDtypeStruct((ITEM_ROWS, K), BF16)),
        [SMEM] + [VMEM] * (5 + len(pieces)),
        flops=2 * 32 * TILE * K * K,
        moved=4 << 20,
    )(lanes, own, other, *state, *pieces)


def per_device(
    user_factors,
    user_m,
    user_v,
    item_factors,
    item_m,
    item_v,
    ratings,
    user_tiles,
    item_tiles,
    tile_counts,
):
    strata = lax.axis_size("blk")
    narrow = lax.axis_index("narrow")
    plane, place = narrow // RING, narrow % RING
    forward = [(z * RING + y, z * RING + (y + 1) % RING) for z in range(2) for y in range(RING)]
    backward = [(target, source) for source, target in forward]
    across = [(n, (n + RING) % (2 * RING)) for n in range(2 * RING)]
    rings = [[z * RING + y for y in range(RING)] for z in range(2)]

    def to_earlier(value, swap):
        members = 2 * RING
        route = [
            (b * members + n, ((b - 1) % strata) * members + (n + swap) % members)
            for b in range(strata)
            for n in range(members)
        ]
        return lax.ppermute(value, ("blk", "narrow"), route)

    def tiles_of(places):
        owner = jnp.stack([plane, 1 - plane])[None, :, None] * RING + places[:, None, None]
        return (owner * 2 + jnp.arange(2)[None, None, :]).reshape(-1).astype(jnp.int32)

    distance = jnp.array([0, -1, 1, -2, 2, -3, 3, 4], jnp.int32)
    arrival = tiles_of((place + distance) % RING)
    by_place = tiles_of(jnp.arange(RING, dtype=jnp.int32))
    lanes = (narrow * 2).reshape(1).astype(jnp.int32)

    users_at, items_at, live = user_tiles[0, 0], item_tiles[0, 0], tile_counts[0, 0]
    alive = jnp.arange(MAXT)[None, :] < live[:, None]
    pair = users_at * ITEM_TILES + items_at
    slots = items_at * USER_TILES + users_at
    counts = jnp.sum(
        ((pair[:, :, None] == jnp.arange(K)[None, None, :]) & alive[:, :, None]).astype(F32), axis=1
    )
    count_rows = jnp.broadcast_to(counts[:, None, :], (STEPS, COUNT_ROWS, K)).astype(BF16)

    user_state = (user_factors, user_m, user_v)
    item_state = (item_factors, item_m, item_v)
    item_bf = item_factors.astype(BF16)
    user_bf = user_factors.astype(BF16)
    first = jnp.concatenate([user_bf, count_rows[0], item_bf], axis=0)
    arrived = lax.ppermute(first, "narrow", across)
    item_other, part_other = arrived[PART:], arrived[:PART]
    part_own = first[:PART]
    for s in range(STEPS):
        dense = dense_ratings(slots[s], live[s].reshape(1), ratings[0, 0, s])
        partial = lax.psum_scatter(
            rating_part(by_place, part_own, dense),
            "narrow",
            scatter_dimension=0,
            tiled=True,
            axis_index_groups=rings,
        )
        load = jnp.concatenate([item_bf, item_other, part_own, part_other], axis=0)
        pieces = [load]
        up = down = load
        for _ in range(3):
            up = lax.ppermute(up, "narrow", forward)
            down = lax.ppermute(down, "narrow", backward)
            pieces += [up, down]
        last_items = lax.ppermute(up[: 2 * ITEM_ROWS], "narrow", forward)
        last_users = lax.ppermute(down[2 * ITEM_ROWS :], "narrow", backward)
        other = lax.ppermute(partial[ITEM_ROWS:], "narrow", across)
        *item_state, item_bf = item_step(
            lanes, partial[:ITEM_ROWS], other, item_state, pieces + [last_users]
        )
        if s + 1 < STEPS:
            item_other = to_earlier(item_bf, RING)
            item_bf = to_earlier(item_bf, 0)
        *user_state, user_bf = user_step(
            arrival, counts[s], dense, user_state, pieces + [last_items]
        )
        if s + 1 < STEPS:
            part_own = jnp.concatenate([user_bf, count_rows[s + 1]], axis=0)
            part_other = lax.ppermute(part_own, "narrow", across)
            item_state = [to_earlier(array, 0) for array in item_state]
    return (*user_state, *item_state)


def solution(mesh):
    return jax.shard_map(
        per_device,
        mesh=mesh,
        in_specs=(
            P(("blk", "narrow"), None),
            P(("blk", "narrow"), None),
            P(("blk", "narrow"), None),
            P(("blk", "narrow"), None),
            P(("blk", "narrow"), None),
            P(("blk", "narrow"), None),
            P("blk", "narrow", None, None, None, None),
            P("blk", "narrow", None, None),
            P("blk", "narrow", None, None),
            P("blk", "narrow", None),
        ),
        out_specs=(
            P(("blk", "narrow"), None),
            P(("blk", "narrow"), None),
            P(("blk", "narrow"), None),
            P(("blk", "narrow"), None),
            P(("blk", "narrow"), None),
            P(("blk", "narrow"), None),
        ),
        check_vma=False,
    )
```

time: 992 us -> 296 us (0.30)
  waiting for transfers between devices: 903 us -> 63.9 us
  starting transfers between devices: 15.2 us -> 142 us
  Pallas kernels: 0 us -> 27.7 us
  matrix products: 16.4 us -> 0 us
    reduce_scatter x3, waiting for transfers between devices: 628 us -> 0.06 us  [per_device(): lax.psum_scatter(rating_part(by_place, part_own, dense), 'narrow', scatte...]
    all_gather x3 -> x0, waiting for transfers between devices: 267 us -> none  [per_device(): lax.all_gather(item_fac.astype(jnp.bfloat16), 'narrow', axis=0, tiled=True)]
    ppermute x6 -> x40, starting transfers between devices: 14.6 us -> 142 us  [the longest x9 40.2 us: per_device(): down = lax.ppermute(down, 'narrow', backward)]
    ppermute x6 -> x40, waiting for transfers between devices: 7.81 us -> 63.8 us  [the longest x9 20.8 us: per_device(): up = lax.ppermute(up, 'narrow', forward)]
    pallas_call x0 -> x12, Pallas kernels: none -> 27.7 us  [the longest x3 7.88 us: user_step(): kernel_call(user_body, (like, like, like, jax.ShapeDtypeStruct((USER_ROWS...]
    dot_general x15 -> x0, matrix products: 16.4 us -> none  [the longest x3 6.64 us: slot_terms(): jnp.einsum('tak,tbk->tab', user_rows, item_rows, preferred_element_type=j...]
  transfers between devices with their start and end apart: 12 -> 43, of which waited for: 9 -> 15; matrix products, arithmetic and copies ran while one was open for 2% -> 7% of each run, Pallas kernels for 0% -> 9%
where the time goes in v2:
time: 296 us; the launch traced here: 290 us
  starting transfers between devices  142 us (48%)
  waiting for transfers between devices  63.9 us (22%)
  local copies, waits for them, and re-layouts  34.7 us (12%)
  Pallas kernels  27.7 us (9%)
  between operations  15.1 us (5%)
  other arithmetic  7.17 us (2%)
    ppermute x9, starting transfers between devices, per_device(): down = lax.ppermute(down, 'narrow', backward)  40.2 us
    ppermute x10, starting transfers between devices, to_earlier(): return lax.ppermute(value, ('blk', 'narrow'), route)  31.4 us
    ppermute x9, starting transfers between devices, per_device(): up = lax.ppermute(up, 'narrow', forward)  20.9 us
    ppermute x9, waiting for transfers between devices, per_device(): up = lax.ppermute(up, 'narrow', forward)  20.8 us
    unnamed x152, local copies, waits for them, and re-layouts  19.8 us
    ppermute x3, starting transfers between devices, per_device(): last_users = lax.ppermute(down[2 * ITEM_ROWS:], 'narrow', backward)  12.1 us
    ppermute x3, waiting for transfers between devices, per_device(): other = lax.ppermute(partial[ITEM_ROWS:], 'narrow', across)  11.6 us
    ppermute x10, waiting for transfers between devices, to_earlier(): return lax.ppermute(value, ('blk', 'narrow'), route)  11.3 us
  transfers between devices with their start and end apart: 43, of which 15 were waited for; matrix products, arithmetic and copies ran while one was open for 7% of the time, Pallas kernels for 9%

profile of v2, /device:TPU:6, one launch (start us, length us, event | category | flops | bytes accessed | tf_op | source)
XLA Modules:
  0.0 290.2 jit_solution(12345201711539073538)
XLA Ops:
  11.9 10.9 %collective-permute-start = (bf16[528,128]{1,0:T(8,128)(2,1)}, bf16[528,128]{1,0:T(8,128)(2,1)}, u32[]{:S(2)}, u32[]{:S(2)}) collective-permute-start(bf16[528,128]{1,0:T(8,128)(2,1)} %pad_maximum_fusion), channel_id=1, source_target_pairs={{0,8},{1,9},{2,10},{3,11},{4,12},{5,13},{6,14},{7,15},{8,0},{9,1},... | collective-permute-start | bytes 405512 | tf_op jit(solution)/shard_map/ppermute | solution.py:249
  26.5 3.4 %slice_bitcast_fusion = (bf16[36,128,128]{2,1,0:T(8,128)(2,1)S(1)}, bf16[36,128,128]{2,1,0:T(8,128)(2,1)S(1)}, bf16[36,128,128]{2,1,0:T(8,128)(2,1)}) fusion(bf16[1,1,3,36,128,128]{5,4,3,2,1,0:T(8,128)(2,1)} %param.17), kind=kLoop, calls=%fused_computation | loop fusion | bytes 7077888 | tf_op jit(solution)/shard_map/squeeze | solution.py:253
  29.9 2.1 shard_map.156.dense_ref
  37.7 3.2 %collective-permute-start.1 = (bf16[1056,128]{1,0:T(8,128)(2,1)S(1)}, bf16[1056,128]{1,0:T(8,128)(2,1)S(1)}, u32[]{:S(2)}, u32[]{:S(2)}) collective-permute-start(bf16[1056,128]{1,0:T(8,128)(2,1)S(1)} %slice_dynamic-update-slice_fusion.rest_0_), channel_id=1, source_target_pairs={{0,1},{1,2},{2,3},{3,4},{4,5},{5,6},{6,7},{7,0},{8,9},{9,10},{10,1... | collective-permute-start | bytes 811016 | tf_op jit(solution)/shard_map/ppermute | solution.py:265
  40.9 3.8 %collective-permute-start.2 = (bf16[1056,128]{1,0:T(8,128)(2,1)S(1)}, bf16[1056,128]{1,0:T(8,128)(2,1)S(1)}, u32[]{:S(2)}, u32[]{:S(2)}) collective-permute-start(bf16[1056,128]{1,0:T(8,128)(2,1)S(1)} %slice_dynamic-update-slice_fusion.rest_0_), channel_id=1, source_target_pairs={{1,0},{2,1},{3,2},{4,3},{5,4},{6,5},{7,6},{0,7},{9,8},{10,9},{11,1... | collective-permute-start | bytes 811016 | tf_op jit(solution)/shard_map/ppermute | solution.py:266
  45.5 3.6 %collective-permute-done.1.rest_1_ = bf16[1056,128]{1,0:T(8,128)(2,1)S(1)} collective-permute-done((bf16[1056,128]{1,0:T(8,128)(2,1)S(1)}, bf16[1056,128]{1,0:T(8,128)(2,1)S(1)}, u32[]{:S(2)}, u32[]{:S(2)}) %collective-permute-start.1) | collective-permute-done | bytes 270368 | tf_op jit(solution)/shard_map/ppermute | solution.py:265
  49.1 1.9 collective-permute-start.3
  52.0 5.7 %collective-permute-start.4 = (bf16[1056,128]{1,0:T(8,128)(2,1)S(1)}, bf16[1056,128]{1,0:T(8,128)(2,1)}, u32[]{:S(2)}, u32[]{:S(2)}) collective-permute-start(bf16[1056,128]{1,0:T(8,128)(2,1)S(1)} %collective-permute-done.2.rest_2_), channel_id=1, source_target_pairs={{1,0},{2,1},{3,2},{4,3},{5,4},{6,5},{7,6},{0,7},{9,8},{10,9},{11,1... | collective-permute-start | bytes 811016 | tf_op jit(solution)/shard_map/ppermute | solution.py:266
  58.4 5.6 %collective-permute-done.3.rest_3_ = bf16[1056,128]{1,0:T(8,128)(2,1)} collective-permute-done((bf16[1056,128]{1,0:T(8,128)(2,1)S(1)}, bf16[1056,128]{1,0:T(8,128)(2,1)}, u32[]{:S(2)}, u32[]{:S(2)}) %collective-permute-start.3) | collective-permute-done | bytes 270368 | tf_op jit(solution)/shard_map/ppermute | solution.py:265
  64.0 1.9 collective-permute-start.5
  66.0 5.7 %collective-permute-start.6 = (bf16[1056,128]{1,0:T(8,128)(2,1)}, bf16[1056,128]{1,0:T(8,128)(2,1)S(1)}, u32[]{:S(2)}, u32[]{:S(2)}) collective-permute-start(bf16[1056,128]{1,0:T(8,128)(2,1)} %collective-permute-done.4.rest_4_), channel_id=1, source_target_pairs={{1,0},{2,1},{3,2},{4,3},{5,4},{6,5},{7,6},{0,7},{9,8},{10,9},{11,1... | collective-permute-start | bytes 811016 | tf_op jit(solution)/shard_map/ppermute | solution.py:266
  75.1 1.9 shard_map.155.dense_ref
  78.1 1.9 collective-permute-start.7
  81.3 5.1 %collective-permute-start.9 = (bf16[544,128]{1,0:T(8,128)(2,1)}, bf16[544,128]{1,0:T(8,128)(2,1)}, u32[]{:S(2)}, u32[]{:S(2)}) collective-permute-start(bf16[544,128]{1,0:T(8,128)(2,1)} %slice.138), channel_id=1, source_target_pairs={{1,0},{2,1},{3,2},{4,3},{5,4},{6,5},{7,6},{0,7},{9,8},{10,9},{11,1... | collective-permute-start | bytes 417800 | tf_op jit(solution)/shard_map/ppermute | solution.py:269
  86.5 2.6 shard_map.157
  91.8 2.3 shard_map.161
  95.1 1.9 collective-permute-start.8
  97.1 8.2 %collective-permute-done.8.other_ref = bf16[256,128]{1,0:T(8,128)(2,1)S(1)} collective-permute-done((bf16[256,128]{1,0:T(8,128)(2,1)S(1)}, bf16[256,128]{1,0:T(8,128)(2,1)S(1)}, u32[]{:S(2)}, u32[]{:S(2)}) %collective-permute-start.8) | collective-permute-done | bytes 65568 | tf_op jit(solution)/shard_map/ppermute | solution.py:270
  105.3 2.2 shard_map.159
  107.6 1.9 collective-permute-start.10
  109.5 3.7 %collective-permute-start.12 = (bf16[272,128]{1,0:T(8,128)(2,1)S(1)}, bf16[272,128]{1,0:T(8,128)(2,1)S(1)}, u32[]{:S(2)}, u32[]{:S(2)}) collective-permute-start(bf16[272,128]{1,0:T(8,128)(2,1)S(1)} %pad_maximum_fusion.2.users_ref), channel_id=1, source_target_pairs={{0,8},{1,9},{2,10},{3,11},{4,12},{5,13},{6,14},{7,15},{8,0},{9,1},... | collective-permute-start | bytes 208904 | tf_op jit(solution)/shard_map/ppermute | solution.py:282
  113.2 6.8 %collective-permute-start.11 = (bf16[256,128]{1,0:T(8,128)(2,1)S(1)}, bf16[256,128]{1,0:T(8,128)(2,1)S(1)}, u32[]{:S(2)}, u32[]{:S(2)}) collective-permute-start(bf16[256,128]{1,0:T(8,128)(2,1)S(1)} %get-tuple-element.31), channel_id=1, source_target_pairs={{0,504},{1,505},{2,506},{3,507},{4,508},{5,509},{6,510},{7,511},{8... | collective-permute-start | bytes 196616 | tf_op jit(solution)/shard_map/ppermute | solution.py:224
  120.0 2.8 collective-permute-done.11
  122.9 1.9 collective-permute-start.13
  124.8 5.1 %collective-permute-start.14 = (bf16[1056,128]{1,0:T(8,128)(2,1)S(1)}, bf16[1056,128]{1,0:T(8,128)(2,1)S(1)}, u32[]{:S(2)}, u32[]{:S(2)}) collective-permute-start(bf16[1056,128]{1,0:T(8,128)(2,1)S(1)} %constant_dynamic-update-slice_fusion.3.rest_0_), channel_id=1, source_target_pairs={{1,0},{2,1},{3,2},{4,3},{5,4},{6,5},{7,6},{0,7},{9,8},{10,9},{11,1... | collective-permute-start | bytes 811016 | tf_op jit(solution)/shard_map/ppermute | solution.py:266
  130.0 5.2 %collective-permute-done.13.rest_1_ = bf16[1056,128]{1,0:T(8,128)(2,1)S(1)} collective-permute-done((bf16[1056,128]{1,0:T(8,128)(2,1)S(1)}, bf16[1056,128]{1,0:T(8,128)(2,1)S(1)}, u32[]{:S(2)}, u32[]{:S(2)}) %collective-permute-start.13) | collective-permute-done | bytes 270368 | tf_op jit(solution)/shard_map/ppermute | solution.py:265
  137.2 5.1 %collective-permute-start.16 = (bf16[1056,128]{1,0:T(8,128)(2,1)S(1)}, bf16[1056,128]{1,0:T(8,128)(2,1)S(1)}, u32[]{:S(2)}, u32[]{:S(2)}) collective-permute-start(bf16[1056,128]{1,0:T(8,128)(2,1)S(1)} %collective-permute-done.14.rest_2_), channel_id=1, source_target_pairs={{1,0},{2,1},{3,2},{4,3},{5,4},{6,5},{7,6},{0,7},{9,8},{10,9},{11,1... | collective-permute-start | bytes 811016 | tf_op jit(solution)/shard_map/ppermute | solution.py:266
  142.3 3.6 %collective-permute-done.15.rest_3_ = bf16[1056,128]{1,0:T(8,128)(2,1)S(1)} collective-permute-done((bf16[1056,128]{1,0:T(8,128)(2,1)S(1)}, bf16[1056,128]{1,0:T(8,128)(2,1)S(1)}, u32[]{:S(2)}, u32[]{:S(2)}) %collective-permute-start.15) | collective-permute-done | bytes 270368 | tf_op jit(solution)/shard_map/ppermute | solution.py:265
  147.9 5.1 %collective-permute-start.18 = (bf16[1056,128]{1,0:T(8,128)(2,1)S(1)}, bf16[1056,128]{1,0:T(8,128)(2,1)S(1)}, u32[]{:S(2)}, u32[]{:S(2)}) collective-permute-start(bf16[1056,128]{1,0:T(8,128)(2,1)S(1)} %collective-permute-done.16.rest_4_), channel_id=1, source_target_pairs={{1,0},{2,1},{3,2},{4,3},{5,4},{6,5},{7,6},{0,7},{9,8},{10,9},{11,1... | collective-permute-start | bytes 811016 | tf_op jit(solution)/shard_map/ppermute | solution.py:266
  153.0 2.7 collective-permute-done.17.rest_5_
  155.8 1.9 collective-permute-start.19
  157.8 2.1 shard_map.154.dense_ref
  159.9 4.0 %collective-permute-done.19.rest_7_ = bf16[512,128]{1,0:T(8,128)(2,1)S(1)} collective-permute-done((bf16[512,128]{1,0:T(8,128)(2,1)S(1)}, bf16[512,128]{1,0:T(8,128)(2,1)S(1)}, u32[]{:S(2)}, u32[]{:S(2)}) %collective-permute-start.19) | collective-permute-done | bytes 131104 | tf_op jit(solution)/shard_map/ppermute | solution.py:268
  164.0 2.1 shard_map.160
  168.6 2.3 shard_map.164
  171.6 2.4 collective-permute-start.21
  174.0 5.8 %collective-permute-start.22 = (f32[256,128]{1,0:T(8,128)}, f32[256,128]{1,0:T(8,128)}, u32[]{:S(2)}, u32[]{:S(2)}) collective-permute-start(f32[256,128]{1,0:T(8,128)} %copy-done.58), channel_id=1, source_target_pairs={{0,496},{1,497},{2,498},{3,499},{4,500},{5,501},{6,502},{7,503},{8... | collective-permute-start | bytes 393224 | tf_op jit(solution)/shard_map/ppermute | solution.py:224
  179.8 1.9 collective-permute-start.23
  182.4 1.9 collective-permute-start.24
  185.3 4.1 %collective-permute-start.20 = (bf16[256,128]{1,0:T(8,128)(2,1)S(1)}, bf16[256,128]{1,0:T(8,128)(2,1)S(1)}, u32[]{:S(2)}, u32[]{:S(2)}) collective-permute-start(bf16[256,128]{1,0:T(8,128)(2,1)S(1)} %get-tuple-element.57), channel_id=1, source_target_pairs={{0,8},{1,9},{2,10},{3,11},{4,12},{5,13},{6,14},{7,15},{8,0},{9,1},... | collective-permute-start | bytes 196616 | tf_op jit(solution)/shard_map/ppermute | solution.py:270
  189.5 2.7 collective-permute-done.24.rest_7_
  192.1 3.5 %collective-permute-done.20.other_ref = bf16[256,128]{1,0:T(8,128)(2,1)S(1)} collective-permute-done((bf16[256,128]{1,0:T(8,128)(2,1)S(1)}, bf16[256,128]{1,0:T(8,128)(2,1)S(1)}, u32[]{:S(2)}, u32[]{:S(2)}) %collective-permute-start.20) | collective-permute-done | bytes 65568 | tf_op jit(solution)/shard_map/ppermute | solution.py:270
  197.5 2.8 shard_map.162
  200.3 3.7 %collective-permute-start.25 = (bf16[256,128]{1,0:T(8,128)(2,1)S(1)}, bf16[256,128]{1,0:T(8,128)(2,1)S(1)}, u32[]{:S(2)}, u32[]{:S(2)}) collective-permute-start(bf16[256,128]{1,0:T(8,128)(2,1)S(1)} %get-tuple-element.39), channel_id=1, source_target_pairs={{0,496},{1,497},{2,498},{3,499},{4,500},{5,501},{6,502},{7,503},{8... | collective-permute-start | bytes 196616 | tf_op jit(solution)/shard_map/ppermute | solution.py:224
  204.1 6.1 %collective-permute-start.27 = (bf16[272,128]{1,0:T(8,128)(2,1)S(1)}, bf16[272,128]{1,0:T(8,128)(2,1)S(1)}, u32[]{:S(2)}, u32[]{:S(2)}) collective-permute-start(bf16[272,128]{1,0:T(8,128)(2,1)S(1)} %copy-done.32), channel_id=1, source_target_pairs={{0,8},{1,9},{2,10},{3,11},{4,12},{5,13},{6,14},{7,15},{8,0},{9,1},... | collective-permute-start | bytes 208904 | tf_op jit(solution)/shard_map/ppermute | solution.py:282
  210.2 1.9 collective-permute-start.26
  212.2 8.5 %collective-permute-done.26 = bf16[256,128]{1,0:T(8,128)(2,1)S(1)} collective-permute-done((bf16[256,128]{1,0:T(8,128)(2,1)S(1)}, bf16[256,128]{1,0:T(8,128)(2,1)S(1)}, u32[]{:S(2)}, u32[]{:S(2)}) %collective-permute-start.26) | collective-permute-done | bytes 65568 | tf_op jit(solution)/shard_map/ppermute | solution.py:224
  220.7 2.6 collective-permute-start.29
  223.3 3.3 %collective-permute-start.28 = (bf16[1056,128]{1,0:T(8,128)(2,1)S(1)}, bf16[1056,128]{1,0:T(8,128)(2,1)S(1)}, u32[]{:S(2)}, u32[]{:S(2)}) collective-permute-start(bf16[1056,128]{1,0:T(8,128)(2,1)S(1)} %constant_dynamic-update-slice_fusion.8.rest_0_), channel_id=1, source_target_pairs={{0,1},{1,2},{2,3},{3,4},{4,5},{5,6},{6,7},{7,0},{8,9},{9,10},{10,1... | collective-permute-start | bytes 811016 | tf_op jit(solution)/shard_map/ppermute | solution.py:265
  226.6 3.4 %collective-permute-done.29.rest_2_ = bf16[1056,128]{1,0:T(8,128)(2,1)S(1)} collective-permute-done((bf16[1056,128]{1,0:T(8,128)(2,1)S(1)}, bf16[1056,128]{1,0:T(8,128)(2,1)S(1)}, u32[]{:S(2)}, u32[]{:S(2)}) %collective-permute-start.29) | collective-permute-done | bytes 270368 | tf_op jit(solution)/shard_map/ppermute | solution.py:266
  230.0 2.9 %collective-permute-start.31 = (bf16[1056,128]{1,0:T(8,128)(2,1)S(1)}, bf16[1056,128]{1,0:T(8,128)(2,1)S(1)}, u32[]{:S(2)}, u32[]{:S(2)}) collective-permute-start(bf16[1056,128]{1,0:T(8,128)(2,1)S(1)} %collective-permute-done.29.rest_2_), channel_id=1, source_target_pairs={{1,0},{2,1},{3,2},{4,3},{5,4},{6,5},{7,6},{0,7},{9,8},{10,9},{11,1... | collective-permute-start | bytes 811016 | tf_op jit(solution)/shard_map/ppermute | solution.py:266
  232.9 2.9 %collective-permute-start.30 = (bf16[1056,128]{1,0:T(8,128)(2,1)S(1)}, bf16[1056,128]{1,0:T(8,128)(2,1)S(1)}, u32[]{:S(2)}, u32[]{:S(2)}) collective-permute-start(bf16[1056,128]{1,0:T(8,128)(2,1)S(1)} %collective-permute-done.28.rest_1_), channel_id=1, source_target_pairs={{0,1},{1,2},{2,3},{3,4},{4,5},{5,6},{6,7},{7,0},{8,9},{9,10},{10,1... | collective-permute-start | bytes 811016 | tf_op jit(solution)/shard_map/ppermute | solution.py:265
  236.5 3.5 %collective-permute-done.31.rest_4_ = bf16[1056,128]{1,0:T(8,128)(2,1)S(1)} collective-permute-done((bf16[1056,128]{1,0:T(8,128)(2,1)S(1)}, bf16[1056,128]{1,0:T(8,128)(2,1)S(1)}, u32[]{:S(2)}, u32[]{:S(2)}) %collective-permute-start.31) | collective-permute-done | bytes 270368 | tf_op jit(solution)/shard_map/ppermute | solution.py:266
  240.0 4.1 %collective-permute-start.33 = (bf16[1056,128]{1,0:T(8,128)(2,1)S(1)}, bf16[1056,128]{1,0:T(8,128)(2,1)S(1)}, u32[]{:S(2)}, u32[]{:S(2)}) collective-permute-start(bf16[1056,128]{1,0:T(8,128)(2,1)S(1)} %collective-permute-done.31.rest_4_), channel_id=1, source_target_pairs={{1,0},{2,1},{3,2},{4,3},{5,4},{6,5},{7,6},{0,7},{9,8},{10,9},{11,1... | collective-permute-start | bytes 811016 | tf_op jit(solution)/shard_map/ppermute | solution.py:266
  244.1 1.9 collective-permute-start.32
  246.1 1.9 collective-permute-start.36
  248.0 3.0 %collective-permute-start.37 = (f32[256,128]{1,0:T(8,128)}, f32[256,128]{1,0:T(8,128)}, u32[]{:S(2)}, u32[]{:S(2)}) collective-permute-start(f32[256,128]{1,0:T(8,128)} %get-tuple-element.45), channel_id=1, source_target_pairs={{0,496},{1,497},{2,498},{3,499},{4,500},{5,501},{6,502},{7,503},{8... | collective-permute-start | bytes 393224 | tf_op jit(solution)/shard_map/ppermute | solution.py:224
  251.0 1.9 collective-permute-start.38
  253.6 5.1 %collective-permute-start.39 = (bf16[544,128]{1,0:T(8,128)(2,1)}, bf16[544,128]{1,0:T(8,128)(2,1)}, u32[]{:S(2)}, u32[]{:S(2)}) collective-permute-start(bf16[544,128]{1,0:T(8,128)(2,1)} %slice.146), channel_id=1, source_target_pairs={{1,0},{2,1},{3,2},{4,3},{5,4},{6,5},{7,6},{0,7},{9,8},{10,9},{11,1... | collective-permute-start | bytes 417800 | tf_op jit(solution)/shard_map/ppermute | solution.py:269
  259.4 1.9 collective-permute-start.34
  262.3 6.2 %collective-permute-done.34.rest_7_ = bf16[512,128]{1,0:T(8,128)(2,1)} collective-permute-done((bf16[512,128]{1,0:T(8,128)(2,1)}, bf16[512,128]{1,0:T(8,128)(2,1)}, u32[]{:S(2)}, u32[]{:S(2)}) %collective-permute-start.34) | collective-permute-done | bytes 131104 | tf_op jit(solution)/shard_map/ppermute | solution.py:268
  268.5 4.5 %collective-permute-start.35 = (bf16[256,128]{1,0:T(8,128)(2,1)S(1)}, bf16[256,128]{1,0:T(8,128)(2,1)S(1)}, u32[]{:S(2)}, u32[]{:S(2)}) collective-permute-start(bf16[256,128]{1,0:T(8,128)(2,1)S(1)} %get-tuple-element.55), channel_id=1, source_target_pairs={{0,8},{1,9},{2,10},{3,11},{4,12},{5,13},{6,14},{7,15},{8,0},{9,1},... | collective-permute-start | bytes 196616 | tf_op jit(solution)/shard_map/ppermute | solution.py:270
  277.7 3.2 %shard_map.163 = (f32[256,128]{1,0:T(8,128)}, f32[256,128]{1,0:T(8,128)}, f32[256,128]{1,0:T(8,128)}, bf16[256,128]{1,0:T(8,128)(2,1)}) custom-call(s32[32]{0:T(128)S(1)} %add.111.order_ref, f32[128]{0:T(128)S(1)} %copy-done.53, bf16[8192,128]{1,0:T(8,128)(2,1)S(1)} %shard_map.154.dense_ref, f32[256,128]{1,0:T(8,128)S(1)} %copy-done.42, ...), custom_call_target="tpu_custom_call" | custom-call | flops 536870912 | bytes 5242880 | tf_op jit(solution)/shard_map/pallas_call | solution.py:134
  280.9 2.8 shard_map.165
  (227 shorter events, 44.2 us)
Async XLA Ops:
  7.2 87.0 %reduce-scatter.4.cloned.1.call-start = ((), (), s32[]{:S(2)}) async-start(), calls=%async_computation.3 | async-start | bytes 1179648 | tf_op jit(solution)/shard_map/reduce_scatter | solution.py:254
  9.4 16.5 %copy-start.70 = (bf16[128]{0:T(256)(128)(2,1)}, bf16[128]{0:T(256)(128)(2,1)S(1)}, u32[]{:S(2)}) copy-start(bf16[128]{0:T(256)(128)(2,1)S(1)} %get-tuple-element.71) | copy-start | bytes 772
  11.3 14.6 %copy-start.62 = (bf16[16,128]{1,0:T(8,128)(2,1)}, bf16[16,128]{1,0:T(8,128)(2,1)S(1)}, u32[]{:S(2)}) copy-start(bf16[16,128]{1,0:T(8,128)(2,1)S(1)} %broadcast_in_dim.13) | copy-start | bytes 12292
  11.9 22.4 %collective-permute-start = (bf16[528,128]{1,0:T(8,128)(2,1)}, bf16[528,128]{1,0:T(8,128)(2,1)}, u32[]{:S(2)}, u32[]{:S(2)}) collective-permute-start(bf16[528,128]{1,0:T(8,128)(2,1)} %pad_maximum_fusion), channel_id=1, source_target_pairs={{0,8},{1,9},{2,10},{3,11},{4,12},{5,13},{6,14},{7,15},{8,0},{9,1},... | collective-permute-start | bytes 405512 | tf_op jit(solution)/shard_map/ppermute | solution.py:249
  34.3 37.3 %copy-start.64 = (s32[8,2]{1,0:T(8,128)S(1)}, s32[8,2]{1,0:T(8,128)}, u32[]{:S(2)}) copy-start(s32[8,2]{1,0:T(8,128)} %get-tuple-element.73) | copy-start | bytes 196
  34.3 150.0 %reduce-scatter.6.cloned.1.call-start = ((), (), s32[]{:S(2)}) async-start(), calls=%async_computation.4 | async-start | bytes 1179648 | tf_op jit(solution)/shard_map/reduce_scatter | solution.py:254
  37.7 11.4 %collective-permute-start.1 = (bf16[1056,128]{1,0:T(8,128)(2,1)S(1)}, bf16[1056,128]{1,0:T(8,128)(2,1)S(1)}, u32[]{:S(2)}, u32[]{:S(2)}) collective-permute-start(bf16[1056,128]{1,0:T(8,128)(2,1)S(1)} %slice_dynamic-update-slice_fusion.rest_0_), channel_id=1, source_target_pairs={{0,1},{1,2},{2,3},{3,4},{4,5},{5,6},{6,7},{7,0},{8,9},{9,10},{10,1... | collective-permute-start | bytes 811016 | tf_op jit(solution)/shard_map/ppermute | solution.py:265
  40.9 11.1 %collective-permute-start.2 = (bf16[1056,128]{1,0:T(8,128)(2,1)S(1)}, bf16[1056,128]{1,0:T(8,128)(2,1)S(1)}, u32[]{:S(2)}, u32[]{:S(2)}) collective-permute-start(bf16[1056,128]{1,0:T(8,128)(2,1)S(1)} %slice_dynamic-update-slice_fusion.rest_0_), channel_id=1, source_target_pairs={{1,0},{2,1},{3,2},{4,3},{5,4},{6,5},{7,6},{0,7},{9,8},{10,9},{11,1... | collective-permute-start | bytes 811016 | tf_op jit(solution)/shard_map/ppermute | solution.py:266
  49.1 14.9 %collective-permute-start.3 = (bf16[1056,128]{1,0:T(8,128)(2,1)S(1)}, bf16[1056,128]{1,0:T(8,128)(2,1)}, u32[]{:S(2)}, u32[]{:S(2)}) collective-permute-start(bf16[1056,128]{1,0:T(8,128)(2,1)S(1)} %collective-permute-done.1.rest_1_), channel_id=1, source_target_pairs={{0,1},{1,2},{2,3},{3,4},{4,5},{5,6},{6,7},{7,0},{8,9},{9,10},{10,1... | collective-permute-start | bytes 811016 | tf_op jit(solution)/shard_map/ppermute | solution.py:265
  52.0 13.9 %collective-permute-start.4 = (bf16[1056,128]{1,0:T(8,128)(2,1)S(1)}, bf16[1056,128]{1,0:T(8,128)(2,1)}, u32[]{:S(2)}, u32[]{:S(2)}) collective-permute-start(bf16[1056,128]{1,0:T(8,128)(2,1)S(1)} %collective-permute-done.2.rest_2_), channel_id=1, source_target_pairs={{1,0},{2,1},{3,2},{4,3},{5,4},{6,5},{7,6},{0,7},{9,8},{10,9},{11,1... | collective-permute-start | bytes 811016 | tf_op jit(solution)/shard_map/ppermute | solution.py:266
  64.0 13.0 %collective-permute-start.5 = (bf16[1056,128]{1,0:T(8,128)(2,1)}, bf16[1056,128]{1,0:T(8,128)(2,1)}, u32[]{:S(2)}, u32[]{:S(2)}) collective-permute-start(bf16[1056,128]{1,0:T(8,128)(2,1)} %collective-permute-done.3.rest_3_), channel_id=1, source_target_pairs={{0,1},{1,2},{2,3},{3,4},{4,5},{5,6},{6,7},{7,0},{8,9},{9,10},{10,1... | collective-permute-start | bytes 811016 | tf_op jit(solution)/shard_map/ppermute | solution.py:265
  66.0 14.7 %collective-permute-start.6 = (bf16[1056,128]{1,0:T(8,128)(2,1)}, bf16[1056,128]{1,0:T(8,128)(2,1)S(1)}, u32[]{:S(2)}, u32[]{:S(2)}) collective-permute-start(bf16[1056,128]{1,0:T(8,128)(2,1)} %collective-permute-done.4.rest_4_), channel_id=1, source_target_pairs={{1,0},{2,1},{3,2},{4,3},{5,4},{6,5},{7,6},{0,7},{9,8},{10,9},{11,1... | collective-permute-start | bytes 811016 | tf_op jit(solution)/shard_map/ppermute | solution.py:266
  78.1 8.3 %collective-permute-start.7 = (bf16[512,128]{1,0:T(8,128)(2,1)S(1)}, bf16[512,128]{1,0:T(8,128)(2,1)S(1)}, u32[]{:S(2)}, u32[]{:S(2)}) collective-permute-start(bf16[512,128]{1,0:T(8,128)(2,1)S(1)} %slice.135), channel_id=1, source_target_pairs={{0,1},{1,2},{2,3},{3,4},{4,5},{5,6},{6,7},{7,0},{8,9},{9,10},{10,1... | collective-permute-start | bytes 393224 | tf_op jit(solution)/shard_map/ppermute | solution.py:268
  81.3 15.8 %collective-permute-start.9 = (bf16[544,128]{1,0:T(8,128)(2,1)}, bf16[544,128]{1,0:T(8,128)(2,1)}, u32[]{:S(2)}, u32[]{:S(2)}) collective-permute-start(bf16[544,128]{1,0:T(8,128)(2,1)} %slice.138), channel_id=1, source_target_pairs={{1,0},{2,1},{3,2},{4,3},{5,4},{6,5},{7,6},{0,7},{9,8},{10,9},{11,1... | collective-permute-start | bytes 417800 | tf_op jit(solution)/shard_map/ppermute | solution.py:269
  94.1 167.3 %reduce-scatter.8.cloned.1.call-start = ((), (), s32[]{:S(2)}) async-start(), calls=%async_computation.5 | async-start | bytes 1179648 | tf_op jit(solution)/shard_map/reduce_scatter | solution.py:254
  95.1 10.1 %collective-permute-start.8 = (bf16[256,128]{1,0:T(8,128)(2,1)S(1)}, bf16[256,128]{1,0:T(8,128)(2,1)S(1)}, u32[]{:S(2)}, u32[]{:S(2)}) collective-permute-start(bf16[256,128]{1,0:T(8,128)(2,1)S(1)} %get-tuple-element.59), channel_id=1, source_target_pairs={{0,8},{1,9},{2,10},{3,11},{4,12},{5,13},{6,14},{7,15},{8,0},{9,1},... | collective-permute-start | bytes 196616 | tf_op jit(solution)/shard_map/ppermute | solution.py:270
  105.3 17.5 %copy-start.36 = (bf16[256,128]{1,0:T(8,128)(2,1)S(1)}, bf16[256,128]{1,0:T(8,128)(2,1)}, u32[]{:S(2)}) copy-start(bf16[256,128]{1,0:T(8,128)(2,1)} %copy-done.35) | copy-start | bytes 196612
  105.3 17.5 %copy-start.69 = (bf16[128]{0:T(256)(128)(2,1)S(1)}, bf16[128]{0:T(256)(128)(2,1)}, u32[]{:S(2)}) copy-start(bf16[128]{0:T(256)(128)(2,1)} %get-tuple-element.70) | copy-start | bytes 772
  105.3 52.4 %copy-start.54 = (s32[36]{0:T(128)S(1)}, s32[36]{0:T(128)}, u32[]{:S(2)}) copy-start(s32[36]{0:T(128)} %get-tuple-element.65.slots_ref) | copy-start | bytes 436
  107.5 29.6 %copy-start.57 = (f32[256,128]{1,0:T(8,128)}, f32[256,128]{1,0:T(8,128)S(1)}, u32[]{:S(2)}) copy-start(f32[256,128]{1,0:T(8,128)S(1)} %get-tuple-element.38) | copy-start | bytes 393220
  107.6 29.6 %copy-start.58 = (f32[256,128]{1,0:T(8,128)}, f32[256,128]{1,0:T(8,128)S(1)}, u32[]{:S(2)}) copy-start(f32[256,128]{1,0:T(8,128)S(1)} %get-tuple-element.37) | copy-start | bytes 393220
  107.6 29.6 %copy-start.59 = (f32[256,128]{1,0:T(8,128)}, f32[256,128]{1,0:T(8,128)S(1)}, u32[]{:S(2)}) copy-start(f32[256,128]{1,0:T(8,128)S(1)} %get-tuple-element.36) | copy-start | bytes 393220
  107.6 12.4 %collective-permute-start.10 = (bf16[256,128]{1,0:T(8,128)(2,1)S(1)}, bf16[256,128]{1,0:T(8,128)(2,1)S(1)}, u32[]{:S(2)}, u32[]{:S(2)}) collective-permute-start(bf16[256,128]{1,0:T(8,128)(2,1)S(1)} %get-tuple-element.31), channel_id=1, source_target_pairs={{0,496},{1,497},{2,498},{3,499},{4,500},{5,501},{6,502},{7,503},{8... | collective-permute-start | bytes 196616 | tf_op jit(solution)/shard_map/ppermute | solution.py:224
  109.5 13.4 %collective-permute-start.12 = (bf16[272,128]{1,0:T(8,128)(2,1)S(1)}, bf16[272,128]{1,0:T(8,128)(2,1)S(1)}, u32[]{:S(2)}, u32[]{:S(2)}) collective-permute-start(bf16[272,128]{1,0:T(8,128)(2,1)S(1)} %pad_maximum_fusion.2.users_ref), channel_id=1, source_target_pairs={{0,8},{1,9},{2,10},{3,11},{4,12},{5,13},{6,14},{7,15},{8,0},{9,1},... | collective-permute-start | bytes 208904 | tf_op jit(solution)/shard_map/ppermute | solution.py:282
  113.2 9.6 %collective-permute-start.11 = (bf16[256,128]{1,0:T(8,128)(2,1)S(1)}, bf16[256,128]{1,0:T(8,128)(2,1)S(1)}, u32[]{:S(2)}, u32[]{:S(2)}) collective-permute-start(bf16[256,128]{1,0:T(8,128)(2,1)S(1)} %get-tuple-element.31), channel_id=1, source_target_pairs={{0,504},{1,505},{2,506},{3,507},{4,508},{5,509},{6,510},{7,511},{8... | collective-permute-start | bytes 196616 | tf_op jit(solution)/shard_map/ppermute | solution.py:224
  122.9 41.0 %copy-start.6 = (bf16[1056,128]{1,0:T(8,128)(2,1)}, bf16[1056,128]{1,0:T(8,128)(2,1)S(1)}, u32[]{:S(2)}) copy-start(bf16[1056,128]{1,0:T(8,128)(2,1)S(1)} %constant_dynamic-update-slice_fusion.3.rest_0_) | copy-start | bytes 811012
  122.9 12.3 %collective-permute-start.13 = (bf16[1056,128]{1,0:T(8,128)(2,1)S(1)}, bf16[1056,128]{1,0:T(8,128)(2,1)S(1)}, u32[]{:S(2)}, u32[]{:S(2)}) collective-permute-start(bf16[1056,128]{1,0:T(8,128)(2,1)S(1)} %constant_dynamic-update-slice_fusion.3.rest_0_), channel_id=1, source_target_pairs={{0,1},{1,2},{2,3},{3,4},{4,5},{5,6},{6,7},{7,0},{8,9},{9,10},{10,1... | collective-permute-start | bytes 811016 | tf_op jit(solution)/shard_map/ppermute | solution.py:265
  124.8 12.3 %collective-permute-start.14 = (bf16[1056,128]{1,0:T(8,128)(2,1)S(1)}, bf16[1056,128]{1,0:T(8,128)(2,1)S(1)}, u32[]{:S(2)}, u32[]{:S(2)}) collective-permute-start(bf16[1056,128]{1,0:T(8,128)(2,1)S(1)} %constant_dynamic-update-slice_fusion.3.rest_0_), channel_id=1, source_target_pairs={{1,0},{2,1},{3,2},{4,3},{5,4},{6,5},{7,6},{0,7},{9,8},{10,9},{11,1... | collective-permute-start | bytes 811016 | tf_op jit(solution)/shard_map/ppermute | solution.py:266
  135.2 28.7 %copy-start.12 = (bf16[1056,128]{1,0:T(8,128)(2,1)}, bf16[1056,128]{1,0:T(8,128)(2,1)S(1)}, u32[]{:S(2)}) copy-start(bf16[1056,128]{1,0:T(8,128)(2,1)S(1)} %collective-permute-done.13.rest_1_) | copy-start | bytes 811012
  135.2 10.7 %collective-permute-start.15 = (bf16[1056,128]{1,0:T(8,128)(2,1)S(1)}, bf16[1056,128]{1,0:T(8,128)(2,1)S(1)}, u32[]{:S(2)}, u32[]{:S(2)}) collective-permute-start(bf16[1056,128]{1,0:T(8,128)(2,1)S(1)} %collective-permute-done.13.rest_1_), channel_id=1, source_target_pairs={{0,1},{1,2},{2,3},{3,4},{4,5},{5,6},{6,7},{7,0},{8,9},{9,10},{10,1... | collective-permute-start | bytes 811016 | tf_op jit(solution)/shard_map/ppermute | solution.py:265
  137.2 26.7 %copy-start.14 = (bf16[1056,128]{1,0:T(8,128)(2,1)}, bf16[1056,128]{1,0:T(8,128)(2,1)S(1)}, u32[]{:S(2)}) copy-start(bf16[1056,128]{1,0:T(8,128)(2,1)S(1)} %collective-permute-done.14.rest_2_) | copy-start | bytes 811012
  137.2 10.7 %collective-permute-start.16 = (bf16[1056,128]{1,0:T(8,128)(2,1)S(1)}, bf16[1056,128]{1,0:T(8,128)(2,1)S(1)}, u32[]{:S(2)}, u32[]{:S(2)}) collective-permute-start(bf16[1056,128]{1,0:T(8,128)(2,1)S(1)} %collective-permute-done.14.rest_2_), channel_id=1, source_target_pairs={{1,0},{2,1},{3,2},{4,3},{5,4},{6,5},{7,6},{0,7},{9,8},{10,9},{11,1... | collective-permute-start | bytes 811016 | tf_op jit(solution)/shard_map/ppermute | solution.py:266
  145.9 17.9 %copy-start.16 = (bf16[1056,128]{1,0:T(8,128)(2,1)}, bf16[1056,128]{1,0:T(8,128)(2,1)S(1)}, u32[]{:S(2)}) copy-start(bf16[1056,128]{1,0:T(8,128)(2,1)S(1)} %collective-permute-done.15.rest_3_) | copy-start | bytes 811012
  145.9 9.8 %collective-permute-start.17 = (bf16[1056,128]{1,0:T(8,128)(2,1)S(1)}, bf16[1056,128]{1,0:T(8,128)(2,1)S(1)}, u32[]{:S(2)}, u32[]{:S(2)}) collective-permute-start(bf16[1056,128]{1,0:T(8,128)(2,1)S(1)} %collective-permute-done.15.rest_3_), channel_id=1, source_target_pairs={{0,1},{1,2},{2,3},{3,4},{4,5},{5,6},{6,7},{7,0},{8,9},{9,10},{10,1... | collective-permute-start | bytes 811016 | tf_op jit(solution)/shard_map/ppermute | solution.py:265
  147.9 16.0 %copy-start.18 = (bf16[1056,128]{1,0:T(8,128)(2,1)}, bf16[1056,128]{1,0:T(8,128)(2,1)S(1)}, u32[]{:S(2)}) copy-start(bf16[1056,128]{1,0:T(8,128)(2,1)S(1)} %collective-permute-done.16.rest_4_) | copy-start | bytes 811012
  147.9 12.0 %collective-permute-start.18 = (bf16[1056,128]{1,0:T(8,128)(2,1)S(1)}, bf16[1056,128]{1,0:T(8,128)(2,1)S(1)}, u32[]{:S(2)}, u32[]{:S(2)}) collective-permute-start(bf16[1056,128]{1,0:T(8,128)(2,1)S(1)} %collective-permute-done.16.rest_4_), channel_id=1, source_target_pairs={{1,0},{2,1},{3,2},{4,3},{5,4},{6,5},{7,6},{0,7},{9,8},{10,9},{11,1... | collective-permute-start | bytes 811016 | tf_op jit(solution)/shard_map/ppermute | solution.py:266
  155.8 8.1 %collective-permute-start.19 = (bf16[512,128]{1,0:T(8,128)(2,1)S(1)}, bf16[512,128]{1,0:T(8,128)(2,1)S(1)}, u32[]{:S(2)}, u32[]{:S(2)}) collective-permute-start(bf16[512,128]{1,0:T(8,128)(2,1)S(1)} %slice.139), channel_id=1, source_target_pairs={{0,1},{1,2},{2,3},{3,4},{4,5},{5,6},{6,7},{7,0},{8,9},{9,10},{10,1... | collective-permute-start | bytes 393224 | tf_op jit(solution)/shard_map/ppermute | solution.py:268
  171.5 24.0 %copy-start.5 = (bf16[1056,128]{1,0:T(8,128)(2,1)S(1)}, bf16[1056,128]{1,0:T(8,128)(2,1)}, u32[]{:S(2)}) copy-start(bf16[1056,128]{1,0:T(8,128)(2,1)} %copy-done.4) | copy-start | bytes 811012
  171.5 24.0 %copy-start.7 = (bf16[1056,128]{1,0:T(8,128)(2,1)S(1)}, bf16[1056,128]{1,0:T(8,128)(2,1)}, u32[]{:S(2)}) copy-start(bf16[1056,128]{1,0:T(8,128)(2,1)} %copy-done.6) | copy-start | bytes 811012
  171.5 24.0 %copy-start.13 = (bf16[1056,128]{1,0:T(8,128)(2,1)S(1)}, bf16[1056,128]{1,0:T(8,128)(2,1)}, u32[]{:S(2)}) copy-start(bf16[1056,128]{1,0:T(8,128)(2,1)} %copy-done.12) | copy-start | bytes 811012
  171.5 24.0 %copy-start.15 = (bf16[1056,128]{1,0:T(8,128)(2,1)S(1)}, bf16[1056,128]{1,0:T(8,128)(2,1)}, u32[]{:S(2)}) copy-start(bf16[1056,128]{1,0:T(8,128)(2,1)} %copy-done.14) | copy-start | bytes 811012
  171.6 17.9 %collective-permute-start.21 = (f32[256,128]{1,0:T(8,128)}, f32[256,128]{1,0:T(8,128)}, u32[]{:S(2)}, u32[]{:S(2)}) collective-permute-start(f32[256,128]{1,0:T(8,128)} %copy-done.59), channel_id=1, source_target_pairs={{0,496},{1,497},{2,498},{3,499},{4,500},{5,501},{6,502},{7,503},{8... | collective-permute-start | bytes 393224 | tf_op jit(solution)/shard_map/ppermute | solution.py:224
  174.0 15.4 %collective-permute-start.22 = (f32[256,128]{1,0:T(8,128)}, f32[256,128]{1,0:T(8,128)}, u32[]{:S(2)}, u32[]{:S(2)}) collective-permute-start(f32[256,128]{1,0:T(8,128)} %copy-done.58), channel_id=1, source_target_pairs={{0,496},{1,497},{2,498},{3,499},{4,500},{5,501},{6,502},{7,503},{8... | collective-permute-start | bytes 393224 | tf_op jit(solution)/shard_map/ppermute | solution.py:224
  179.8 9.6 %collective-permute-start.23 = (f32[256,128]{1,0:T(8,128)}, f32[256,128]{1,0:T(8,128)}, u32[]{:S(2)}, u32[]{:S(2)}) collective-permute-start(f32[256,128]{1,0:T(8,128)} %copy-done.57), channel_id=1, source_target_pairs={{0,496},{1,497},{2,498},{3,499},{4,500},{5,501},{6,502},{7,503},{8... | collective-permute-start | bytes 393224 | tf_op jit(solution)/shard_map/ppermute | solution.py:224
  182.4 9.7 %collective-permute-start.24 = (bf16[544,128]{1,0:T(8,128)(2,1)}, bf16[544,128]{1,0:T(8,128)(2,1)}, u32[]{:S(2)}, u32[]{:S(2)}) collective-permute-start(bf16[544,128]{1,0:T(8,128)(2,1)} %slice.142), channel_id=1, source_target_pairs={{1,0},{2,1},{3,2},{4,3},{5,4},{6,5},{7,6},{0,7},{9,8},{10,9},{11,1... | collective-permute-start | bytes 417800 | tf_op jit(solution)/shard_map/ppermute | solution.py:269
  185.3 10.3 %collective-permute-start.20 = (bf16[256,128]{1,0:T(8,128)(2,1)S(1)}, bf16[256,128]{1,0:T(8,128)(2,1)S(1)}, u32[]{:S(2)}, u32[]{:S(2)}) collective-permute-start(bf16[256,128]{1,0:T(8,128)(2,1)S(1)} %get-tuple-element.57), channel_id=1, source_target_pairs={{0,8},{1,9},{2,10},{3,11},{4,12},{5,13},{6,14},{7,15},{8,0},{9,1},... | collective-permute-start | bytes 196616 | tf_op jit(solution)/shard_map/ppermute | solution.py:270
  197.5 23.2 %copy-start.34 = (bf16[256,128]{1,0:T(8,128)(2,1)S(1)}, bf16[256,128]{1,0:T(8,128)(2,1)}, u32[]{:S(2)}) copy-start(bf16[256,128]{1,0:T(8,128)(2,1)} %copy-done.33) | copy-start | bytes 196612
  200.3 72.7 %copy-start.53 = (f32[128]{0:T(128)S(1)}, f32[128]{0:T(128)}, u32[]{:S(2)}) copy-start(f32[128]{0:T(128)} %get-tuple-element.68.counts_ref) | copy-start | bytes 1540
  200.3 11.8 %collective-permute-start.25 = (bf16[256,128]{1,0:T(8,128)(2,1)S(1)}, bf16[256,128]{1,0:T(8,128)(2,1)S(1)}, u32[]{:S(2)}, u32[]{:S(2)}) collective-permute-start(bf16[256,128]{1,0:T(8,128)(2,1)S(1)} %get-tuple-element.39), channel_id=1, source_target_pairs={{0,496},{1,497},{2,498},{3,499},{4,500},{5,501},{6,502},{7,503},{8... | collective-permute-start | bytes 196616 | tf_op jit(solution)/shard_map/ppermute | solution.py:224
  204.1 16.6 %collective-permute-start.27 = (bf16[272,128]{1,0:T(8,128)(2,1)S(1)}, bf16[272,128]{1,0:T(8,128)(2,1)S(1)}, u32[]{:S(2)}, u32[]{:S(2)}) collective-permute-start(bf16[272,128]{1,0:T(8,128)(2,1)S(1)} %copy-done.32), channel_id=1, source_target_pairs={{0,8},{1,9},{2,10},{3,11},{4,12},{5,13},{6,14},{7,15},{8,0},{9,1},... | collective-permute-start | bytes 208904 | tf_op jit(solution)/shard_map/ppermute | solution.py:282
  210.2 10.4 %collective-permute-start.26 = (bf16[256,128]{1,0:T(8,128)(2,1)S(1)}, bf16[256,128]{1,0:T(8,128)(2,1)S(1)}, u32[]{:S(2)}, u32[]{:S(2)}) collective-permute-start(bf16[256,128]{1,0:T(8,128)(2,1)S(1)} %get-tuple-element.39), channel_id=1, source_target_pairs={{0,504},{1,505},{2,506},{3,507},{4,508},{5,509},{6,510},{7,511},{8... | collective-permute-start | bytes 196616 | tf_op jit(solution)/shard_map/ppermute | solution.py:224
  220.7 9.2 %collective-permute-start.29 = (bf16[1056,128]{1,0:T(8,128)(2,1)S(1)}, bf16[1056,128]{1,0:T(8,128)(2,1)S(1)}, u32[]{:S(2)}, u32[]{:S(2)}) collective-permute-start(bf16[1056,128]{1,0:T(8,128)(2,1)S(1)} %constant_dynamic-update-slice_fusion.8.rest_0_), channel_id=1, source_target_pairs={{1,0},{2,1},{3,2},{4,3},{5,4},{6,5},{7,6},{0,7},{9,8},{10,9},{11,1... | collective-permute-start | bytes 811016 | tf_op jit(solution)/shard_map/ppermute | solution.py:266
  223.3 9.6 %collective-permute-start.28 = (bf16[1056,128]{1,0:T(8,128)(2,1)S(1)}, bf16[1056,128]{1,0:T(8,128)(2,1)S(1)}, u32[]{:S(2)}, u32[]{:S(2)}) collective-permute-start(bf16[1056,128]{1,0:T(8,128)(2,1)S(1)} %constant_dynamic-update-slice_fusion.8.rest_0_), channel_id=1, source_target_pairs={{0,1},{1,2},{2,3},{3,4},{4,5},{5,6},{6,7},{7,0},{8,9},{9,10},{10,1... | collective-permute-start | bytes 811016 | tf_op jit(solution)/shard_map/ppermute | solution.py:265
  230.0 10.0 %collective-permute-start.31 = (bf16[1056,128]{1,0:T(8,128)(2,1)S(1)}, bf16[1056,128]{1,0:T(8,128)(2,1)S(1)}, u32[]{:S(2)}, u32[]{:S(2)}) collective-permute-start(bf16[1056,128]{1,0:T(8,128)(2,1)S(1)} %collective-permute-done.29.rest_2_), channel_id=1, source_target_pairs={{1,0},{2,1},{3,2},{4,3},{5,4},{6,5},{7,6},{0,7},{9,8},{10,9},{11,1... | collective-permute-start | bytes 811016 | tf_op jit(solution)/shard_map/ppermute | solution.py:266
  232.9 11.2 %collective-permute-start.30 = (bf16[1056,128]{1,0:T(8,128)(2,1)S(1)}, bf16[1056,128]{1,0:T(8,128)(2,1)S(1)}, u32[]{:S(2)}, u32[]{:S(2)}) collective-permute-start(bf16[1056,128]{1,0:T(8,128)(2,1)S(1)} %collective-permute-done.28.rest_1_), channel_id=1, source_target_pairs={{0,1},{1,2},{2,3},{3,4},{4,5},{5,6},{6,7},{7,0},{8,9},{9,10},{10,1... | collective-permute-start | bytes 811016 | tf_op jit(solution)/shard_map/ppermute | solution.py:265
  240.0 13.0 %collective-permute-start.33 = (bf16[1056,128]{1,0:T(8,128)(2,1)S(1)}, bf16[1056,128]{1,0:T(8,128)(2,1)S(1)}, u32[]{:S(2)}, u32[]{:S(2)}) collective-permute-start(bf16[1056,128]{1,0:T(8,128)(2,1)S(1)} %collective-permute-done.31.rest_4_), channel_id=1, source_target_pairs={{1,0},{2,1},{3,2},{4,3},{5,4},{6,5},{7,6},{0,7},{9,8},{10,9},{11,1... | collective-permute-start | bytes 811016 | tf_op jit(solution)/shard_map/ppermute | solution.py:266
  244.1 14.7 %copy-start.28 = (bf16[1056,128]{1,0:T(8,128)(2,1)}, bf16[1056,128]{1,0:T(8,128)(2,1)S(1)}, u32[]{:S(2)}) copy-start(bf16[1056,128]{1,0:T(8,128)(2,1)S(1)} %collective-permute-done.30.rest_3_) | copy-start | bytes 811012
  244.1 14.6 %collective-permute-start.32 = (bf16[1056,128]{1,0:T(8,128)(2,1)S(1)}, bf16[1056,128]{1,0:T(8,128)(2,1)S(1)}, u32[]{:S(2)}, u32[]{:S(2)}) collective-permute-start(bf16[1056,128]{1,0:T(8,128)(2,1)S(1)} %collective-permute-done.30.rest_3_), channel_id=1, source_target_pairs={{0,1},{1,2},{2,3},{3,4},{4,5},{5,6},{6,7},{7,0},{8,9},{9,10},{10,1... | collective-permute-start | bytes 811016 | tf_op jit(solution)/shard_map/ppermute | solution.py:265
  246.1 34.8 %collective-permute-start.36 = (f32[256,128]{1,0:T(8,128)}, f32[256,128]{1,0:T(8,128)}, u32[]{:S(2)}, u32[]{:S(2)}) collective-permute-start(f32[256,128]{1,0:T(8,128)} %get-tuple-element.44), channel_id=1, source_target_pairs={{0,496},{1,497},{2,498},{3,499},{4,500},{5,501},{6,502},{7,503},{8... | collective-permute-start | bytes 393224 | tf_op jit(solution)/shard_map/ppermute | solution.py:224
  248.0 32.8 %collective-permute-start.37 = (f32[256,128]{1,0:T(8,128)}, f32[256,128]{1,0:T(8,128)}, u32[]{:S(2)}, u32[]{:S(2)}) collective-permute-start(f32[256,128]{1,0:T(8,128)} %get-tuple-element.45), channel_id=1, source_target_pairs={{0,496},{1,497},{2,498},{3,499},{4,500},{5,501},{6,502},{7,503},{8... | collective-permute-start | bytes 393224 | tf_op jit(solution)/shard_map/ppermute | solution.py:224
  251.0 29.8 %collective-permute-start.38 = (f32[256,128]{1,0:T(8,128)}, f32[256,128]{1,0:T(8,128)}, u32[]{:S(2)}, u32[]{:S(2)}) collective-permute-start(f32[256,128]{1,0:T(8,128)} %get-tuple-element.46), channel_id=1, source_target_pairs={{0,496},{1,497},{2,498},{3,499},{4,500},{5,501},{6,502},{7,503},{8... | collective-permute-start | bytes 393224 | tf_op jit(solution)/shard_map/ppermute | solution.py:224
  253.6 27.2 %collective-permute-start.39 = (bf16[544,128]{1,0:T(8,128)(2,1)}, bf16[544,128]{1,0:T(8,128)(2,1)}, u32[]{:S(2)}, u32[]{:S(2)}) collective-permute-start(bf16[544,128]{1,0:T(8,128)(2,1)} %slice.146), channel_id=1, source_target_pairs={{1,0},{2,1},{3,2},{4,3},{5,4},{6,5},{7,6},{0,7},{9,8},{10,9},{11,1... | collective-permute-start | bytes 417800 | tf_op jit(solution)/shard_map/ppermute | solution.py:269
  259.4 9.0 %collective-permute-start.34 = (bf16[512,128]{1,0:T(8,128)(2,1)}, bf16[512,128]{1,0:T(8,128)(2,1)}, u32[]{:S(2)}, u32[]{:S(2)}) collective-permute-start(bf16[512,128]{1,0:T(8,128)(2,1)} %slice.143), channel_id=1, source_target_pairs={{0,1},{1,2},{2,3},{3,4},{4,5},{5,6},{6,7},{7,0},{8,9},{9,10},{10,1... | collective-permute-start | bytes 393224 | tf_op jit(solution)/shard_map/ppermute | solution.py:268
  268.5 12.4 %collective-permute-start.35 = (bf16[256,128]{1,0:T(8,128)(2,1)S(1)}, bf16[256,128]{1,0:T(8,128)(2,1)S(1)}, u32[]{:S(2)}, u32[]{:S(2)}) collective-permute-start(bf16[256,128]{1,0:T(8,128)(2,1)S(1)} %get-tuple-element.55), channel_id=1, source_target_pairs={{0,8},{1,9},{2,10},{3,11},{4,12},{5,13},{6,14},{7,15},{8,0},{9,1},... | collective-permute-start | bytes 196616 | tf_op jit(solution)/shard_map/ppermute | solution.py:270
  (50 other events, 235.0 us)
Sparse Core Ops, SparseCore 0:
  34.5 41.4 reduce-scatter.3
  94.2 40.0 reduce-scatter.5
  171.7 42.8 reduce-scatter.7

commit v3 on v2

v3 whole, which is shorter than its diff:
```python
import functools

import jax
import jax.numpy as jnp
from jax import lax
from jax.experimental import pallas as pl
from jax.experimental.pallas import tpu as pltpu
from jax.sharding import PartitionSpec as P

K = 128
TILE = 128
MAXT = 36
STEPS = 3
RING = 8
USER_ROWS = 256
ITEM_ROWS = 256
USER_TILES = 2
ITEM_TILES = 32
COUNT_ROWS = 16
PART = USER_ROWS + COUNT_ROWS
PAIRS = USER_TILES * ITEM_TILES
DISTANCES = (0, -1, 1, -2, 2, -3, 3, -4)


LEARN_RATE = 0.01
BETA_ONE = 0.8
BETA_TWO = 0.95
ADAM_EPS = 1e-08
DECAY_REG = 0.05
GRAD_SCALE = 0.03125

VMEM = pl.BlockSpec(memory_space=pltpu.VMEM)
SMEM = pl.BlockSpec(memory_space=pltpu.SMEM)
ANY = pl.BlockSpec(memory_space=pl.ANY)
F32 = jnp.float32
BF16 = jnp.bfloat16


def shape(rows, dtype=F32):
    return jax.ShapeDtypeStruct((rows, K), dtype)


def adam_update(param, first, second, grad):
    first = BETA_ONE * first + (1.0 - BETA_ONE) * grad
    second = BETA_TWO * second + (1.0 - BETA_TWO) * grad * grad
    return (param - LEARN_RATE * first / (jnp.sqrt(second) + ADAM_EPS), first, second)


def kernel_call(body, outs, in_specs, out_specs=None, scratch=(), flops=0, moved=1 << 20):
    return pl.pallas_call(
        body,
        out_shape=outs,
        in_specs=in_specs,
        out_specs=out_specs or jax.tree.map(lambda _: VMEM, outs),
        scratch_shapes=list(scratch),
        cost_estimate=pl.CostEstimate(flops=flops, bytes_accessed=moved, transcendentals=0),
        compiler_params=pltpu.CompilerParams(vmem_limit_bytes=40 << 20),
    )


def loaded(refs):
    if len(refs) == 3:
        return [ref[...] for ref in refs]
    return [refs[0][i * 256 : (i + 1) * 256] for i in range(3)]


def stored(refs, values):
    if len(refs) == 3:
        for ref, value in zip(refs, values):
            ref[...] = value
    else:
        for i, value in enumerate(values):
            refs[0][i * 256 : (i + 1) * 256] = value


def owned_tile(me, swap, place, half):
    plane = me // RING
    plane = 1 - plane if swap else plane
    return (plane * RING + place) * 2 + half


def opening_body(users_at, items_at, live, users, items, first_out, rows_out, counts_out):
    lane = lax.broadcasted_iota(jnp.int32, (COUNT_ROWS, K), 1)

    def clear(i, carry):
        counts_out[i] = 0.0
        return carry

    lax.fori_loop(0, STEPS * PAIRS, clear, 0)
    for s in range(STEPS):

        def add(t, row):
            pair = users_at[s * MAXT + t] * ITEM_TILES + items_at[s * MAXT + t]
            counts_out[s * PAIRS + pair] = counts_out[s * PAIRS + pair] + 1.0
            return row + jnp.where(lane == pair, 1.0, 0.0)

        row = lax.fori_loop(0, live[s], add, jnp.zeros((COUNT_ROWS, K), F32)).astype(BF16)
        if s == 0:
            first_out[USER_ROWS:PART] = row
        rows_out[s * COUNT_ROWS : (s + 1) * COUNT_ROWS] = row
    first_out[:USER_ROWS] = users[...].astype(BF16)
    first_out[PART:] = items[...].astype(BF16)


def opening(users_at, items_at, live, users, items):
    return kernel_call(
        opening_body,
        (
            shape(PART + ITEM_ROWS, BF16),
            shape(STEPS * COUNT_ROWS, BF16),
            jax.ShapeDtypeStruct((STEPS * PAIRS,), F32),
        ),
        [SMEM, SMEM, SMEM, VMEM, VMEM],
        (VMEM, VMEM, SMEM),
    )(users_at, items_at, live, users, items)


def joined_body(part, state, out):
    out[:PART] = part[...]
    out[PART:] = state[:ITEM_ROWS].astype(BF16)


def joined(part, state):
    return kernel_call(joined_body, shape(PART + ITEM_ROWS, BF16), [VMEM, VMEM])(part, state)


def packed_body(own, other, out):
    out[:ITEM_ROWS] = own[PART:]
    out[ITEM_ROWS : 2 * ITEM_ROWS] = other[PART:]
    out[2 * ITEM_ROWS : 2 * ITEM_ROWS + PART] = own[:PART]
    out[2 * ITEM_ROWS + PART :] = other[:PART]


def packed(own, other):
    return kernel_call(packed_body, shape(2 * (ITEM_ROWS + PART), BF16), [VMEM, VMEM])(own, other)


def dense_body(s, users_at, items_at, live, ratings, *rest):
    out_ref, total, tiles, sem = rest[-4:]
    fetch = pltpu.make_async_copy(ratings.at[0, 0, s], tiles, sem)
    fetch.start()
    total[...] = jnp.zeros_like(total)
    fetch.wait()

    def add(t, carry):
        slot = items_at[s * MAXT + t] * USER_TILES + users_at[s * MAXT + t]
        row = pl.multiple_of(slot * TILE, TILE)
        total[pl.ds(row, TILE), :] += tiles[t].astype(F32)
        return carry

    lax.fori_loop(0, live[s], add, 0)
    out_ref[...] = total[...].astype(BF16)


def dense_ratings(s, users_at, items_at, live, ratings, *later):
    rows = ITEM_TILES * USER_ROWS
    return kernel_call(
        functools.partial(dense_body, s),
        shape(rows, BF16),
        [SMEM, SMEM, SMEM, ANY] + [ANY] * len(later),
        scratch=[
            pltpu.VMEM((rows, TILE), F32),
            pltpu.VMEM((MAXT, TILE, TILE), BF16),
            pltpu.SemaphoreType.DMA,
        ],
        moved=10 << 20,
    )(users_at, items_at, live, ratings, *later)


def rating_part_body(me_ref, users_ref, dense_ref, out_ref):
    users = users_ref[:USER_ROWS]
    for k in range(ITEM_TILES):
        tile = owned_tile(me_ref[0], k // 2 % 2, k // 4, k % 2)
        row = pl.multiple_of(tile * USER_ROWS, USER_ROWS)
        part = lax.dot_general(
            dense_ref[pl.ds(row, USER_ROWS), :],
            users,
            (((0,), (0,)), ((), ())),
            preferred_element_type=F32,
        )
        out_ref[k * TILE : (k + 1) * TILE] = part.astype(BF16)


def rating_part(me, users, dense):
    return kernel_call(
        rating_part_body,
        shape(ITEM_TILES * TILE, BF16),
        [SMEM, VMEM, VMEM],
        flops=2 * ITEM_TILES * USER_ROWS * TILE * K,
        moved=3 << 20,
    )(me, users, dense)


def fetched(pieces, top, held, sems):
    rows = held.shape[1]
    copies = [
        pltpu.make_async_copy(piece.at[pl.ds(top, rows)], held.at[i], sems.at[i])
        for i, piece in enumerate(pieces)
    ]
    for copy in copies:
        copy.start()
    return copies


def fetch_scratch(rows):
    count = len(DISTANCES)
    return [pltpu.VMEM((count, rows, K), BF16), pltpu.SemaphoreType.DMA((count,))]


def user_body(s, states, me_ref, counts_ref, dense_ref, rows_ref, *rest):
    state_refs, pieces = rest[:states], rest[states : states + len(DISTANCES)]
    *outs, held, sems = rest[states + len(DISTANCES) :]
    outs = outs[-3:] if s + 1 == STEPS else outs[-2:]
    copies = fetched(pieces, 0, held, sems)
    fac, first, second = loaded(state_refs)
    users = fac.astype(BF16)
    total = jnp.zeros((USER_ROWS, K), F32)
    upper = lax.broadcasted_iota(jnp.int32, (USER_ROWS, TILE), 0) < TILE
    me = me_ref[0]
    for i, distance in enumerate(DISTANCES):
        copies[i].wait()
        place = (me % RING + distance + RING) % RING
        for swap in range(2):
            rows = held[i, swap * ITEM_ROWS : (swap + 1) * ITEM_ROWS]
            predicted = lax.dot_general(
                users, rows, (((1,), (1,)), ((), ())), preferred_element_type=F32
            )
            errors = []
            for h in range(2):
                tile = owned_tile(me, swap, place, h)
                row = pl.multiple_of(tile * USER_ROWS, USER_ROWS)
                at = s * PAIRS + tile
                many = jnp.where(upper, counts_ref[at], counts_ref[at + ITEM_TILES])
                ratings = dense_ref[pl.ds(row, USER_ROWS), :].astype(F32)
                errors.append(
                    (predicted[:, h * TILE : (h + 1) * TILE] * many - ratings).astype(BF16)
                )
            total += jnp.dot(
                jnp.concatenate(errors, axis=1), rows, preferred_element_type=F32
            )
    grad = GRAD_SCALE * total + DECAY_REG * fac
    fac, first, second = adam_update(fac, first, second, grad)
    if s + 1 < STEPS:
        part_out, *outs = outs
        part_out[:USER_ROWS] = fac.astype(BF16)
        part_out[USER_ROWS:] = rows_ref[(s + 1) * COUNT_ROWS : (s + 2) * COUNT_ROWS]
    stored(outs, (fac, first, second))


def user_step(s, me, counts, dense, rows, state, pieces, later):
    last = s + 1 == STEPS
    outs = [shape(USER_ROWS)] * 3 if last else [shape(PART, BF16), shape(3 * USER_ROWS)]
    return kernel_call(
        functools.partial(user_body, s, len(state)),
        outs,
        [SMEM, SMEM] + [VMEM] * (2 + len(state)) + [ANY] * (len(pieces) + len(later)),
        scratch=fetch_scratch(2 * ITEM_ROWS),
        flops=4 * ITEM_TILES * USER_ROWS * TILE * K,
        moved=5 << 20,
    )(me, counts, dense, rows, *state, *pieces, *later)


def item_body(s, states, me_ref, own_ref, other_ref, *rest):
    state_refs, pieces = rest[:states], rest[states : states + len(DISTANCES)]
    *outs, held, sems = rest[states + len(DISTANCES) :]
    copies = fetched(pieces, 2 * ITEM_ROWS, held, sems)
    lane = lax.broadcasted_iota(jnp.int32, (COUNT_ROWS, K), 1)
    weighted = [jnp.zeros((K, K), F32) for _ in range(2)]
    for i, copy in enumerate(copies):
        copy.wait()
        for swap in range(2):
            top = swap * PART
            counts = held[i, top + USER_ROWS : top + PART].astype(F32)
            for u in range(USER_TILES):
                users = held[i, top + u * TILE : top + (u + 1) * TILE]
                gram = lax.dot_general(
                    users, users, (((0,), (0,)), ((), ())), preferred_element_type=F32
                )
                for h in range(2):
                    at = u * ITEM_TILES + me_ref[0] * 2 + h
                    many = jnp.sum(jnp.where(lane == at, counts, 0.0), axis=1, keepdims=True)
                    weighted[h] = weighted[h] + many[0:1] * gram
    fac, first, second = loaded(state_refs)
    rows = fac.astype(BF16)
    parts = []
    for h in range(2):
        high = weighted[h].astype(BF16)
        low = (weighted[h] - high.astype(F32)).astype(BF16)
        mine = rows[h * TILE : (h + 1) * TILE]
        parts.append(
            jnp.dot(mine, high, preferred_element_type=F32)
            + jnp.dot(mine, low, preferred_element_type=F32)
        )
    total = jnp.concatenate(parts, axis=0) - (
        own_ref[:ITEM_ROWS].astype(F32) + other_ref[...].astype(F32)
    )
    grad = GRAD_SCALE * total + DECAY_REG * fac
    fac, first, second = adam_update(fac, first, second, grad)
    stored(outs, (fac, first, second))


def item_step(s, me, own, other, state, pieces):
    last = s + 1 == STEPS
    outs = [shape(ITEM_ROWS)] * 3 if last else [shape(3 * ITEM_ROWS)]
    return kernel_call(
        functools.partial(item_body, s, len(state)),
        outs,
        [SMEM] + [VMEM] * (2 + len(state)) + [ANY] * len(pieces),
        scratch=fetch_scratch(2 * PART),
        flops=2 * 32 * TILE * K * K,
        moved=4 << 20,
    )(me, own, other, *state, *pieces)


def after(value, *others):
    return lax.optimization_barrier((value, *others))[0]


def per_device(
    user_factors,
    user_m,
    user_v,
    item_factors,
    item_m,
    item_v,
    ratings,
    user_tiles,
    item_tiles,
    tile_counts,
):
    strata = lax.axis_size("blk")
    forward = [(z * RING + y, z * RING + (y + 1) % RING) for z in range(2) for y in range(RING)]
    backward = [(target, source) for source, target in forward]
    across = [(n, (n + RING) % (2 * RING)) for n in range(2 * RING)]
    rings = [[z * RING + y for y in range(RING)] for z in range(2)]

    earlier = [(b, (b - 1) % strata) for b in range(strata)]
    me = lax.axis_index("narrow").reshape(1).astype(jnp.int32)
    users_at, items_at = user_tiles.reshape(-1), item_tiles.reshape(-1)
    live = tile_counts.reshape(-1)
    first, rows, counts = opening(users_at, items_at, live, user_factors, item_factors)
    dense = dense_ratings(0, users_at, items_at, live, ratings, first)
    user_state = (user_factors, user_m, user_v)
    item_state = (item_factors, item_m, item_v)
    for s in range(STEPS):
        load = packed(first, lax.ppermute(first, "narrow", across))
        partial = lax.psum_scatter(
            rating_part(me, first, dense),
            "narrow",
            scatter_dimension=0,
            tiled=True,
            axis_index_groups=rings,
        )
        pieces = [load]
        up = down = load
        for step in range(3):
            up = lax.ppermute(up, "narrow", forward)
            down = lax.ppermute(down, "narrow", backward)
            pieces += [up, down]
            if step == 1 and s + 1 < STEPS:
                dense_next = dense_ratings(s + 1, users_at, items_at, live, ratings, pieces[1])
                up = after(up, dense_next)
            if step == (1 if s > 0 else 2):
                ready = after(partial[ITEM_ROWS:], up, down)
                other = lax.ppermute(ready, "narrow", across)
        pieces.append(lax.ppermute(after(up, other) if s > 0 else up, "narrow", forward))
        item_state = item_step(s, me, partial, other, item_state, pieces)
        if s + 1 < STEPS:
            moved = lax.ppermute(item_state[0], "blk", earlier)
            part, *user_state = user_step(
                s, me, counts, dense, rows, user_state, pieces, item_state
            )
            first = joined(part, moved)
            item_state = [moved]
            dense = dense_next
        else:
            user_state = user_step(s, me, counts, dense, rows, user_state, pieces, [])
    return (*user_state, *item_state)


def solution(mesh):
    return jax.shard_map(
        per_device,
        mesh=mesh,
        in_specs=(
            P(("blk", "narrow"), None),
            P(("blk", "narrow"), None),
            P(("blk", "narrow"), None),
            P(("blk", "narrow"), None),
            P(("blk", "narrow"), None),
            P(("blk", "narrow"), None),
            P("blk", "narrow", None, None, None, None),
            P("blk", "narrow", None, None),
            P("blk", "narrow", None, None),
            P("blk", "narrow", None),
        ),
        out_specs=(
            P(("blk", "narrow"), None),
            P(("blk", "narrow"), None),
            P(("blk", "narrow"), None),
            P(("blk", "narrow"), None),
            P(("blk", "narrow"), None),
            P(("blk", "narrow"), None),
        ),
        check_vma=False,
    )
```

time: 296 us -> 289 us (0.976)
  starting transfers between devices: 142 us -> 114 us
  waiting for transfers between devices: 63.9 us -> 78 us
  local copies, waits for them, and re-layouts: 34.7 us -> 42.5 us
  Pallas kernels: 27.7 us -> 35.1 us
  other arithmetic: 7.17 us -> 1.4 us
    ppermute x22 -> x11, starting transfers between devices: 80.6 us -> 52.3 us  [the longest x3 21.7 us: per_device(): load = packed(first, lax.ppermute(first, 'narrow', across))]
    unnamed x152 -> x118, local copies, waits for them, and re-layouts: 19.8 us -> 39.6 us
    ppermute x9, waiting for transfers between devices: 20.8 us -> 32.1 us  [per_device(): up = lax.ppermute(up, 'narrow', forward)]
    pallas_call x12 -> x18, Pallas kernels: 27.7 us -> 35.1 us  [the longest x3 14.9 us: user_step(): kernel_call(functools.partial(user_body, s, len(state)), outs, [SMEM, SME...]
    reduce_scatter x3, waiting for transfers between devices: 0.06 us -> 6.51 us  [per_device(): lax.psum_scatter(rating_part(me, first, dense), 'narrow', scatter_dimensi...]
    slice x10 -> x3, local copies, waits for them, and re-layouts: 7.89 us -> 2.73 us  [per_device(): ready = after(partial[ITEM_ROWS:], up, down)]
    squeeze x3 -> x0, local copies, waits for them, and re-layouts: 4.59 us -> none  [the longest x2 4.01 us: per_device(): dense = dense_ratings(slots[s], live[s].reshape(1), ratings[0, 0, s])]
    ppermute x22 -> x11, waiting for transfers between devices: 35.7 us -> 32.6 us  [the longest x3 16.6 us: per_device(): load = packed(first, lax.ppermute(first, 'narrow', across))]
  transfers between devices with their start and end apart: 43 -> 32, of which waited for: 15 -> 19; matrix products, arithmetic and copies ran while one was open for 7% -> 1% of each run, Pallas kernels for 9% -> 4%
where the time goes in v3:
time: 289 us; the launch traced here: 286 us
  starting transfers between devices  114 us (39%)
  waiting for transfers between devices  78 us (27%)
  local copies, waits for them, and re-layouts  42.5 us (15%)
  Pallas kernels  35.1 us (12%)
  between operations  14.5 us (5%)
    ppermute x9, starting transfers between devices, per_device(): down = lax.ppermute(down, 'narrow', backward)  41 us
    unnamed x118, local copies, waits for them, and re-layouts  39.6 us
    ppermute x9, waiting for transfers between devices, per_device(): up = lax.ppermute(up, 'narrow', forward)  32.1 us
    ppermute x3, starting transfers between devices, per_device(): load = packed(first, lax.ppermute(first, 'narrow', across))  21.7 us
    ppermute x9, starting transfers between devices, per_device(): up = lax.ppermute(up, 'narrow', forward)  20.7 us
    ppermute x3, starting transfers between devices, per_device(): other = lax.ppermute(ready, 'narrow', across)  20.1 us
    ppermute x3, waiting for transfers between devices, per_device(): load = packed(first, lax.ppermute(first, 'narrow', across))  16.6 us
    pallas_call x3, Pallas kernels, user_step(): kernel_call(functools.partial(user_body, s, len(state)), outs, [SMEM, SME...  14.9 us
  transfers between devices with their start and end apart: 32, of which 19 were waited for; matrix products, arithmetic and copies ran while one was open for 1% of the time, Pallas kernels for 4%

profile of v3, /device:TPU:6, one launch (start us, length us, event | category | flops | bytes accessed | tf_op | source)
XLA Modules:
  0.0 285.6 jit_solution(10343540371503633031)
XLA Ops:
  11.3 2.9 %shard_map.145 = (bf16[528,128]{1,0:T(8,128)(2,1)S(1)}, bf16[48,128]{1,0:T(8,128)(2,1)S(1)}, f32[192]{0:T(256)S(1)}) custom-call(s32[108]{0:T(128)S(1)} %reshape.25.users_at, s32[108]{0:T(128)S(1)} %reshape.26.items_at, s32[3]{0:T(128)S(1)} %bitcast.2, f32[256,128]{1,0:T(8,128)S(1)} %copy-done.35, f32[256,128]{1,0:T(8,128)S(1)} %copy-done.37), custom_call_target="tpu_custom_call" | custom-call | bytes 1048576 | tf_op jit(solution)/shard_map/pallas_call | solution.py:106
  14.7 2.0 copy-done
  16.8 1.4 shard_map.146.dense_ref
  19.0 1.3 copy-done.7
  21.4 11.1 %collective-permute-start = (bf16[528,128]{1,0:T(8,128)(2,1)}, bf16[528,128]{1,0:T(8,128)(2,1)S(1)}, u32[]{:S(2)}, u32[]{:S(2)}) collective-permute-start(bf16[528,128]{1,0:T(8,128)(2,1)} %copy-done.27), channel_id=1, source_target_pairs={{0,8},{1,9},{2,10},{3,11},{4,12},{5,13},{6,14},{7,15},{8,0},{9,1},... | collective-permute-start | bytes 405512 | tf_op jit(solution)/shard_map/ppermute | solution.py:346
  32.5 3.9 %collective-permute-done.other = bf16[528,128]{1,0:T(8,128)(2,1)S(1)} collective-permute-done((bf16[528,128]{1,0:T(8,128)(2,1)}, bf16[528,128]{1,0:T(8,128)(2,1)S(1)}, u32[]{:S(2)}, u32[]{:S(2)}) %collective-permute-start) | collective-permute-done | bytes 135200 | tf_op jit(solution)/shard_map/ppermute | solution.py:346
  37.4 3.7 %collective-permute-start.1 = (bf16[1056,128]{1,0:T(8,128)(2,1)S(1)}, bf16[1056,128]{1,0:T(8,128)(2,1)S(1)}, u32[]{:S(2)}, u32[]{:S(2)}) collective-permute-start(bf16[1056,128]{1,0:T(8,128)(2,1)S(1)} %shard_map.147.rest_3_), channel_id=1, source_target_pairs={{0,1},{1,2},{2,3},{3,4},{4,5},{5,6},{6,7},{7,0},{8,9},{9,10},{10,1... | collective-permute-start | bytes 811016 | tf_op jit(solution)/shard_map/ppermute | solution.py:357
  41.1 3.4 %collective-permute-start.2 = (bf16[1056,128]{1,0:T(8,128)(2,1)S(1)}, bf16[1056,128]{1,0:T(8,128)(2,1)S(1)}, u32[]{:S(2)}, u32[]{:S(2)}) collective-permute-start(bf16[1056,128]{1,0:T(8,128)(2,1)S(1)} %shard_map.147.rest_3_), channel_id=1, source_target_pairs={{1,0},{2,1},{3,2},{4,3},{5,4},{6,5},{7,6},{0,7},{9,8},{10,9},{11,1... | collective-permute-start | bytes 811016 | tf_op jit(solution)/shard_map/ppermute | solution.py:358
  45.2 7.2 %collective-permute-done.1.rest_0_.rest_4_ = bf16[1056,128]{1,0:T(8,128)(2,1)S(1)} collective-permute-done((bf16[1056,128]{1,0:T(8,128)(2,1)S(1)}, bf16[1056,128]{1,0:T(8,128)(2,1)S(1)}, u32[]{:S(2)}, u32[]{:S(2)}) %collective-permute-start.1) | collective-permute-done | bytes 270368 | tf_op jit(solution)/shard_map/ppermute | solution.py:357
  52.4 1.9 collective-permute-start.3
  54.3 5.1 %collective-permute-start.4 = (bf16[1056,128]{1,0:T(8,128)(2,1)S(1)}, bf16[1056,128]{1,0:T(8,128)(2,1)}, u32[]{:S(2)}, u32[]{:S(2)}) collective-permute-start(bf16[1056,128]{1,0:T(8,128)(2,1)S(1)} %collective-permute-done.2.rest_5_), channel_id=1, source_target_pairs={{1,0},{2,1},{3,2},{4,3},{5,4},{6,5},{7,6},{0,7},{9,8},{10,9},{11,1... | collective-permute-start | bytes 811016 | tf_op jit(solution)/shard_map/ppermute | solution.py:358
  60.8 1.4 shard_map.148.dense_ref
  62.2 1.3 copy-done.4
  63.5 2.9 %collective-permute-done.3.rest_6_ = bf16[1056,128]{1,0:T(8,128)(2,1)S(1)} collective-permute-done((bf16[1056,128]{1,0:T(8,128)(2,1)S(1)}, bf16[1056,128]{1,0:T(8,128)(2,1)S(1)}, u32[]{:S(2)}, u32[]{:S(2)}) %collective-permute-start.3) | collective-permute-done | bytes 270368 | tf_op jit(solution)/shard_map/ppermute | solution.py:357
  66.4 1.9 collective-permute-start.5
  69.1 5.1 %collective-permute-start.6 = (bf16[1056,128]{1,0:T(8,128)(2,1)}, bf16[1056,128]{1,0:T(8,128)(2,1)}, u32[]{:S(2)}, u32[]{:S(2)}) collective-permute-start(bf16[1056,128]{1,0:T(8,128)(2,1)} %collective-permute-done.4.rest_7_), channel_id=1, source_target_pairs={{1,0},{2,1},{3,2},{4,3},{5,4},{6,5},{7,6},{0,7},{9,8},{10,9},{11,1... | collective-permute-start | bytes 811016 | tf_op jit(solution)/shard_map/ppermute | solution.py:358
  74.2 2.3 collective-permute-done.5.rest_8_
  76.5 1.9 collective-permute-start.7
  79.5 4.2 %collective-permute-start.8 = (bf16[256,128]{1,0:T(8,128)(2,1)S(1)}, bf16[256,128]{1,0:T(8,128)(2,1)S(1)}, u32[]{:S(2)}, u32[]{:S(2)}) collective-permute-start(bf16[256,128]{1,0:T(8,128)(2,1)S(1)} %slice.12), channel_id=1, source_target_pairs={{0,8},{1,9},{2,10},{3,11},{4,12},{5,13},{6,14},{7,15},{8,0},{9,1},... | collective-permute-start | bytes 196616 | tf_op jit(solution)/shard_map/ppermute | solution.py:365
  83.7 2.7 collective-permute-done.7.rest_10_
  86.4 3.1 %collective-permute-done.8.other_ref = bf16[256,128]{1,0:T(8,128)(2,1)S(1)} collective-permute-done((bf16[256,128]{1,0:T(8,128)(2,1)S(1)}, bf16[256,128]{1,0:T(8,128)(2,1)S(1)}, u32[]{:S(2)}, u32[]{:S(2)}) %collective-permute-start.8) | collective-permute-done | bytes 65568 | tf_op jit(solution)/shard_map/ppermute | solution.py:365
  97.0 2.9 shard_map.150.rest_11_
  99.9 2.5 collective-permute-start.9
  105.8 4.6 %shard_map.151 = (bf16[272,128]{1,0:T(8,128)(2,1)S(1)}, f32[768,128]{1,0:T(8,128)S(1)}) custom-call(s32[1]{0:T(128)} %bitcast.me_ref, f32[192]{0:T(256)S(1)} %copy-done.54, bf16[8192,128]{1,0:T(8,128)(2,1)S(1)} %copy-done.8, bf16[48,128]{1,0:T(8,128)(2,1)S(1)} %get-tuple-element.28.rows_ref, f32[256,128]{1,0:T(8,128)S(1)} %copy-done.36, ...), custom_call_target="tpu_custom_call" | custom-call | flops 536870912 | bytes 5242880 | tf_op jit(solution)/shard_map/pallas_call | solution.py:253
  114.4 3.6 %collective-permute-start.10 = (bf16[528,128]{1,0:T(8,128)(2,1)}, bf16[528,128]{1,0:T(8,128)(2,1)S(1)}, u32[]{:S(2)}, u32[]{:S(2)}) collective-permute-start(bf16[528,128]{1,0:T(8,128)(2,1)} %copy-done.25), channel_id=1, source_target_pairs={{0,8},{1,9},{2,10},{3,11},{4,12},{5,13},{6,14},{7,15},{8,0},{9,1},... | collective-permute-start | bytes 405512 | tf_op jit(solution)/shard_map/ppermute | solution.py:346
  118.1 7.8 %collective-permute-done.10.other = bf16[528,128]{1,0:T(8,128)(2,1)S(1)} collective-permute-done((bf16[528,128]{1,0:T(8,128)(2,1)}, bf16[528,128]{1,0:T(8,128)(2,1)S(1)}, u32[]{:S(2)}, u32[]{:S(2)}) %collective-permute-start.10) | collective-permute-done | bytes 135200 | tf_op jit(solution)/shard_map/ppermute | solution.py:346
  126.8 2.1 collective-permute-start.11
  128.9 5.0 %collective-permute-start.12 = (bf16[1056,128]{1,0:T(8,128)(2,1)S(1)}, bf16[1056,128]{1,0:T(8,128)(2,1)}, u32[]{:S(2)}, u32[]{:S(2)}) collective-permute-start(bf16[1056,128]{1,0:T(8,128)(2,1)S(1)} %shard_map.153.rest_1_), channel_id=1, source_target_pairs={{1,0},{2,1},{3,2},{4,3},{5,4},{6,5},{7,6},{0,7},{9,8},{10,9},{11,1... | collective-permute-start | bytes 811016 | tf_op jit(solution)/shard_map/ppermute | solution.py:358
  134.6 4.9 %collective-permute-done.11.rest_0_.rest_2_ = bf16[1056,128]{1,0:T(8,128)(2,1)S(1)} collective-permute-done((bf16[1056,128]{1,0:T(8,128)(2,1)S(1)}, bf16[1056,128]{1,0:T(8,128)(2,1)S(1)}, u32[]{:S(2)}, u32[]{:S(2)}) %collective-permute-start.11) | collective-permute-done | bytes 270368 | tf_op jit(solution)/shard_map/ppermute | solution.py:357
  139.5 2.4 collective-permute-start.13
  141.9 1.6 collective-permute-done.12.rest_3_
  143.5 3.4 %collective-permute-start.14 = (bf16[1056,128]{1,0:T(8,128)(2,1)}, bf16[1056,128]{1,0:T(8,128)(2,1)}, u32[]{:S(2)}, u32[]{:S(2)}) collective-permute-start(bf16[1056,128]{1,0:T(8,128)(2,1)} %collective-permute-done.12.rest_3_), channel_id=1, source_target_pairs={{1,0},{2,1},{3,2},{4,3},{5,4},{6,5},{7,6},{0,7},{9,8},{10,9},{11,1... | collective-permute-start | bytes 811016 | tf_op jit(solution)/shard_map/ppermute | solution.py:358
  148.3 1.7 shard_map.154.dense_ref
  150.0 1.3 copy-done.2
  151.4 2.4 collective-permute-done.13.rest_4_
  153.8 3.0 %collective-permute-start.15 = (bf16[1056,128]{1,0:T(8,128)(2,1)}, bf16[1056,128]{1,0:T(8,128)(2,1)S(1)}, u32[]{:S(2)}, u32[]{:S(2)}) collective-permute-start(bf16[1056,128]{1,0:T(8,128)(2,1)} %collective-permute-done.13.rest_4_), channel_id=1, source_target_pairs={{0,1},{1,2},{2,3},{3,4},{4,5},{5,6},{6,7},{7,0},{8,9},{9,10},{10,1... | collective-permute-start | bytes 811016 | tf_op jit(solution)/shard_map/ppermute | solution.py:357
  156.8 5.2 %reduce-scatter.6.cloned.1.call-done.own_ref = bf16[512,128]{1,0:T(8,128)(2,1)} async-done(((bf16[4096,128]{1,0:T(8,128)(2,1)}), bf16[512,128]{1,0:T(8,128)(2,1)}) %reduce-scatter.6.cloned.1.call-update) | async-done | bytes 131088 | tf_op jit(solution)/shard_map/reduce_scatter | solution.py:347
  162.9 7.7 %collective-permute-start.17 = (bf16[256,128]{1,0:T(8,128)(2,1)S(1)}, bf16[256,128]{1,0:T(8,128)(2,1)S(1)}, u32[]{:S(2)}, u32[]{:S(2)}) collective-permute-start(bf16[256,128]{1,0:T(8,128)(2,1)S(1)} %slice.13), channel_id=1, source_target_pairs={{0,8},{1,9},{2,10},{3,11},{4,12},{5,13},{6,14},{7,15},{8,0},{9,1},... | collective-permute-start | bytes 196616 | tf_op jit(solution)/shard_map/ppermute | solution.py:365
  170.6 3.7 %collective-permute-start.16 = (bf16[1056,128]{1,0:T(8,128)(2,1)}, bf16[1056,128]{1,0:T(8,128)(2,1)S(1)}, u32[]{:S(2)}, u32[]{:S(2)}) collective-permute-start(bf16[1056,128]{1,0:T(8,128)(2,1)} %collective-permute-done.14.rest_5_), channel_id=1, source_target_pairs={{1,0},{2,1},{3,2},{4,3},{5,4},{6,5},{7,6},{0,7},{9,8},{10,9},{11,1... | collective-permute-start | bytes 811016 | tf_op jit(solution)/shard_map/ppermute | solution.py:358
  174.3 2.1 collective-permute-start.18
  176.5 2.7 collective-permute-done.16.rest_7_
  179.1 4.8 %collective-permute-done.18.rest_8_ = bf16[1056,128]{1,0:T(8,128)(2,1)S(1)} collective-permute-done((bf16[1056,128]{1,0:T(8,128)(2,1)S(1)}, bf16[1056,128]{1,0:T(8,128)(2,1)S(1)}, u32[]{:S(2)}, u32[]{:S(2)}) %collective-permute-start.18) | collective-permute-done | bytes 270368 | tf_op jit(solution)/shard_map/ppermute | solution.py:366
  187.7 3.0 %shard_map.156.rest_9_ = f32[768,128]{1,0:T(8,128)S(1)} custom-call(s32[1]{0:T(128)} %bitcast.me_ref, bf16[512,128]{1,0:T(8,128)(2,1)S(1)} %copy-done.44, bf16[256,128]{1,0:T(8,128)(2,1)S(1)} %collective-permute-done.17.other_ref, f32[768,128]{1,0:T(8,128)S(1)} %copy-done.24, bf16[1056,128]{1,0:T(8,128)(2,1)S(1)} %copy-done.18, ...), custom_call_target="tpu_custom_call" | custom-call | flops 134217728 | bytes 4194304 | tf_op jit(solution)/shard_map/pallas_call | solution.py:305
  190.7 2.1 collective-permute-start.19
  192.8 1.6 copy-done.6
  196.4 4.8 %shard_map.157 = (bf16[272,128]{1,0:T(8,128)(2,1)S(1)}, f32[768,128]{1,0:T(8,128)S(1)}) custom-call(s32[1]{0:T(128)} %bitcast.me_ref, f32[192]{0:T(256)S(1)} %copy-done.55, bf16[8192,128]{1,0:T(8,128)(2,1)S(1)} %copy-done.6, bf16[48,128]{1,0:T(8,128)(2,1)S(1)} %get-tuple-element.28.rows_ref, f32[768,128]{1,0:T(8,128)S(1)} %copy-done.40, ...), custom_call_target="tpu_custom_call" | custom-call | flops 536870912 | bytes 5242880 | tf_op jit(solution)/shard_map/pallas_call | solution.py:253
  201.9 1.7 shard_map.160
  203.7 6.9 %collective-permute-start.20 = (bf16[528,128]{1,0:T(8,128)(2,1)S(1)}, bf16[528,128]{1,0:T(8,128)(2,1)S(1)}, u32[]{:S(2)}, u32[]{:S(2)}) collective-permute-start(bf16[528,128]{1,0:T(8,128)(2,1)S(1)} %shard_map.158.own.users_ref), channel_id=1, source_target_pairs={{0,8},{1,9},{2,10},{3,11},{4,12},{5,13},{6,14},{7,15},{8,0},{9,1},... | collective-permute-start | bytes 405512 | tf_op jit(solution)/shard_map/ppermute | solution.py:346
  210.6 4.9 %collective-permute-done.20.other = bf16[528,128]{1,0:T(8,128)(2,1)S(1)} collective-permute-done((bf16[528,128]{1,0:T(8,128)(2,1)S(1)}, bf16[528,128]{1,0:T(8,128)(2,1)S(1)}, u32[]{:S(2)}, u32[]{:S(2)}) %collective-permute-start.20) | collective-permute-done | bytes 135200 | tf_op jit(solution)/shard_map/ppermute | solution.py:346
  215.6 1.9 collective-permute-start.21
  217.5 5.1 %collective-permute-start.22 = (bf16[1056,128]{1,0:T(8,128)(2,1)S(1)}, bf16[1056,128]{1,0:T(8,128)(2,1)S(1)}, u32[]{:S(2)}, u32[]{:S(2)}) collective-permute-start(bf16[1056,128]{1,0:T(8,128)(2,1)S(1)} %shard_map.159.rest_1_), channel_id=1, source_target_pairs={{1,0},{2,1},{3,2},{4,3},{5,4},{6,5},{7,6},{0,7},{9,8},{10,9},{11,1... | collective-permute-start | bytes 811016 | tf_op jit(solution)/shard_map/ppermute | solution.py:358
  222.7 7.2 %collective-permute-done.21.rest_2_ = bf16[1056,128]{1,0:T(8,128)(2,1)S(1)} collective-permute-done((bf16[1056,128]{1,0:T(8,128)(2,1)S(1)}, bf16[1056,128]{1,0:T(8,128)(2,1)S(1)}, u32[]{:S(2)}, u32[]{:S(2)}) %collective-permute-start.21) | collective-permute-done | bytes 270368 | tf_op jit(solution)/shard_map/ppermute | solution.py:357
  229.9 1.9 collective-permute-start.23
  231.8 5.5 %collective-permute-start.24 = (bf16[1056,128]{1,0:T(8,128)(2,1)S(1)}, bf16[1056,128]{1,0:T(8,128)(2,1)}, u32[]{:S(2)}, u32[]{:S(2)}) collective-permute-start(bf16[1056,128]{1,0:T(8,128)(2,1)S(1)} %collective-permute-done.22.rest_3_), channel_id=1, source_target_pairs={{1,0},{2,1},{3,2},{4,3},{5,4},{6,5},{7,6},{0,7},{9,8},{10,9},{11,1... | collective-permute-start | bytes 811016 | tf_op jit(solution)/shard_map/ppermute | solution.py:358
  237.3 5.0 %collective-permute-done.23.rest_4_ = bf16[1056,128]{1,0:T(8,128)(2,1)} collective-permute-done((bf16[1056,128]{1,0:T(8,128)(2,1)S(1)}, bf16[1056,128]{1,0:T(8,128)(2,1)}, u32[]{:S(2)}, u32[]{:S(2)}) %collective-permute-start.23) | collective-permute-done | bytes 270368 | tf_op jit(solution)/shard_map/ppermute | solution.py:357
  242.3 1.9 collective-permute-start.25
  244.2 1.3 reduce-scatter.8.cloned.1.call-done.own_ref
  246.4 8.2 %collective-permute-start.27 = (bf16[256,128]{1,0:T(8,128)(2,1)S(1)}, bf16[256,128]{1,0:T(8,128)(2,1)S(1)}, u32[]{:S(2)}, u32[]{:S(2)}) collective-permute-start(bf16[256,128]{1,0:T(8,128)(2,1)S(1)} %slice.14), channel_id=1, source_target_pairs={{0,8},{1,9},{2,10},{3,11},{4,12},{5,13},{6,14},{7,15},{8,0},{9,1},... | collective-permute-start | bytes 196616 | tf_op jit(solution)/shard_map/ppermute | solution.py:365
  254.6 4.6 %collective-permute-start.26 = (bf16[1056,128]{1,0:T(8,128)(2,1)}, bf16[1056,128]{1,0:T(8,128)(2,1)S(1)}, u32[]{:S(2)}, u32[]{:S(2)}) collective-permute-start(bf16[1056,128]{1,0:T(8,128)(2,1)} %collective-permute-done.24.rest_5_), channel_id=1, source_target_pairs={{1,0},{2,1},{3,2},{4,3},{5,4},{6,5},{7,6},{0,7},{9,8},{10,9},{11,1... | collective-permute-start | bytes 811016 | tf_op jit(solution)/shard_map/ppermute | solution.py:358
  259.2 1.9 collective-permute-start.28
  261.1 2.5 collective-permute-done.26.rest_7_
  263.6 5.4 %collective-permute-done.28.rest_8_ = bf16[1056,128]{1,0:T(8,128)(2,1)S(1)} collective-permute-done((bf16[1056,128]{1,0:T(8,128)(2,1)}, bf16[1056,128]{1,0:T(8,128)(2,1)S(1)}, u32[]{:S(2)}, u32[]{:S(2)}) %collective-permute-start.28) | collective-permute-done | bytes 270368 | tf_op jit(solution)/shard_map/ppermute | solution.py:366
  269.9 3.7 %shard_map.162 = (f32[256,128]{1,0:T(8,128)}, f32[256,128]{1,0:T(8,128)}, f32[256,128]{1,0:T(8,128)}) custom-call(s32[1]{0:T(128)} %bitcast.me_ref, bf16[512,128]{1,0:T(8,128)(2,1)S(1)} %copy-done.43, bf16[256,128]{1,0:T(8,128)(2,1)S(1)} %collective-permute-done.27.other_ref, f32[768,128]{1,0:T(8,128)S(1)} %collective-permute-done.19.state.rest_0_, ...), custom_call_target="tpu_custom_call" | custom-call | flops 134217728 | bytes 4194304 | tf_op jit(solution)/shard_map/pallas_call | solution.py:305
  273.6 5.5 %shard_map.161 = (f32[256,128]{1,0:T(8,128)}, f32[256,128]{1,0:T(8,128)}, f32[256,128]{1,0:T(8,128)}) custom-call(s32[1]{0:T(128)} %bitcast.me_ref, f32[192]{0:T(256)S(1)} %copy-done.55, bf16[8192,128]{1,0:T(8,128)(2,1)S(1)} %copy-done.3, bf16[48,128]{1,0:T(8,128)(2,1)S(1)} %get-tuple-element.28.rows_ref, f32[768,128]{1,0:T(8,128)S(1)} %copy-done.42, ...), custom_call_target="tpu_custom_call" | custom-call | flops 536870912 | bytes 5242880 | tf_op jit(solution)/shard_map/pallas_call | solution.py:253
  (146 shorter events, 38.1 us)
Async XLA Ops:
  7.2 71.3 %reduce-scatter.4.cloned.1.call-start = ((), (), s32[]{:S(2)}) async-start(), calls=%async_computation.3 | async-start | bytes 1179648 | tf_op jit(solution)/shard_map/reduce_scatter | solution.py:347
  8.8 9.4 %copy-start.50 = (s32[108]{0:T(128)}, s32[108]{0:T(128)S(1)}, u32[]{:S(2)}) copy-start(s32[108]{0:T(128)S(1)} %reshape.26.items_at) | copy-start | bytes 1300
  14.7 3.5 %copy-start.27 = (bf16[528,128]{1,0:T(8,128)(2,1)}, bf16[528,128]{1,0:T(8,128)(2,1)S(1)}, u32[]{:S(2)}) copy-start(bf16[528,128]{1,0:T(8,128)(2,1)S(1)} %get-tuple-element.27.rest_0_.own.users_ref) | copy-start | bytes 405508
  14.7 2.1 copy-start
  18.2 41.3 %copy-start.1 = (bf16[1,1,3,36,128,128]{5,4,3,2,1,0:T(8,128)(2,1)S(1)}, bf16[1,1,3,36,128,128]{5,4,3,2,1,0:T(8,128)(2,1)}, u32[]{:S(2)}) copy-start(bf16[1,1,3,36,128,128]{5,4,3,2,1,0:T(8,128)(2,1)} %ratings.5) | copy-start | bytes 10616836
  19.0 1.4 copy-start.7
  20.3 1.0 copy-start.9
  21.4 140.7 %reduce-scatter.6.cloned.1.call-start = ((), (), s32[]{:S(2)}) async-start(), calls=%async_computation.4 | async-start | bytes 1179648 | tf_op jit(solution)/shard_map/reduce_scatter | solution.py:347
  21.4 15.0 %collective-permute-start = (bf16[528,128]{1,0:T(8,128)(2,1)}, bf16[528,128]{1,0:T(8,128)(2,1)S(1)}, u32[]{:S(2)}, u32[]{:S(2)}) collective-permute-start(bf16[528,128]{1,0:T(8,128)(2,1)} %copy-done.27), channel_id=1, source_target_pairs={{0,8},{1,9},{2,10},{3,11},{4,12},{5,13},{6,14},{7,15},{8,0},{9,1},... | collective-permute-start | bytes 405512 | tf_op jit(solution)/shard_map/ppermute | solution.py:346
  37.4 15.0 %collective-permute-start.1 = (bf16[1056,128]{1,0:T(8,128)(2,1)S(1)}, bf16[1056,128]{1,0:T(8,128)(2,1)S(1)}, u32[]{:S(2)}, u32[]{:S(2)}) collective-permute-start(bf16[1056,128]{1,0:T(8,128)(2,1)S(1)} %shard_map.147.rest_3_), channel_id=1, source_target_pairs={{0,1},{1,2},{2,3},{3,4},{4,5},{5,6},{6,7},{7,0},{8,9},{9,10},{10,1... | collective-permute-start | bytes 811016 | tf_op jit(solution)/shard_map/ppermute | solution.py:357
  41.1 13.2 %collective-permute-start.2 = (bf16[1056,128]{1,0:T(8,128)(2,1)S(1)}, bf16[1056,128]{1,0:T(8,128)(2,1)S(1)}, u32[]{:S(2)}, u32[]{:S(2)}) collective-permute-start(bf16[1056,128]{1,0:T(8,128)(2,1)S(1)} %shard_map.147.rest_3_), channel_id=1, source_target_pairs={{1,0},{2,1},{3,2},{4,3},{5,4},{6,5},{7,6},{0,7},{9,8},{10,9},{11,1... | collective-permute-start | bytes 811016 | tf_op jit(solution)/shard_map/ppermute | solution.py:358
  52.4 9.8 %copy-start.14 = (bf16[1056,128]{1,0:T(8,128)(2,1)}, bf16[1056,128]{1,0:T(8,128)(2,1)S(1)}, u32[]{:S(2)}) copy-start(bf16[1056,128]{1,0:T(8,128)(2,1)S(1)} %collective-permute-done.1.rest_0_.rest_4_) | copy-start | bytes 811012
  52.4 14.1 %collective-permute-start.3 = (bf16[1056,128]{1,0:T(8,128)(2,1)S(1)}, bf16[1056,128]{1,0:T(8,128)(2,1)S(1)}, u32[]{:S(2)}, u32[]{:S(2)}) collective-permute-start(bf16[1056,128]{1,0:T(8,128)(2,1)S(1)} %collective-permute-done.1.rest_0_.rest_4_), channel_id=1, source_target_pairs={{0,1},{1,2},{2,3},{3,4},{4,5},{5,6},{6,7},{7,0},{8,9},{9,10},{10,1... | collective-permute-start | bytes 811016 | tf_op jit(solution)/shard_map/ppermute | solution.py:357
  54.3 7.9 %copy-start.29 = (bf16[1056,128]{1,0:T(8,128)(2,1)}, bf16[1056,128]{1,0:T(8,128)(2,1)S(1)}, u32[]{:S(2)}) copy-start(bf16[1056,128]{1,0:T(8,128)(2,1)S(1)} %collective-permute-done.2.rest_5_) | copy-start | bytes 811012
  54.3 14.8 %collective-permute-start.4 = (bf16[1056,128]{1,0:T(8,128)(2,1)S(1)}, bf16[1056,128]{1,0:T(8,128)(2,1)}, u32[]{:S(2)}, u32[]{:S(2)}) collective-permute-start(bf16[1056,128]{1,0:T(8,128)(2,1)S(1)} %collective-permute-done.2.rest_5_), channel_id=1, source_target_pairs={{1,0},{2,1},{3,2},{4,3},{5,4},{6,5},{7,6},{0,7},{9,8},{10,9},{11,1... | collective-permute-start | bytes 811016 | tf_op jit(solution)/shard_map/ppermute | solution.py:358
  62.2 1.3 copy-start.4
  66.4 10.1 %collective-permute-start.5 = (bf16[1056,128]{1,0:T(8,128)(2,1)S(1)}, bf16[1056,128]{1,0:T(8,128)(2,1)}, u32[]{:S(2)}, u32[]{:S(2)}) collective-permute-start(bf16[1056,128]{1,0:T(8,128)(2,1)S(1)} %collective-permute-done.3.rest_6_), channel_id=1, source_target_pairs={{0,1},{1,2},{2,3},{3,4},{4,5},{5,6},{6,7},{7,0},{8,9},{9,10},{10,1... | collective-permute-start | bytes 811016 | tf_op jit(solution)/shard_map/ppermute | solution.py:357
  69.1 10.4 %collective-permute-start.6 = (bf16[1056,128]{1,0:T(8,128)(2,1)}, bf16[1056,128]{1,0:T(8,128)(2,1)}, u32[]{:S(2)}, u32[]{:S(2)}) collective-permute-start(bf16[1056,128]{1,0:T(8,128)(2,1)} %collective-permute-done.4.rest_7_), channel_id=1, source_target_pairs={{1,0},{2,1},{3,2},{4,3},{5,4},{6,5},{7,6},{0,7},{9,8},{10,9},{11,1... | collective-permute-start | bytes 811016 | tf_op jit(solution)/shard_map/ppermute | solution.py:358
  76.5 9.9 %collective-permute-start.7 = (bf16[1056,128]{1,0:T(8,128)(2,1)}, bf16[1056,128]{1,0:T(8,128)(2,1)}, u32[]{:S(2)}, u32[]{:S(2)}) collective-permute-start(bf16[1056,128]{1,0:T(8,128)(2,1)} %collective-permute-done.5.rest_8_), channel_id=1, source_target_pairs={{0,1},{1,2},{2,3},{3,4},{4,5},{5,6},{6,7},{7,0},{8,9},{9,10},{10,1... | collective-permute-start | bytes 811016 | tf_op jit(solution)/shard_map/ppermute | solution.py:366
  78.5 23.9 %copy-start.8 = (bf16[8192,128]{1,0:T(8,128)(2,1)S(1)}, bf16[8192,128]{1,0:T(8,128)(2,1)}, u32[]{:S(2)}) copy-start(bf16[8192,128]{1,0:T(8,128)(2,1)} %copy-done.7) | copy-start | bytes 6291460
  79.5 10.1 %collective-permute-start.8 = (bf16[256,128]{1,0:T(8,128)(2,1)S(1)}, bf16[256,128]{1,0:T(8,128)(2,1)S(1)}, u32[]{:S(2)}, u32[]{:S(2)}) collective-permute-start(bf16[256,128]{1,0:T(8,128)(2,1)S(1)} %slice.12), channel_id=1, source_target_pairs={{0,8},{1,9},{2,10},{3,11},{4,12},{5,13},{6,14},{7,15},{8,0},{9,1},... | collective-permute-start | bytes 196616 | tf_op jit(solution)/shard_map/ppermute | solution.py:365
  89.6 1.0 copy-start.15
  90.5 1.0 copy-start.21
  91.5 1.0 copy-start.30
  92.4 1.0 copy-start.33
  97.0 5.4 %copy-start.16 = (bf16[1056,128]{1,0:T(8,128)(2,1)S(1)}, bf16[1056,128]{1,0:T(8,128)(2,1)}, u32[]{:S(2)}) copy-start(bf16[1056,128]{1,0:T(8,128)(2,1)} %copy-done.14) | copy-start | bytes 811012
  97.0 5.4 %copy-start.22 = (bf16[1056,128]{1,0:T(8,128)(2,1)S(1)}, bf16[1056,128]{1,0:T(8,128)(2,1)}, u32[]{:S(2)}) copy-start(bf16[1056,128]{1,0:T(8,128)(2,1)} %copy-done.20) | copy-start | bytes 811012
  97.0 5.4 %copy-start.31 = (bf16[1056,128]{1,0:T(8,128)(2,1)S(1)}, bf16[1056,128]{1,0:T(8,128)(2,1)}, u32[]{:S(2)}) copy-start(bf16[1056,128]{1,0:T(8,128)(2,1)} %copy-done.29) | copy-start | bytes 811012
  97.0 5.4 %copy-start.34 = (bf16[1056,128]{1,0:T(8,128)(2,1)S(1)}, bf16[1056,128]{1,0:T(8,128)(2,1)}, u32[]{:S(2)}) copy-start(bf16[1056,128]{1,0:T(8,128)(2,1)} %copy-done.32) | copy-start | bytes 811012
  99.9 10.6 %collective-permute-start.9 = (f32[768,128]{1,0:T(8,128)S(1)}, f32[768,128]{1,0:T(8,128)S(1)}, u32[]{:S(2)}, u32[]{:S(2)}) collective-permute-start(f32[768,128]{1,0:T(8,128)S(1)} %shard_map.150.rest_11_), channel_id=1, source_target_pairs={{0,496},{16,0},{32,16},{48,32},{64,48},{80,64},{96,80},{112,96},{1... | collective-permute-start | bytes 1179656 | tf_op jit(solution)/shard_map/ppermute | solution.py:369
  105.8 6.1 %copy-start.5 = (bf16[8192,128]{1,0:T(8,128)(2,1)S(1)}, bf16[8192,128]{1,0:T(8,128)(2,1)}, u32[]{:S(2)}) copy-start(bf16[8192,128]{1,0:T(8,128)(2,1)} %copy-done.4) | copy-start | bytes 6291460
  112.7 1.0 copy-start.10
  114.4 131.1 %reduce-scatter.8.cloned.1.call-start = ((), (), s32[]{:S(2)}) async-start(), calls=%async_computation.5 | async-start | bytes 1179648 | tf_op jit(solution)/shard_map/reduce_scatter | solution.py:347
  114.4 11.4 %collective-permute-start.10 = (bf16[528,128]{1,0:T(8,128)(2,1)}, bf16[528,128]{1,0:T(8,128)(2,1)S(1)}, u32[]{:S(2)}, u32[]{:S(2)}) collective-permute-start(bf16[528,128]{1,0:T(8,128)(2,1)} %copy-done.25), channel_id=1, source_target_pairs={{0,8},{1,9},{2,10},{3,11},{4,12},{5,13},{6,14},{7,15},{8,0},{9,1},... | collective-permute-start | bytes 405512 | tf_op jit(solution)/shard_map/ppermute | solution.py:346
  126.8 12.8 %collective-permute-start.11 = (bf16[1056,128]{1,0:T(8,128)(2,1)S(1)}, bf16[1056,128]{1,0:T(8,128)(2,1)S(1)}, u32[]{:S(2)}, u32[]{:S(2)}) collective-permute-start(bf16[1056,128]{1,0:T(8,128)(2,1)S(1)} %shard_map.153.rest_1_), channel_id=1, source_target_pairs={{0,1},{1,2},{2,3},{3,4},{4,5},{5,6},{6,7},{7,0},{8,9},{9,10},{10,1... | collective-permute-start | bytes 811016 | tf_op jit(solution)/shard_map/ppermute | solution.py:357
  128.9 14.7 %collective-permute-start.12 = (bf16[1056,128]{1,0:T(8,128)(2,1)S(1)}, bf16[1056,128]{1,0:T(8,128)(2,1)}, u32[]{:S(2)}, u32[]{:S(2)}) collective-permute-start(bf16[1056,128]{1,0:T(8,128)(2,1)S(1)} %shard_map.153.rest_1_), channel_id=1, source_target_pairs={{1,0},{2,1},{3,2},{4,3},{5,4},{6,5},{7,6},{0,7},{9,8},{10,9},{11,1... | collective-permute-start | bytes 811016 | tf_op jit(solution)/shard_map/ppermute | solution.py:358
  139.5 10.5 %copy-start.11 = (bf16[1056,128]{1,0:T(8,128)(2,1)}, bf16[1056,128]{1,0:T(8,128)(2,1)S(1)}, u32[]{:S(2)}) copy-start(bf16[1056,128]{1,0:T(8,128)(2,1)S(1)} %collective-permute-done.11.rest_0_.rest_2_) | copy-start | bytes 811012
  139.5 14.3 %collective-permute-start.13 = (bf16[1056,128]{1,0:T(8,128)(2,1)S(1)}, bf16[1056,128]{1,0:T(8,128)(2,1)}, u32[]{:S(2)}, u32[]{:S(2)}) collective-permute-start(bf16[1056,128]{1,0:T(8,128)(2,1)S(1)} %collective-permute-done.11.rest_0_.rest_2_), channel_id=1, source_target_pairs={{0,1},{1,2},{2,3},{3,4},{4,5},{5,6},{6,7},{7,0},{8,9},{9,10},{10,1... | collective-permute-start | bytes 811016 | tf_op jit(solution)/shard_map/ppermute | solution.py:357
  143.5 19.4 %collective-permute-start.14 = (bf16[1056,128]{1,0:T(8,128)(2,1)}, bf16[1056,128]{1,0:T(8,128)(2,1)}, u32[]{:S(2)}, u32[]{:S(2)}) collective-permute-start(bf16[1056,128]{1,0:T(8,128)(2,1)} %collective-permute-done.12.rest_3_), channel_id=1, source_target_pairs={{1,0},{2,1},{3,2},{4,3},{5,4},{6,5},{7,6},{0,7},{9,8},{10,9},{11,1... | collective-permute-start | bytes 811016 | tf_op jit(solution)/shard_map/ppermute | solution.py:358
  150.0 1.4 copy-start.2
  151.4 41.4 %copy-start.55 = (f32[192]{0:T(256)S(1)}, f32[192]{0:T(256)}, u32[]{:S(2)}) copy-start(f32[192]{0:T(256)} %copy-done.53) | copy-start | bytes 2308
  153.8 20.5 %collective-permute-start.15 = (bf16[1056,128]{1,0:T(8,128)(2,1)}, bf16[1056,128]{1,0:T(8,128)(2,1)S(1)}, u32[]{:S(2)}, u32[]{:S(2)}) collective-permute-start(bf16[1056,128]{1,0:T(8,128)(2,1)} %collective-permute-done.13.rest_4_), channel_id=1, source_target_pairs={{0,1},{1,2},{2,3},{3,4},{4,5},{5,6},{6,7},{7,0},{8,9},{9,10},{10,1... | collective-permute-start | bytes 811016 | tf_op jit(solution)/shard_map/ppermute | solution.py:357
  162.9 11.5 %collective-permute-start.17 = (bf16[256,128]{1,0:T(8,128)(2,1)S(1)}, bf16[256,128]{1,0:T(8,128)(2,1)S(1)}, u32[]{:S(2)}, u32[]{:S(2)}) collective-permute-start(bf16[256,128]{1,0:T(8,128)(2,1)S(1)} %slice.13), channel_id=1, source_target_pairs={{0,8},{1,9},{2,10},{3,11},{4,12},{5,13},{6,14},{7,15},{8,0},{9,1},... | collective-permute-start | bytes 196616 | tf_op jit(solution)/shard_map/ppermute | solution.py:365
  170.6 8.6 %collective-permute-start.16 = (bf16[1056,128]{1,0:T(8,128)(2,1)}, bf16[1056,128]{1,0:T(8,128)(2,1)S(1)}, u32[]{:S(2)}, u32[]{:S(2)}) collective-permute-start(bf16[1056,128]{1,0:T(8,128)(2,1)} %collective-permute-done.14.rest_5_), channel_id=1, source_target_pairs={{1,0},{2,1},{3,2},{4,3},{5,4},{6,5},{7,6},{0,7},{9,8},{10,9},{11,1... | collective-permute-start | bytes 811016 | tf_op jit(solution)/shard_map/ppermute | solution.py:358
  174.3 9.6 %collective-permute-start.18 = (bf16[1056,128]{1,0:T(8,128)(2,1)S(1)}, bf16[1056,128]{1,0:T(8,128)(2,1)S(1)}, u32[]{:S(2)}, u32[]{:S(2)}) collective-permute-start(bf16[1056,128]{1,0:T(8,128)(2,1)S(1)} %collective-permute-done.15.rest_6_), channel_id=1, source_target_pairs={{0,1},{1,2},{2,3},{3,4},{4,5},{5,6},{6,7},{7,0},{8,9},{9,10},{10,1... | collective-permute-start | bytes 811016 | tf_op jit(solution)/shard_map/ppermute | solution.py:366
  183.9 1.0 copy-start.12
  184.9 1.0 copy-start.18
  185.8 1.0 copy-start.24
  187.7 5.1 %copy-start.13 = (bf16[1056,128]{1,0:T(8,128)(2,1)S(1)}, bf16[1056,128]{1,0:T(8,128)(2,1)}, u32[]{:S(2)}) copy-start(bf16[1056,128]{1,0:T(8,128)(2,1)} %copy-done.11) | copy-start | bytes 811012
  190.7 11.2 %collective-permute-start.19 = (f32[768,128]{1,0:T(8,128)S(1)}, f32[768,128]{1,0:T(8,128)S(1)}, u32[]{:S(2)}, u32[]{:S(2)}) collective-permute-start(f32[768,128]{1,0:T(8,128)S(1)} %shard_map.156.rest_9_), channel_id=1, source_target_pairs={{0,496},{16,0},{32,16},{48,32},{64,48},{80,64},{96,80},{112,96},{1... | collective-permute-start | bytes 1179656 | tf_op jit(solution)/shard_map/ppermute | solution.py:369
  192.8 1.6 copy-start.6
  194.4 1.0 copy-start.19
  195.4 1.0 copy-start.40
  196.4 5.5 %copy-start.3 = (bf16[8192,128]{1,0:T(8,128)(2,1)S(1)}, bf16[8192,128]{1,0:T(8,128)(2,1)}, u32[]{:S(2)}) copy-start(bf16[8192,128]{1,0:T(8,128)(2,1)} %copy-done.2) | copy-start | bytes 6291460
  203.7 11.9 %collective-permute-start.20 = (bf16[528,128]{1,0:T(8,128)(2,1)S(1)}, bf16[528,128]{1,0:T(8,128)(2,1)S(1)}, u32[]{:S(2)}, u32[]{:S(2)}) collective-permute-start(bf16[528,128]{1,0:T(8,128)(2,1)S(1)} %shard_map.158.own.users_ref), channel_id=1, source_target_pairs={{0,8},{1,9},{2,10},{3,11},{4,12},{5,13},{6,14},{7,15},{8,0},{9,1},... | collective-permute-start | bytes 405512 | tf_op jit(solution)/shard_map/ppermute | solution.py:346
  215.6 14.3 %collective-permute-start.21 = (bf16[1056,128]{1,0:T(8,128)(2,1)S(1)}, bf16[1056,128]{1,0:T(8,128)(2,1)S(1)}, u32[]{:S(2)}, u32[]{:S(2)}) collective-permute-start(bf16[1056,128]{1,0:T(8,128)(2,1)S(1)} %shard_map.159.rest_1_), channel_id=1, source_target_pairs={{0,1},{1,2},{2,3},{3,4},{4,5},{5,6},{6,7},{7,0},{8,9},{9,10},{10,1... | collective-permute-start | bytes 811016 | tf_op jit(solution)/shard_map/ppermute | solution.py:357
  217.5 14.3 %collective-permute-start.22 = (bf16[1056,128]{1,0:T(8,128)(2,1)S(1)}, bf16[1056,128]{1,0:T(8,128)(2,1)S(1)}, u32[]{:S(2)}, u32[]{:S(2)}) collective-permute-start(bf16[1056,128]{1,0:T(8,128)(2,1)S(1)} %shard_map.159.rest_1_), channel_id=1, source_target_pairs={{1,0},{2,1},{3,2},{4,3},{5,4},{6,5},{7,6},{0,7},{9,8},{10,9},{11,1... | collective-permute-start | bytes 811016 | tf_op jit(solution)/shard_map/ppermute | solution.py:358
  229.9 12.5 %collective-permute-start.23 = (bf16[1056,128]{1,0:T(8,128)(2,1)S(1)}, bf16[1056,128]{1,0:T(8,128)(2,1)}, u32[]{:S(2)}, u32[]{:S(2)}) collective-permute-start(bf16[1056,128]{1,0:T(8,128)(2,1)S(1)} %collective-permute-done.21.rest_2_), channel_id=1, source_target_pairs={{0,1},{1,2},{2,3},{3,4},{4,5},{5,6},{6,7},{7,0},{8,9},{9,10},{10,1... | collective-permute-start | bytes 811016 | tf_op jit(solution)/shard_map/ppermute | solution.py:357
  231.8 14.6 %collective-permute-start.24 = (bf16[1056,128]{1,0:T(8,128)(2,1)S(1)}, bf16[1056,128]{1,0:T(8,128)(2,1)}, u32[]{:S(2)}, u32[]{:S(2)}) collective-permute-start(bf16[1056,128]{1,0:T(8,128)(2,1)S(1)} %collective-permute-done.22.rest_3_), channel_id=1, source_target_pairs={{1,0},{2,1},{3,2},{4,3},{5,4},{6,5},{7,6},{0,7},{9,8},{10,9},{11,1... | collective-permute-start | bytes 811016 | tf_op jit(solution)/shard_map/ppermute | solution.py:358
  242.3 16.8 %collective-permute-start.25 = (bf16[1056,128]{1,0:T(8,128)(2,1)}, bf16[1056,128]{1,0:T(8,128)(2,1)}, u32[]{:S(2)}, u32[]{:S(2)}) collective-permute-start(bf16[1056,128]{1,0:T(8,128)(2,1)} %collective-permute-done.23.rest_4_), channel_id=1, source_target_pairs={{0,1},{1,2},{2,3},{3,4},{4,5},{5,6},{6,7},{7,0},{8,9},{9,10},{10,1... | collective-permute-start | bytes 811016 | tf_op jit(solution)/shard_map/ppermute | solution.py:357
  245.5 28.1 %copy-start.42 = (f32[768,128]{1,0:T(8,128)S(1)}, f32[768,128]{1,0:T(8,128)}, u32[]{:S(2)}) copy-start(f32[768,128]{1,0:T(8,128)} %copy-done.41) | copy-start | bytes 1179652
  246.4 12.8 %collective-permute-start.27 = (bf16[256,128]{1,0:T(8,128)(2,1)S(1)}, bf16[256,128]{1,0:T(8,128)(2,1)S(1)}, u32[]{:S(2)}, u32[]{:S(2)}) collective-permute-start(bf16[256,128]{1,0:T(8,128)(2,1)S(1)} %slice.14), channel_id=1, source_target_pairs={{0,8},{1,9},{2,10},{3,11},{4,12},{5,13},{6,14},{7,15},{8,0},{9,1},... | collective-permute-start | bytes 196616 | tf_op jit(solution)/shard_map/ppermute | solution.py:365
  254.6 9.0 %collective-permute-start.26 = (bf16[1056,128]{1,0:T(8,128)(2,1)}, bf16[1056,128]{1,0:T(8,128)(2,1)S(1)}, u32[]{:S(2)}, u32[]{:S(2)}) collective-permute-start(bf16[1056,128]{1,0:T(8,128)(2,1)} %collective-permute-done.24.rest_5_), channel_id=1, source_target_pairs={{1,0},{2,1},{3,2},{4,3},{5,4},{6,5},{7,6},{0,7},{9,8},{10,9},{11,1... | collective-permute-start | bytes 811016 | tf_op jit(solution)/shard_map/ppermute | solution.py:358
  259.2 9.8 %collective-permute-start.28 = (bf16[1056,128]{1,0:T(8,128)(2,1)}, bf16[1056,128]{1,0:T(8,128)(2,1)S(1)}, u32[]{:S(2)}, u32[]{:S(2)}) collective-permute-start(bf16[1056,128]{1,0:T(8,128)(2,1)} %collective-permute-done.25.rest_6_), channel_id=1, source_target_pairs={{0,1},{1,2},{2,3},{3,4},{4,5},{5,6},{6,7},{7,0},{8,9},{9,10},{10,1... | collective-permute-start | bytes 811016 | tf_op jit(solution)/shard_map/ppermute | solution.py:366
  (27 other events, 21.4 us)
Sparse Core Ops, SparseCore 0:
  21.5 48.7 reduce-scatter.3
  114.5 47.5 reduce-scatter.5
  203.8 41.6 reduce-scatter.7

commit v4 on v3

--- a/solution.py
+++ b/solution.py
@@ -54,7 +54,7 @@
         out_specs=out_specs or jax.tree.map(lambda _: VMEM, outs),
         scratch_shapes=list(scratch),
         cost_estimate=pl.CostEstimate(flops=flops, bytes_accessed=moved, transcendentals=0),
-        compiler_params=pltpu.CompilerParams(vmem_limit_bytes=40 << 20),
+        compiler_params=pltpu.CompilerParams(vmem_limit_bytes=60 << 20),
     )
 
 
@@ -90,11 +90,11 @@
     for s in range(STEPS):
 
         def add(t, row):
-            pair = users_at[s * MAXT + t] * ITEM_TILES + items_at[s * MAXT + t]
+            pair = users_at[0, 0, s, t] * ITEM_TILES + items_at[0, 0, s, t]
             counts_out[s * PAIRS + pair] = counts_out[s * PAIRS + pair] + 1.0
             return row + jnp.where(lane == pair, 1.0, 0.0)
 
-        row = lax.fori_loop(0, live[s], add, jnp.zeros((COUNT_ROWS, K), F32)).astype(BF16)
+        row = lax.fori_loop(0, live[0, 0, s], add, jnp.zeros((COUNT_ROWS, K), F32)).astype(BF16)
         if s == 0:
             first_out[USER_ROWS:PART] = row
         rows_out[s * COUNT_ROWS : (s + 1) * COUNT_ROWS] = row
@@ -143,12 +143,12 @@
     fetch.wait()
 
     def add(t, carry):
-        slot = items_at[s * MAXT + t] * USER_TILES + users_at[s * MAXT + t]
+        slot = items_at[0, 0, s, t] * USER_TILES + users_at[0, 0, s, t]
         row = pl.multiple_of(slot * TILE, TILE)
         total[pl.ds(row, TILE), :] += tiles[t].astype(F32)
         return carry
 
-    lax.fori_loop(0, live[s], add, 0)
+    lax.fori_loop(0, live[0, 0, s], add, 0)
     out_ref[...] = total[...].astype(BF16)
 
 
@@ -336,8 +336,7 @@
 
     earlier = [(b, (b - 1) % strata) for b in range(strata)]
     me = lax.axis_index("narrow").reshape(1).astype(jnp.int32)
-    users_at, items_at = user_tiles.reshape(-1), item_tiles.reshape(-1)
-    live = tile_counts.reshape(-1)
+    users_at, items_at, live = user_tiles, item_tiles, tile_counts
     first, rows, counts = opening(users_at, items_at, live, user_factors, item_factors)
     dense = dense_ratings(0, users_at, items_at, live, ratings, first)
     user_state = (user_factors, user_m, user_v)
@@ -360,10 +359,10 @@
             if step == 1 and s + 1 < STEPS:
                 dense_next = dense_ratings(s + 1, users_at, items_at, live, ratings, pieces[1])
                 up = after(up, dense_next)
-            if step == (1 if s > 0 else 2):
+            if step == 2:
                 ready = after(partial[ITEM_ROWS:], up, down)
                 other = lax.ppermute(ready, "narrow", across)
-        pieces.append(lax.ppermute(after(up, other) if s > 0 else up, "narrow", forward))
+        pieces.append(lax.ppermute(after(up, ready), "narrow", forward))
         item_state = item_step(s, me, partial, other, item_state, pieces)
         if s + 1 < STEPS:
             moved = lax.ppermute(item_state[0], "blk", earlier)

time: 289 us -> 300 us (1.038)
  Pallas kernels: 35.1 us -> 68.3 us
  local copies, waits for them, and re-layouts: 42.5 us -> 12.5 us
  starting transfers between devices: 114 us -> 123 us
    unnamed x118 -> x66, local copies, waits for them, and re-layouts: 39.6 us -> 9.94 us
    ppermute x9, waiting for transfers between devices: 6.79 us -> 26.1 us  [per_device(): down = lax.ppermute(down, 'narrow', backward)]
    ppermute x3, waiting for transfers between devices: 12.9 us -> 1.52 us  [per_device(): pieces.append(lax.ppermute(after(up, ready), 'narrow', forward))]
    pallas_call x3, Pallas kernels: 3.27 us -> 10.4 us  [rating_part(): kernel_call(rating_part_body, shape(ITEM_TILES * TILE, BF16), [SMEM, VMEM...]
    pallas_call x3, Pallas kernels: 4.46 us -> 11.4 us  [dense_ratings(): kernel_call(functools.partial(dense_body, s), shape(rows, BF16), [SMEM, S...]
    reduce_scatter x3, waiting for transfers between devices: 6.51 us -> 0.06 us  [per_device(): lax.psum_scatter(rating_part(me, first, dense), 'narrow', scatter_dimensi...]
    ppermute x3, waiting for transfers between devices: 16.6 us -> 10.9 us  [per_device(): load = packed(first, lax.ppermute(first, 'narrow', across))]
    pallas_call x3, Pallas kernels: 14.9 us -> 20 us  [user_step(): kernel_call(functools.partial(user_body, s, len(state)), outs, [SMEM, SME...]
  transfers between devices with their start and end apart: 32 -> 32, of which waited for: 19 -> 22; matrix products, arithmetic and copies ran while one was open for 1% -> 1% of each run, Pallas kernels for 4% -> 11%
where the time goes in v4:
time: 300 us; the launch traced here: 297 us
  starting transfers between devices  123 us (41%)
  waiting for transfers between devices  78.8 us (26%)
  Pallas kernels  68.3 us (23%)
  between operations  14.4 us (5%)
  local copies, waits for them, and re-layouts  12.5 us (4%)
    ppermute x9, starting transfers between devices, per_device(): down = lax.ppermute(down, 'narrow', backward)  44 us
    ppermute x9, waiting for transfers between devices, per_device(): up = lax.ppermute(up, 'narrow', forward)  34.9 us
    ppermute x9, waiting for transfers between devices, per_device(): down = lax.ppermute(down, 'narrow', backward)  26.1 us
    ppermute x3, starting transfers between devices, per_device(): load = packed(first, lax.ppermute(first, 'narrow', across))  25.3 us
    ppermute x9, starting transfers between devices, per_device(): up = lax.ppermute(up, 'narrow', forward)  22.1 us
    ppermute x3, starting transfers between devices, per_device(): other = lax.ppermute(ready, 'narrow', across)  21.9 us
    pallas_call x3, Pallas kernels, user_step(): kernel_call(functools.partial(user_body, s, len(state)), outs, [SMEM, SME...  20 us
    pallas_call x3, Pallas kernels, item_step(): kernel_call(functools.partial(item_body, s, len(state)), outs, [SMEM] + [...  14.5 us
  transfers between devices with their start and end apart: 32, of which 22 were waited for; matrix products, arithmetic and copies ran while one was open for 1% of the time, Pallas kernels for 11%

profile of v4, /device:TPU:6, one launch (start us, length us, event | category | flops | bytes accessed | tf_op | source)
XLA Modules:
  0.0 297.5 jit_solution(11176304438293741583)
XLA Ops:
  9.7 3.5 %shard_map.145 = (bf16[528,128]{1,0:T(8,128)(2,1)}, bf16[48,128]{1,0:T(8,128)(2,1)}, f32[192]{0:T(256)}) custom-call(s32[1,1,3,36]{3,2,1,0:T(4,128)} %copy.16.users_at, s32[1,1,3,36]{3,2,1,0:T(4,128)} %copy.17.items_at, s32[1,1,3]{2,1,0:T(1,128)} %live.7, f32[256,128]{1,0:T(8,128)} %rest_0_.3, f32[256,128]{1,0:T(8,128)} %rest_0_.2), custom_call_target="tpu_custom_call" | custom-call | bytes 1048576 | tf_op jit(solution)/shard_map/pallas_call | solution.py:106
  13.2 3.8 %shard_map.146.dense_ref = bf16[8192,128]{1,0:T(8,128)(2,1)} custom-call(s32[1,1,3,36]{3,2,1,0:T(4,128)} %copy.16.users_at, s32[1,1,3,36]{3,2,1,0:T(4,128)} %copy.17.items_at, s32[1,1,3]{2,1,0:T(1,128)} %live.7, bf16[1,1,3,36,128,128]{5,4,3,2,1,0:T(8,128)(2,1)} %ratings.5, bf16[528,128]{1,0:T(8,128)(2,1)} %get-tuple-element.28.rest_0_.own.users_ref), custom_call_target="tpu_custom_call" | custom-call | bytes 10485760 | tf_op jit(solution)/shard_map/pallas_call | solution.py:157
  17.0 3.4 %shard_map.149 = bf16[4096,128]{1,0:T(8,128)(2,1)} custom-call(s32[1]{0:T(128)} %bitcast.me_ref, bf16[528,128]{1,0:T(8,128)(2,1)} %get-tuple-element.28.rest_0_.own.users_ref, bf16[8192,128]{1,0:T(8,128)(2,1)} %shard_map.146.dense_ref), custom_call_target="tpu_custom_call" | custom-call | flops 268435456 | bytes 3145728 | tf_op jit(solution)/shard_map/pallas_call | solution.py:185
  20.5 10.5 %collective-permute-start = (bf16[528,128]{1,0:T(8,128)(2,1)S(1)}, bf16[528,128]{1,0:T(8,128)(2,1)S(1)}, u32[]{:S(2)}, u32[]{:S(2)}) collective-permute-start(bf16[528,128]{1,0:T(8,128)(2,1)S(1)} %copy-done.4), channel_id=1, source_target_pairs={{0,8},{1,9},{2,10},{3,11},{4,12},{5,13},{6,14},{7,15},{8,0},{9,1},... | collective-permute-start | bytes 405512 | tf_op jit(solution)/shard_map/ppermute | solution.py:345
  31.0 4.0 %collective-permute-done.other = bf16[528,128]{1,0:T(8,128)(2,1)S(1)} collective-permute-done((bf16[528,128]{1,0:T(8,128)(2,1)S(1)}, bf16[528,128]{1,0:T(8,128)(2,1)S(1)}, u32[]{:S(2)}, u32[]{:S(2)}) %collective-permute-start) | collective-permute-done | bytes 135200 | tf_op jit(solution)/shard_map/ppermute | solution.py:345
  35.7 1.7 shard_map.147.rest_3_
  37.4 3.7 %collective-permute-start.1 = (bf16[1056,128]{1,0:T(8,128)(2,1)}, bf16[1056,128]{1,0:T(8,128)(2,1)S(1)}, u32[]{:S(2)}, u32[]{:S(2)}) collective-permute-start(bf16[1056,128]{1,0:T(8,128)(2,1)} %shard_map.147.rest_3_), channel_id=1, source_target_pairs={{0,1},{1,2},{2,3},{3,4},{4,5},{5,6},{6,7},{7,0},{8,9},{9,10},{10,1... | collective-permute-start | bytes 811016 | tf_op jit(solution)/shard_map/ppermute | solution.py:356
  41.1 5.7 %collective-permute-start.2 = (bf16[1056,128]{1,0:T(8,128)(2,1)}, bf16[1056,128]{1,0:T(8,128)(2,1)S(1)}, u32[]{:S(2)}, u32[]{:S(2)}) collective-permute-start(bf16[1056,128]{1,0:T(8,128)(2,1)} %shard_map.147.rest_3_), channel_id=1, source_target_pairs={{1,0},{2,1},{3,2},{4,3},{5,4},{6,5},{7,6},{0,7},{9,8},{10,9},{11,1... | collective-permute-start | bytes 811016 | tf_op jit(solution)/shard_map/ppermute | solution.py:357
  46.8 6.5 %collective-permute-done.1.rest_0_.rest_4_ = bf16[1056,128]{1,0:T(8,128)(2,1)S(1)} collective-permute-done((bf16[1056,128]{1,0:T(8,128)(2,1)}, bf16[1056,128]{1,0:T(8,128)(2,1)S(1)}, u32[]{:S(2)}, u32[]{:S(2)}) %collective-permute-start.1) | collective-permute-done | bytes 270368 | tf_op jit(solution)/shard_map/ppermute | solution.py:356
  53.3 1.9 collective-permute-start.3
  55.2 5.1 %collective-permute-start.4 = (bf16[1056,128]{1,0:T(8,128)(2,1)S(1)}, bf16[1056,128]{1,0:T(8,128)(2,1)S(1)}, u32[]{:S(2)}, u32[]{:S(2)}) collective-permute-start(bf16[1056,128]{1,0:T(8,128)(2,1)S(1)} %collective-permute-done.2.rest_5_), channel_id=1, source_target_pairs={{1,0},{2,1},{3,2},{4,3},{5,4},{6,5},{7,6},{0,7},{9,8},{10,9},{11,1... | collective-permute-start | bytes 811016 | tf_op jit(solution)/shard_map/ppermute | solution.py:357
  60.4 4.0 %shard_map.148.dense_ref = bf16[8192,128]{1,0:T(8,128)(2,1)} custom-call(s32[1,1,3,36]{3,2,1,0:T(4,128)} %copy.16.users_at, s32[1,1,3,36]{3,2,1,0:T(4,128)} %copy.17.items_at, s32[1,1,3]{2,1,0:T(1,128)} %live.7, bf16[1,1,3,36,128,128]{5,4,3,2,1,0:T(8,128)(2,1)} %ratings.5, bf16[1056,128]{1,0:T(8,128)(2,1)} %copy-done.1), custom_call_target="tpu_custom_call" | custom-call | bytes 10485760 | tf_op jit(solution)/shard_map/pallas_call | solution.py:157
  66.0 4.7 %collective-permute-start.6 = (bf16[1056,128]{1,0:T(8,128)(2,1)S(1)}, bf16[1056,128]{1,0:T(8,128)(2,1)S(1)}, u32[]{:S(2)}, u32[]{:S(2)}) collective-permute-start(bf16[1056,128]{1,0:T(8,128)(2,1)S(1)} %collective-permute-done.4.rest_7_), channel_id=1, source_target_pairs={{1,0},{2,1},{3,2},{4,3},{5,4},{6,5},{7,6},{0,7},{9,8},{10,9},{11,1... | collective-permute-start | bytes 811016 | tf_op jit(solution)/shard_map/ppermute | solution.py:357
  70.7 1.9 collective-permute-start.5
  73.5 2.2 collective-permute-done.6.rest_9_
  75.7 4.6 %collective-permute-done.5.rest_8_ = bf16[1056,128]{1,0:T(8,128)(2,1)S(1)} collective-permute-done((bf16[1056,128]{1,0:T(8,128)(2,1)S(1)}, bf16[1056,128]{1,0:T(8,128)(2,1)S(1)}, u32[]{:S(2)}, u32[]{:S(2)}) %collective-permute-start.5) | collective-permute-done | bytes 270368 | tf_op jit(solution)/shard_map/ppermute | solution.py:356
  80.3 1.9 collective-permute-start.7
  82.2 8.0 %collective-permute-start.8 = (bf16[256,128]{1,0:T(8,128)(2,1)S(1)}, bf16[256,128]{1,0:T(8,128)(2,1)S(1)}, u32[]{:S(2)}, u32[]{:S(2)}) collective-permute-start(bf16[256,128]{1,0:T(8,128)(2,1)S(1)} %slice.12), channel_id=1, source_target_pairs={{0,8},{1,9},{2,10},{3,11},{4,12},{5,13},{6,14},{7,15},{8,0},{9,1},... | collective-permute-start | bytes 196616 | tf_op jit(solution)/shard_map/ppermute | solution.py:364
  90.2 2.3 collective-permute-done.8.other_ref
  93.8 4.9 %shard_map.150.rest_11_ = f32[768,128]{1,0:T(8,128)} custom-call(s32[1]{0:T(128)} %bitcast.me_ref, bf16[512,128]{1,0:T(8,128)(2,1)} %reduce-scatter.4.cloned.1.call-done.own_ref, bf16[256,128]{1,0:T(8,128)(2,1)} %copy-done.31, f32[256,128]{1,0:T(8,128)} %rest_0_.2, f32[256,128]{1,0:T(8,128)} %rest_1_.2, f32[256,128]{1,0:T(8,128)} %rest_2_.2, ...), custom_call_target="tpu_custom_call" | custom-call | flops 134217728 | bytes 4194304 | tf_op jit(solution)/shard_map/pallas_call | solution.py:305
  98.7 2.3 collective-permute-start.9
  101.0 6.7 %shard_map.151 = (bf16[272,128]{1,0:T(8,128)(2,1)}, f32[768,128]{1,0:T(8,128)}) custom-call(s32[1]{0:T(128)} %bitcast.me_ref, f32[192]{0:T(256)} %get-tuple-element.27.counts_ref, bf16[8192,128]{1,0:T(8,128)(2,1)} %shard_map.146.dense_ref, bf16[48,128]{1,0:T(8,128)(2,1)} %get-tuple-element.29.rows_ref, f32[256,128]{1,0:T(8,128)} %rest_0_.3, ...), custom_call_target="tpu_custom_call" | custom-call | flops 536870912 | bytes 5242880 | tf_op jit(solution)/shard_map/pallas_call | solution.py:253
  108.5 1.7 shard_map.152.own.users_ref
  110.2 3.5 %shard_map.155 = bf16[4096,128]{1,0:T(8,128)(2,1)} custom-call(s32[1]{0:T(128)} %bitcast.me_ref, bf16[528,128]{1,0:T(8,128)(2,1)} %shard_map.152.own.users_ref, bf16[8192,128]{1,0:T(8,128)(2,1)} %shard_map.148.dense_ref), custom_call_target="tpu_custom_call" | custom-call | flops 268435456 | bytes 3145728 | tf_op jit(solution)/shard_map/pallas_call | solution.py:185
  113.8 7.8 %collective-permute-start.10 = (bf16[528,128]{1,0:T(8,128)(2,1)S(1)}, bf16[528,128]{1,0:T(8,128)(2,1)S(1)}, u32[]{:S(2)}, u32[]{:S(2)}) collective-permute-start(bf16[528,128]{1,0:T(8,128)(2,1)S(1)} %copy-done.5), channel_id=1, source_target_pairs={{0,8},{1,9},{2,10},{3,11},{4,12},{5,13},{6,14},{7,15},{8,0},{9,1},... | collective-permute-start | bytes 405512 | tf_op jit(solution)/shard_map/ppermute | solution.py:345
  121.6 3.0 %collective-permute-done.10.other = bf16[528,128]{1,0:T(8,128)(2,1)S(1)} collective-permute-done((bf16[528,128]{1,0:T(8,128)(2,1)S(1)}, bf16[528,128]{1,0:T(8,128)(2,1)S(1)}, u32[]{:S(2)}, u32[]{:S(2)}) %collective-permute-start.10) | collective-permute-done | bytes 135200 | tf_op jit(solution)/shard_map/ppermute | solution.py:345
  125.3 1.7 shard_map.153.rest_1_
  127.0 4.2 %collective-permute-start.11 = (bf16[1056,128]{1,0:T(8,128)(2,1)}, bf16[1056,128]{1,0:T(8,128)(2,1)S(1)}, u32[]{:S(2)}, u32[]{:S(2)}) collective-permute-start(bf16[1056,128]{1,0:T(8,128)(2,1)} %shard_map.153.rest_1_), channel_id=1, source_target_pairs={{0,1},{1,2},{2,3},{3,4},{4,5},{5,6},{6,7},{7,0},{8,9},{9,10},{10,1... | collective-permute-start | bytes 811016 | tf_op jit(solution)/shard_map/ppermute | solution.py:356
  131.2 2.8 collective-permute-start.12
  134.0 7.8 %collective-permute-done.11.rest_0_.rest_2_ = bf16[1056,128]{1,0:T(8,128)(2,1)S(1)} collective-permute-done((bf16[1056,128]{1,0:T(8,128)(2,1)}, bf16[1056,128]{1,0:T(8,128)(2,1)S(1)}, u32[]{:S(2)}, u32[]{:S(2)}) %collective-permute-start.11) | collective-permute-done | bytes 270368 | tf_op jit(solution)/shard_map/ppermute | solution.py:356
  141.8 2.7 collective-permute-start.13
  145.4 4.0 %collective-permute-start.14 = (bf16[1056,128]{1,0:T(8,128)(2,1)S(1)}, bf16[1056,128]{1,0:T(8,128)(2,1)S(1)}, u32[]{:S(2)}, u32[]{:S(2)}) collective-permute-start(bf16[1056,128]{1,0:T(8,128)(2,1)S(1)} %collective-permute-done.12.rest_3_), channel_id=1, source_target_pairs={{1,0},{2,1},{3,2},{4,3},{5,4},{6,5},{7,6},{0,7},{9,8},{10,9},{11,1... | collective-permute-start | bytes 811016 | tf_op jit(solution)/shard_map/ppermute | solution.py:357
  149.4 3.6 %shard_map.154.dense_ref = bf16[8192,128]{1,0:T(8,128)(2,1)} custom-call(s32[1,1,3,36]{3,2,1,0:T(4,128)} %copy.16.users_at, s32[1,1,3,36]{3,2,1,0:T(4,128)} %copy.17.items_at, s32[1,1,3]{2,1,0:T(1,128)} %live.7, bf16[1,1,3,36,128,128]{5,4,3,2,1,0:T(8,128)(2,1)} %ratings.5, bf16[1056,128]{1,0:T(8,128)(2,1)} %copy-done), custom_call_target="tpu_custom_call" | custom-call | bytes 10485760 | tf_op jit(solution)/shard_map/pallas_call | solution.py:157
  153.0 4.6 %collective-permute-done.13.rest_4_ = bf16[1056,128]{1,0:T(8,128)(2,1)S(1)} collective-permute-done((bf16[1056,128]{1,0:T(8,128)(2,1)S(1)}, bf16[1056,128]{1,0:T(8,128)(2,1)S(1)}, u32[]{:S(2)}, u32[]{:S(2)}) %collective-permute-start.13) | collective-permute-done | bytes 270368 | tf_op jit(solution)/shard_map/ppermute | solution.py:356
  158.5 5.5 %collective-permute-start.16 = (bf16[1056,128]{1,0:T(8,128)(2,1)S(1)}, bf16[1056,128]{1,0:T(8,128)(2,1)S(1)}, u32[]{:S(2)}, u32[]{:S(2)}) collective-permute-start(bf16[1056,128]{1,0:T(8,128)(2,1)S(1)} %collective-permute-done.14.rest_5_), channel_id=1, source_target_pairs={{1,0},{2,1},{3,2},{4,3},{5,4},{6,5},{7,6},{0,7},{9,8},{10,9},{11,1... | collective-permute-start | bytes 811016 | tf_op jit(solution)/shard_map/ppermute | solution.py:357
  164.0 1.9 collective-permute-start.15
  166.8 3.3 %collective-permute-done.16.rest_7_ = bf16[1056,128]{1,0:T(8,128)(2,1)S(1)} collective-permute-done((bf16[1056,128]{1,0:T(8,128)(2,1)S(1)}, bf16[1056,128]{1,0:T(8,128)(2,1)S(1)}, u32[]{:S(2)}, u32[]{:S(2)}) %collective-permute-start.16) | collective-permute-done | bytes 270368 | tf_op jit(solution)/shard_map/ppermute | solution.py:357
  170.1 5.3 %collective-permute-done.15.rest_6_ = bf16[1056,128]{1,0:T(8,128)(2,1)S(1)} collective-permute-done((bf16[1056,128]{1,0:T(8,128)(2,1)S(1)}, bf16[1056,128]{1,0:T(8,128)(2,1)S(1)}, u32[]{:S(2)}, u32[]{:S(2)}) %collective-permute-start.15) | collective-permute-done | bytes 270368 | tf_op jit(solution)/shard_map/ppermute | solution.py:356
  175.4 1.9 collective-permute-start.17
  177.3 7.1 %collective-permute-start.18 = (bf16[256,128]{1,0:T(8,128)(2,1)S(1)}, bf16[256,128]{1,0:T(8,128)(2,1)S(1)}, u32[]{:S(2)}, u32[]{:S(2)}) collective-permute-start(bf16[256,128]{1,0:T(8,128)(2,1)S(1)} %slice.13), channel_id=1, source_target_pairs={{0,8},{1,9},{2,10},{3,11},{4,12},{5,13},{6,14},{7,15},{8,0},{9,1},... | collective-permute-start | bytes 196616 | tf_op jit(solution)/shard_map/ppermute | solution.py:364
  184.4 3.0 %collective-permute-done.18.other_ref = bf16[256,128]{1,0:T(8,128)(2,1)S(1)} collective-permute-done((bf16[256,128]{1,0:T(8,128)(2,1)S(1)}, bf16[256,128]{1,0:T(8,128)(2,1)S(1)}, u32[]{:S(2)}, u32[]{:S(2)}) %collective-permute-start.18) | collective-permute-done | bytes 65568 | tf_op jit(solution)/shard_map/ppermute | solution.py:364
  188.7 4.8 %shard_map.156.rest_9_ = f32[768,128]{1,0:T(8,128)} custom-call(s32[1]{0:T(128)} %bitcast.me_ref, bf16[512,128]{1,0:T(8,128)(2,1)} %reduce-scatter.6.cloned.1.call-done.own_ref, bf16[256,128]{1,0:T(8,128)(2,1)} %copy-done.30, f32[768,128]{1,0:T(8,128)} %copy-done.3, bf16[1056,128]{1,0:T(8,128)(2,1)} %shard_map.153.rest_1_, bf16[1056,128]{1,0:T(8,128)(2,1)} %copy-done, ...), custom_call_target="tpu_custom_call" | custom-call | flops 134217728 | bytes 4194304 | tf_op jit(solution)/shard_map/pallas_call | solution.py:305
  193.6 2.1 collective-permute-start.19
  195.7 6.7 %shard_map.157 = (bf16[272,128]{1,0:T(8,128)(2,1)}, f32[768,128]{1,0:T(8,128)}) custom-call(s32[1]{0:T(128)} %bitcast.me_ref, f32[192]{0:T(256)} %get-tuple-element.27.counts_ref, bf16[8192,128]{1,0:T(8,128)(2,1)} %shard_map.148.dense_ref, bf16[48,128]{1,0:T(8,128)(2,1)} %get-tuple-element.29.rows_ref, f32[768,128]{1,0:T(8,128)} %get-tuple-element.34.rest_0_, ...), custom_call_target="tpu_custom_call" | custom-call | flops 536870912 | bytes 5242880 | tf_op jit(solution)/shard_map/pallas_call | solution.py:253
  203.1 1.7 shard_map.158.own.users_ref
  204.8 3.5 %shard_map.160 = bf16[4096,128]{1,0:T(8,128)(2,1)} custom-call(s32[1]{0:T(128)} %bitcast.me_ref, bf16[528,128]{1,0:T(8,128)(2,1)} %shard_map.158.own.users_ref, bf16[8192,128]{1,0:T(8,128)(2,1)} %shard_map.154.dense_ref), custom_call_target="tpu_custom_call" | custom-call | flops 268435456 | bytes 3145728 | tf_op jit(solution)/shard_map/pallas_call | solution.py:185
  208.3 7.1 %collective-permute-start.20 = (bf16[528,128]{1,0:T(8,128)(2,1)S(1)}, bf16[528,128]{1,0:T(8,128)(2,1)S(1)}, u32[]{:S(2)}, u32[]{:S(2)}) collective-permute-start(bf16[528,128]{1,0:T(8,128)(2,1)S(1)} %copy-done.6), channel_id=1, source_target_pairs={{0,8},{1,9},{2,10},{3,11},{4,12},{5,13},{6,14},{7,15},{8,0},{9,1},... | collective-permute-start | bytes 405512 | tf_op jit(solution)/shard_map/ppermute | solution.py:345
  215.4 3.8 %collective-permute-done.20.other = bf16[528,128]{1,0:T(8,128)(2,1)S(1)} collective-permute-done((bf16[528,128]{1,0:T(8,128)(2,1)S(1)}, bf16[528,128]{1,0:T(8,128)(2,1)S(1)}, u32[]{:S(2)}, u32[]{:S(2)}) %collective-permute-start.20) | collective-permute-done | bytes 135200 | tf_op jit(solution)/shard_map/ppermute | solution.py:345
  219.9 1.7 shard_map.159.rest_1_
  221.6 5.1 %collective-permute-start.22 = (bf16[1056,128]{1,0:T(8,128)(2,1)}, bf16[1056,128]{1,0:T(8,128)(2,1)S(1)}, u32[]{:S(2)}, u32[]{:S(2)}) collective-permute-start(bf16[1056,128]{1,0:T(8,128)(2,1)} %shard_map.159.rest_1_), channel_id=1, source_target_pairs={{1,0},{2,1},{3,2},{4,3},{5,4},{6,5},{7,6},{0,7},{9,8},{10,9},{11,1... | collective-permute-start | bytes 811016 | tf_op jit(solution)/shard_map/ppermute | solution.py:357
  226.7 1.9 collective-permute-start.21
  228.7 8.1 %collective-permute-done.22.rest_3_ = bf16[1056,128]{1,0:T(8,128)(2,1)S(1)} collective-permute-done((bf16[1056,128]{1,0:T(8,128)(2,1)}, bf16[1056,128]{1,0:T(8,128)(2,1)S(1)}, u32[]{:S(2)}, u32[]{:S(2)}) %collective-permute-start.22) | collective-permute-done | bytes 270368 | tf_op jit(solution)/shard_map/ppermute | solution.py:357
  236.8 5.5 %collective-permute-start.24 = (bf16[1056,128]{1,0:T(8,128)(2,1)S(1)}, bf16[1056,128]{1,0:T(8,128)(2,1)S(1)}, u32[]{:S(2)}, u32[]{:S(2)}) collective-permute-start(bf16[1056,128]{1,0:T(8,128)(2,1)S(1)} %collective-permute-done.22.rest_3_), channel_id=1, source_target_pairs={{1,0},{2,1},{3,2},{4,3},{5,4},{6,5},{7,6},{0,7},{9,8},{10,9},{11,1... | collective-permute-start | bytes 811016 | tf_op jit(solution)/shard_map/ppermute | solution.py:357
  242.4 1.9 collective-permute-start.23
  244.3 6.7 %collective-permute-done.24.rest_5_ = bf16[1056,128]{1,0:T(8,128)(2,1)S(1)} collective-permute-done((bf16[1056,128]{1,0:T(8,128)(2,1)S(1)}, bf16[1056,128]{1,0:T(8,128)(2,1)S(1)}, u32[]{:S(2)}, u32[]{:S(2)}) %collective-permute-start.24) | collective-permute-done | bytes 270368 | tf_op jit(solution)/shard_map/ppermute | solution.py:357
  251.1 5.6 %collective-permute-start.26 = (bf16[1056,128]{1,0:T(8,128)(2,1)S(1)}, bf16[1056,128]{1,0:T(8,128)(2,1)S(1)}, u32[]{:S(2)}, u32[]{:S(2)}) collective-permute-start(bf16[1056,128]{1,0:T(8,128)(2,1)S(1)} %collective-permute-done.24.rest_5_), channel_id=1, source_target_pairs={{1,0},{2,1},{3,2},{4,3},{5,4},{6,5},{7,6},{0,7},{9,8},{10,9},{11,1... | collective-permute-start | bytes 811016 | tf_op jit(solution)/shard_map/ppermute | solution.py:357
  256.7 1.9 collective-permute-start.25
  259.5 3.0 %collective-permute-done.26.rest_7_ = bf16[1056,128]{1,0:T(8,128)(2,1)S(1)} collective-permute-done((bf16[1056,128]{1,0:T(8,128)(2,1)S(1)}, bf16[1056,128]{1,0:T(8,128)(2,1)S(1)}, u32[]{:S(2)}, u32[]{:S(2)}) %collective-permute-start.26) | collective-permute-done | bytes 270368 | tf_op jit(solution)/shard_map/ppermute | solution.py:357
  262.5 5.3 %collective-permute-done.25.rest_6_ = bf16[1056,128]{1,0:T(8,128)(2,1)S(1)} collective-permute-done((bf16[1056,128]{1,0:T(8,128)(2,1)S(1)}, bf16[1056,128]{1,0:T(8,128)(2,1)S(1)}, u32[]{:S(2)}, u32[]{:S(2)}) %collective-permute-start.25) | collective-permute-done | bytes 270368 | tf_op jit(solution)/shard_map/ppermute | solution.py:356
  267.9 1.9 collective-permute-start.27
  269.8 6.8 %collective-permute-start.28 = (bf16[256,128]{1,0:T(8,128)(2,1)S(1)}, bf16[256,128]{1,0:T(8,128)(2,1)S(1)}, u32[]{:S(2)}, u32[]{:S(2)}) collective-permute-start(bf16[256,128]{1,0:T(8,128)(2,1)S(1)} %slice.14), channel_id=1, source_target_pairs={{0,8},{1,9},{2,10},{3,11},{4,12},{5,13},{6,14},{7,15},{8,0},{9,1},... | collective-permute-start | bytes 196616 | tf_op jit(solution)/shard_map/ppermute | solution.py:364
  276.6 1.5 collective-permute-done.27.rest_8_
  278.9 6.6 %shard_map.161 = (f32[256,128]{1,0:T(8,128)}, f32[256,128]{1,0:T(8,128)}, f32[256,128]{1,0:T(8,128)}) custom-call(s32[1]{0:T(128)} %bitcast.me_ref, f32[192]{0:T(256)} %get-tuple-element.27.counts_ref, bf16[8192,128]{1,0:T(8,128)(2,1)} %shard_map.154.dense_ref, bf16[48,128]{1,0:T(8,128)(2,1)} %get-tuple-element.29.rows_ref, ...), custom_call_target="tpu_custom_call" | custom-call | flops 536870912 | bytes 5242880 | tf_op jit(solution)/shard_map/pallas_call | solution.py:253
  286.1 4.8 %shard_map.162 = (f32[256,128]{1,0:T(8,128)}, f32[256,128]{1,0:T(8,128)}, f32[256,128]{1,0:T(8,128)}) custom-call(s32[1]{0:T(128)} %bitcast.me_ref, bf16[512,128]{1,0:T(8,128)(2,1)} %reduce-scatter.8.cloned.1.call-done.own_ref, bf16[256,128]{1,0:T(8,128)(2,1)} %copy-done.29, f32[768,128]{1,0:T(8,128)} %copy-done.2, bf16[1056,128]{1,0:T(8,128)(2,1)} %shard_map.159.rest_1_, ...), custom_call_target="tpu_custom_call" | custom-call | flops 134217728 | bytes 4194304 | tf_op jit(solution)/shard_map/pallas_call | solution.py:305
  (90 shorter events, 16.2 us)
Async XLA Ops:
  7.2 65.5 %reduce-scatter.4.cloned.1.call-start = ((), (), s32[]{:S(2)}) async-start(), calls=%async_computation.3 | async-start | bytes 1179648 | tf_op jit(solution)/shard_map/reduce_scatter | solution.py:346
  17.0 3.5 %copy-start.4 = (bf16[528,128]{1,0:T(8,128)(2,1)S(1)}, bf16[528,128]{1,0:T(8,128)(2,1)}, u32[]{:S(2)}) copy-start(bf16[528,128]{1,0:T(8,128)(2,1)} %get-tuple-element.28.rest_0_.own.users_ref) | copy-start | bytes 405508
  20.5 145.4 %reduce-scatter.6.cloned.1.call-start = ((), (), s32[]{:S(2)}) async-start(), calls=%async_computation.4 | async-start | bytes 1179648 | tf_op jit(solution)/shard_map/reduce_scatter | solution.py:346
  20.5 14.5 %collective-permute-start = (bf16[528,128]{1,0:T(8,128)(2,1)S(1)}, bf16[528,128]{1,0:T(8,128)(2,1)S(1)}, u32[]{:S(2)}, u32[]{:S(2)}) collective-permute-start(bf16[528,128]{1,0:T(8,128)(2,1)S(1)} %copy-done.4), channel_id=1, source_target_pairs={{0,8},{1,9},{2,10},{3,11},{4,12},{5,13},{6,14},{7,15},{8,0},{9,1},... | collective-permute-start | bytes 405512 | tf_op jit(solution)/shard_map/ppermute | solution.py:345
  35.0 0.7 copy-start.26
  37.4 15.9 %collective-permute-start.1 = (bf16[1056,128]{1,0:T(8,128)(2,1)}, bf16[1056,128]{1,0:T(8,128)(2,1)S(1)}, u32[]{:S(2)}, u32[]{:S(2)}) collective-permute-start(bf16[1056,128]{1,0:T(8,128)(2,1)} %shard_map.147.rest_3_), channel_id=1, source_target_pairs={{0,1},{1,2},{2,3},{3,4},{4,5},{5,6},{6,7},{7,0},{8,9},{9,10},{10,1... | collective-permute-start | bytes 811016 | tf_op jit(solution)/shard_map/ppermute | solution.py:356
  41.1 14.1 %collective-permute-start.2 = (bf16[1056,128]{1,0:T(8,128)(2,1)}, bf16[1056,128]{1,0:T(8,128)(2,1)S(1)}, u32[]{:S(2)}, u32[]{:S(2)}) collective-permute-start(bf16[1056,128]{1,0:T(8,128)(2,1)} %shard_map.147.rest_3_), channel_id=1, source_target_pairs={{1,0},{2,1},{3,2},{4,3},{5,4},{6,5},{7,6},{0,7},{9,8},{10,9},{11,1... | collective-permute-start | bytes 811016 | tf_op jit(solution)/shard_map/ppermute | solution.py:357
  53.3 7.1 %copy-start.1 = (bf16[1056,128]{1,0:T(8,128)(2,1)}, bf16[1056,128]{1,0:T(8,128)(2,1)S(1)}, u32[]{:S(2)}) copy-start(bf16[1056,128]{1,0:T(8,128)(2,1)S(1)} %collective-permute-done.1.rest_0_.rest_4_) | copy-start | bytes 811012
  53.3 11.7 %collective-permute-start.3 = (bf16[1056,128]{1,0:T(8,128)(2,1)S(1)}, bf16[1056,128]{1,0:T(8,128)(2,1)S(1)}, u32[]{:S(2)}, u32[]{:S(2)}) collective-permute-start(bf16[1056,128]{1,0:T(8,128)(2,1)S(1)} %collective-permute-done.1.rest_0_.rest_4_), channel_id=1, source_target_pairs={{0,1},{1,2},{2,3},{3,4},{4,5},{5,6},{6,7},{7,0},{8,9},{9,10},{10,1... | collective-permute-start | bytes 811016 | tf_op jit(solution)/shard_map/ppermute | solution.py:356
  55.2 9.2 %copy-start.15 = (bf16[1056,128]{1,0:T(8,128)(2,1)}, bf16[1056,128]{1,0:T(8,128)(2,1)S(1)}, u32[]{:S(2)}) copy-start(bf16[1056,128]{1,0:T(8,128)(2,1)S(1)} %collective-permute-done.2.rest_5_) | copy-start | bytes 811012
  55.2 10.8 %collective-permute-start.4 = (bf16[1056,128]{1,0:T(8,128)(2,1)S(1)}, bf16[1056,128]{1,0:T(8,128)(2,1)S(1)}, u32[]{:S(2)}, u32[]{:S(2)}) collective-permute-start(bf16[1056,128]{1,0:T(8,128)(2,1)S(1)} %collective-permute-done.2.rest_5_), channel_id=1, source_target_pairs={{1,0},{2,1},{3,2},{4,3},{5,4},{6,5},{7,6},{0,7},{9,8},{10,9},{11,1... | collective-permute-start | bytes 811016 | tf_op jit(solution)/shard_map/ppermute | solution.py:357
  64.9 27.6 %copy-start.17 = (bf16[1056,128]{1,0:T(8,128)(2,1)}, bf16[1056,128]{1,0:T(8,128)(2,1)S(1)}, u32[]{:S(2)}) copy-start(bf16[1056,128]{1,0:T(8,128)(2,1)S(1)} %collective-permute-done.3.rest_6_) | copy-start | bytes 811012
  66.0 26.5 %copy-start.19 = (bf16[1056,128]{1,0:T(8,128)(2,1)}, bf16[1056,128]{1,0:T(8,128)(2,1)S(1)}, u32[]{:S(2)}) copy-start(bf16[1056,128]{1,0:T(8,128)(2,1)S(1)} %collective-permute-done.4.rest_7_) | copy-start | bytes 811012
  66.0 9.6 %collective-permute-start.6 = (bf16[1056,128]{1,0:T(8,128)(2,1)S(1)}, bf16[1056,128]{1,0:T(8,128)(2,1)S(1)}, u32[]{:S(2)}, u32[]{:S(2)}) collective-permute-start(bf16[1056,128]{1,0:T(8,128)(2,1)S(1)} %collective-permute-done.4.rest_7_), channel_id=1, source_target_pairs={{1,0},{2,1},{3,2},{4,3},{5,4},{6,5},{7,6},{0,7},{9,8},{10,9},{11,1... | collective-permute-start | bytes 811016 | tf_op jit(solution)/shard_map/ppermute | solution.py:357
  70.7 9.6 %collective-permute-start.5 = (bf16[1056,128]{1,0:T(8,128)(2,1)S(1)}, bf16[1056,128]{1,0:T(8,128)(2,1)S(1)}, u32[]{:S(2)}, u32[]{:S(2)}) collective-permute-start(bf16[1056,128]{1,0:T(8,128)(2,1)S(1)} %collective-permute-done.3.rest_6_), channel_id=1, source_target_pairs={{0,1},{1,2},{2,3},{3,4},{4,5},{5,6},{6,7},{7,0},{8,9},{9,10},{10,1... | collective-permute-start | bytes 811016 | tf_op jit(solution)/shard_map/ppermute | solution.py:356
  75.7 16.9 %copy-start.21 = (bf16[1056,128]{1,0:T(8,128)(2,1)}, bf16[1056,128]{1,0:T(8,128)(2,1)S(1)}, u32[]{:S(2)}) copy-start(bf16[1056,128]{1,0:T(8,128)(2,1)S(1)} %collective-permute-done.6.rest_9_) | copy-start | bytes 811012
  80.3 12.3 %copy-start.23 = (bf16[1056,128]{1,0:T(8,128)(2,1)}, bf16[1056,128]{1,0:T(8,128)(2,1)S(1)}, u32[]{:S(2)}) copy-start(bf16[1056,128]{1,0:T(8,128)(2,1)S(1)} %collective-permute-done.5.rest_8_) | copy-start | bytes 811012
  80.3 12.3 %collective-permute-start.7 = (bf16[1056,128]{1,0:T(8,128)(2,1)S(1)}, bf16[1056,128]{1,0:T(8,128)(2,1)S(1)}, u32[]{:S(2)}, u32[]{:S(2)}) collective-permute-start(bf16[1056,128]{1,0:T(8,128)(2,1)S(1)} %collective-permute-done.5.rest_8_), channel_id=1, source_target_pairs={{0,1},{1,2},{2,3},{3,4},{4,5},{5,6},{6,7},{7,0},{8,9},{9,10},{10,1... | collective-permute-start | bytes 811016 | tf_op jit(solution)/shard_map/ppermute | solution.py:365
  82.2 10.3 %collective-permute-start.8 = (bf16[256,128]{1,0:T(8,128)(2,1)S(1)}, bf16[256,128]{1,0:T(8,128)(2,1)S(1)}, u32[]{:S(2)}, u32[]{:S(2)}) collective-permute-start(bf16[256,128]{1,0:T(8,128)(2,1)S(1)} %slice.12), channel_id=1, source_target_pairs={{0,8},{1,9},{2,10},{3,11},{4,12},{5,13},{6,14},{7,15},{8,0},{9,1},... | collective-permute-start | bytes 196616 | tf_op jit(solution)/shard_map/ppermute | solution.py:364
  92.5 0.6 copy-start.31
  93.1 0.7 copy-start.25
  98.7 9.0 %collective-permute-start.9 = (f32[768,128]{1,0:T(8,128)}, f32[768,128]{1,0:T(8,128)S(1)}, u32[]{:S(2)}, u32[]{:S(2)}) collective-permute-start(f32[768,128]{1,0:T(8,128)} %shard_map.150.rest_11_), channel_id=1, source_target_pairs={{0,496},{16,0},{32,16},{48,32},{64,48},{80,64},{96,80},{112,96},{1... | collective-permute-start | bytes 1179656 | tf_op jit(solution)/shard_map/ppermute | solution.py:368
  107.8 0.8 copy-start.3
  110.2 3.6 %copy-start.5 = (bf16[528,128]{1,0:T(8,128)(2,1)S(1)}, bf16[528,128]{1,0:T(8,128)(2,1)}, u32[]{:S(2)}) copy-start(bf16[528,128]{1,0:T(8,128)(2,1)} %shard_map.152.own.users_ref) | copy-start | bytes 405508
  113.8 144.9 %reduce-scatter.8.cloned.1.call-start = ((), (), s32[]{:S(2)}) async-start(), calls=%async_computation.5 | async-start | bytes 1179648 | tf_op jit(solution)/shard_map/reduce_scatter | solution.py:346
  113.8 10.8 %collective-permute-start.10 = (bf16[528,128]{1,0:T(8,128)(2,1)S(1)}, bf16[528,128]{1,0:T(8,128)(2,1)S(1)}, u32[]{:S(2)}, u32[]{:S(2)}) collective-permute-start(bf16[528,128]{1,0:T(8,128)(2,1)S(1)} %copy-done.5), channel_id=1, source_target_pairs={{0,8},{1,9},{2,10},{3,11},{4,12},{5,13},{6,14},{7,15},{8,0},{9,1},... | collective-permute-start | bytes 405512 | tf_op jit(solution)/shard_map/ppermute | solution.py:345
  124.6 0.6 copy-start.27
  127.0 14.9 %collective-permute-start.11 = (bf16[1056,128]{1,0:T(8,128)(2,1)}, bf16[1056,128]{1,0:T(8,128)(2,1)S(1)}, u32[]{:S(2)}, u32[]{:S(2)}) collective-permute-start(bf16[1056,128]{1,0:T(8,128)(2,1)} %shard_map.153.rest_1_), channel_id=1, source_target_pairs={{0,1},{1,2},{2,3},{3,4},{4,5},{5,6},{6,7},{7,0},{8,9},{9,10},{10,1... | collective-permute-start | bytes 811016 | tf_op jit(solution)/shard_map/ppermute | solution.py:356
  131.2 14.2 %collective-permute-start.12 = (bf16[1056,128]{1,0:T(8,128)(2,1)}, bf16[1056,128]{1,0:T(8,128)(2,1)S(1)}, u32[]{:S(2)}, u32[]{:S(2)}) collective-permute-start(bf16[1056,128]{1,0:T(8,128)(2,1)} %shard_map.153.rest_1_), channel_id=1, source_target_pairs={{1,0},{2,1},{3,2},{4,3},{5,4},{6,5},{7,6},{0,7},{9,8},{10,9},{11,1... | collective-permute-start | bytes 811016 | tf_op jit(solution)/shard_map/ppermute | solution.py:357
  141.8 7.5 %copy-start = (bf16[1056,128]{1,0:T(8,128)(2,1)}, bf16[1056,128]{1,0:T(8,128)(2,1)S(1)}, u32[]{:S(2)}) copy-start(bf16[1056,128]{1,0:T(8,128)(2,1)S(1)} %collective-permute-done.11.rest_0_.rest_2_) | copy-start | bytes 811012
  141.8 15.8 %collective-permute-start.13 = (bf16[1056,128]{1,0:T(8,128)(2,1)S(1)}, bf16[1056,128]{1,0:T(8,128)(2,1)S(1)}, u32[]{:S(2)}, u32[]{:S(2)}) collective-permute-start(bf16[1056,128]{1,0:T(8,128)(2,1)S(1)} %collective-permute-done.11.rest_0_.rest_2_), channel_id=1, source_target_pairs={{0,1},{1,2},{2,3},{3,4},{4,5},{5,6},{6,7},{7,0},{8,9},{9,10},{10,1... | collective-permute-start | bytes 811016 | tf_op jit(solution)/shard_map/ppermute | solution.py:356
  145.4 7.6 %copy-start.14 = (bf16[1056,128]{1,0:T(8,128)(2,1)}, bf16[1056,128]{1,0:T(8,128)(2,1)S(1)}, u32[]{:S(2)}) copy-start(bf16[1056,128]{1,0:T(8,128)(2,1)S(1)} %collective-permute-done.12.rest_3_) | copy-start | bytes 811012
  145.4 13.0 %collective-permute-start.14 = (bf16[1056,128]{1,0:T(8,128)(2,1)S(1)}, bf16[1056,128]{1,0:T(8,128)(2,1)S(1)}, u32[]{:S(2)}, u32[]{:S(2)}) collective-permute-start(bf16[1056,128]{1,0:T(8,128)(2,1)S(1)} %collective-permute-done.12.rest_3_), channel_id=1, source_target_pairs={{1,0},{2,1},{3,2},{4,3},{5,4},{6,5},{7,6},{0,7},{9,8},{10,9},{11,1... | collective-permute-start | bytes 811016 | tf_op jit(solution)/shard_map/ppermute | solution.py:357
  157.6 29.8 %copy-start.16 = (bf16[1056,128]{1,0:T(8,128)(2,1)}, bf16[1056,128]{1,0:T(8,128)(2,1)S(1)}, u32[]{:S(2)}) copy-start(bf16[1056,128]{1,0:T(8,128)(2,1)S(1)} %collective-permute-done.13.rest_4_) | copy-start | bytes 811012
  158.5 28.9 %copy-start.18 = (bf16[1056,128]{1,0:T(8,128)(2,1)}, bf16[1056,128]{1,0:T(8,128)(2,1)S(1)}, u32[]{:S(2)}) copy-start(bf16[1056,128]{1,0:T(8,128)(2,1)S(1)} %collective-permute-done.14.rest_5_) | copy-start | bytes 811012
  158.5 11.6 %collective-permute-start.16 = (bf16[1056,128]{1,0:T(8,128)(2,1)S(1)}, bf16[1056,128]{1,0:T(8,128)(2,1)S(1)}, u32[]{:S(2)}, u32[]{:S(2)}) collective-permute-start(bf16[1056,128]{1,0:T(8,128)(2,1)S(1)} %collective-permute-done.14.rest_5_), channel_id=1, source_target_pairs={{1,0},{2,1},{3,2},{4,3},{5,4},{6,5},{7,6},{0,7},{9,8},{10,9},{11,1... | collective-permute-start | bytes 811016 | tf_op jit(solution)/shard_map/ppermute | solution.py:357
  164.0 11.4 %collective-permute-start.15 = (bf16[1056,128]{1,0:T(8,128)(2,1)S(1)}, bf16[1056,128]{1,0:T(8,128)(2,1)S(1)}, u32[]{:S(2)}, u32[]{:S(2)}) collective-permute-start(bf16[1056,128]{1,0:T(8,128)(2,1)S(1)} %collective-permute-done.13.rest_4_), channel_id=1, source_target_pairs={{0,1},{1,2},{2,3},{3,4},{4,5},{5,6},{6,7},{7,0},{8,9},{9,10},{10,1... | collective-permute-start | bytes 811016 | tf_op jit(solution)/shard_map/ppermute | solution.py:356
  170.1 17.3 %copy-start.20 = (bf16[1056,128]{1,0:T(8,128)(2,1)}, bf16[1056,128]{1,0:T(8,128)(2,1)S(1)}, u32[]{:S(2)}) copy-start(bf16[1056,128]{1,0:T(8,128)(2,1)S(1)} %collective-permute-done.16.rest_7_) | copy-start | bytes 811012
  175.4 12.0 %copy-start.22 = (bf16[1056,128]{1,0:T(8,128)(2,1)}, bf16[1056,128]{1,0:T(8,128)(2,1)S(1)}, u32[]{:S(2)}) copy-start(bf16[1056,128]{1,0:T(8,128)(2,1)S(1)} %collective-permute-done.15.rest_6_) | copy-start | bytes 811012
  175.4 12.0 %collective-permute-start.17 = (bf16[1056,128]{1,0:T(8,128)(2,1)S(1)}, bf16[1056,128]{1,0:T(8,128)(2,1)S(1)}, u32[]{:S(2)}, u32[]{:S(2)}) collective-permute-start(bf16[1056,128]{1,0:T(8,128)(2,1)S(1)} %collective-permute-done.15.rest_6_), channel_id=1, source_target_pairs={{0,1},{1,2},{2,3},{3,4},{4,5},{5,6},{6,7},{7,0},{8,9},{9,10},{10,1... | collective-permute-start | bytes 811016 | tf_op jit(solution)/shard_map/ppermute | solution.py:365
  177.3 10.1 %collective-permute-start.18 = (bf16[256,128]{1,0:T(8,128)(2,1)S(1)}, bf16[256,128]{1,0:T(8,128)(2,1)S(1)}, u32[]{:S(2)}, u32[]{:S(2)}) collective-permute-start(bf16[256,128]{1,0:T(8,128)(2,1)S(1)} %slice.13), channel_id=1, source_target_pairs={{0,8},{1,9},{2,10},{3,11},{4,12},{5,13},{6,14},{7,15},{8,0},{9,1},... | collective-permute-start | bytes 196616 | tf_op jit(solution)/shard_map/ppermute | solution.py:364
  187.4 0.6 copy-start.30
  188.0 0.7 copy-start.24
  193.6 8.8 %collective-permute-start.19 = (f32[768,128]{1,0:T(8,128)}, f32[768,128]{1,0:T(8,128)S(1)}, u32[]{:S(2)}, u32[]{:S(2)}) collective-permute-start(f32[768,128]{1,0:T(8,128)} %shard_map.156.rest_9_), channel_id=1, source_target_pairs={{0,496},{16,0},{32,16},{48,32},{64,48},{80,64},{96,80},{112,96},{1... | collective-permute-start | bytes 1179656 | tf_op jit(solution)/shard_map/ppermute | solution.py:368
  202.4 0.8 copy-start.2
  204.8 3.5 %copy-start.6 = (bf16[528,128]{1,0:T(8,128)(2,1)S(1)}, bf16[528,128]{1,0:T(8,128)(2,1)}, u32[]{:S(2)}) copy-start(bf16[528,128]{1,0:T(8,128)(2,1)} %shard_map.158.own.users_ref) | copy-start | bytes 405508
  208.3 10.9 %collective-permute-start.20 = (bf16[528,128]{1,0:T(8,128)(2,1)S(1)}, bf16[528,128]{1,0:T(8,128)(2,1)S(1)}, u32[]{:S(2)}, u32[]{:S(2)}) collective-permute-start(bf16[528,128]{1,0:T(8,128)(2,1)S(1)} %copy-done.6), channel_id=1, source_target_pairs={{0,8},{1,9},{2,10},{3,11},{4,12},{5,13},{6,14},{7,15},{8,0},{9,1},... | collective-permute-start | bytes 405512 | tf_op jit(solution)/shard_map/ppermute | solution.py:345
  219.2 0.7 copy-start.28
  221.6 15.2 %collective-permute-start.22 = (bf16[1056,128]{1,0:T(8,128)(2,1)}, bf16[1056,128]{1,0:T(8,128)(2,1)S(1)}, u32[]{:S(2)}, u32[]{:S(2)}) collective-permute-start(bf16[1056,128]{1,0:T(8,128)(2,1)} %shard_map.159.rest_1_), channel_id=1, source_target_pairs={{1,0},{2,1},{3,2},{4,3},{5,4},{6,5},{7,6},{0,7},{9,8},{10,9},{11,1... | collective-permute-start | bytes 811016 | tf_op jit(solution)/shard_map/ppermute | solution.py:357
  226.7 15.7 %collective-permute-start.21 = (bf16[1056,128]{1,0:T(8,128)(2,1)}, bf16[1056,128]{1,0:T(8,128)(2,1)S(1)}, u32[]{:S(2)}, u32[]{:S(2)}) collective-permute-start(bf16[1056,128]{1,0:T(8,128)(2,1)} %shard_map.159.rest_1_), channel_id=1, source_target_pairs={{0,1},{1,2},{2,3},{3,4},{4,5},{5,6},{6,7},{7,0},{8,9},{9,10},{10,1... | collective-permute-start | bytes 811016 | tf_op jit(solution)/shard_map/ppermute | solution.py:356
  236.8 41.4 %copy-start.7 = (bf16[1056,128]{1,0:T(8,128)(2,1)}, bf16[1056,128]{1,0:T(8,128)(2,1)S(1)}, u32[]{:S(2)}) copy-start(bf16[1056,128]{1,0:T(8,128)(2,1)S(1)} %collective-permute-done.22.rest_3_) | copy-start | bytes 811012
  236.8 14.3 %collective-permute-start.24 = (bf16[1056,128]{1,0:T(8,128)(2,1)S(1)}, bf16[1056,128]{1,0:T(8,128)(2,1)S(1)}, u32[]{:S(2)}, u32[]{:S(2)}) collective-permute-start(bf16[1056,128]{1,0:T(8,128)(2,1)S(1)} %collective-permute-done.22.rest_3_), channel_id=1, source_target_pairs={{1,0},{2,1},{3,2},{4,3},{5,4},{6,5},{7,6},{0,7},{9,8},{10,9},{11,1... | collective-permute-start | bytes 811016 | tf_op jit(solution)/shard_map/ppermute | solution.py:357
  242.4 35.7 %copy-start.8 = (bf16[1056,128]{1,0:T(8,128)(2,1)}, bf16[1056,128]{1,0:T(8,128)(2,1)S(1)}, u32[]{:S(2)}) copy-start(bf16[1056,128]{1,0:T(8,128)(2,1)S(1)} %collective-permute-done.21.rest_2_) | copy-start | bytes 811012
  242.4 14.3 %collective-permute-start.23 = (bf16[1056,128]{1,0:T(8,128)(2,1)S(1)}, bf16[1056,128]{1,0:T(8,128)(2,1)S(1)}, u32[]{:S(2)}, u32[]{:S(2)}) collective-permute-start(bf16[1056,128]{1,0:T(8,128)(2,1)S(1)} %collective-permute-done.21.rest_2_), channel_id=1, source_target_pairs={{0,1},{1,2},{2,3},{3,4},{4,5},{5,6},{6,7},{7,0},{8,9},{9,10},{10,1... | collective-permute-start | bytes 811016 | tf_op jit(solution)/shard_map/ppermute | solution.py:356
  251.1 27.1 %copy-start.9 = (bf16[1056,128]{1,0:T(8,128)(2,1)}, bf16[1056,128]{1,0:T(8,128)(2,1)S(1)}, u32[]{:S(2)}) copy-start(bf16[1056,128]{1,0:T(8,128)(2,1)S(1)} %collective-permute-done.24.rest_5_) | copy-start | bytes 811012
  251.1 11.4 %collective-permute-start.26 = (bf16[1056,128]{1,0:T(8,128)(2,1)S(1)}, bf16[1056,128]{1,0:T(8,128)(2,1)S(1)}, u32[]{:S(2)}, u32[]{:S(2)}) collective-permute-start(bf16[1056,128]{1,0:T(8,128)(2,1)S(1)} %collective-permute-done.24.rest_5_), channel_id=1, source_target_pairs={{1,0},{2,1},{3,2},{4,3},{5,4},{6,5},{7,6},{0,7},{9,8},{10,9},{11,1... | collective-permute-start | bytes 811016 | tf_op jit(solution)/shard_map/ppermute | solution.py:357
  256.7 21.5 %copy-start.10 = (bf16[1056,128]{1,0:T(8,128)(2,1)}, bf16[1056,128]{1,0:T(8,128)(2,1)S(1)}, u32[]{:S(2)}) copy-start(bf16[1056,128]{1,0:T(8,128)(2,1)S(1)} %collective-permute-done.23.rest_4_) | copy-start | bytes 811012
  256.7 11.2 %collective-permute-start.25 = (bf16[1056,128]{1,0:T(8,128)(2,1)S(1)}, bf16[1056,128]{1,0:T(8,128)(2,1)S(1)}, u32[]{:S(2)}, u32[]{:S(2)}) collective-permute-start(bf16[1056,128]{1,0:T(8,128)(2,1)S(1)} %collective-permute-done.23.rest_4_), channel_id=1, source_target_pairs={{0,1},{1,2},{2,3},{3,4},{4,5},{5,6},{6,7},{7,0},{8,9},{9,10},{10,1... | collective-permute-start | bytes 811016 | tf_op jit(solution)/shard_map/ppermute | solution.py:356
  262.5 15.6 %copy-start.11 = (bf16[1056,128]{1,0:T(8,128)(2,1)}, bf16[1056,128]{1,0:T(8,128)(2,1)S(1)}, u32[]{:S(2)}) copy-start(bf16[1056,128]{1,0:T(8,128)(2,1)S(1)} %collective-permute-done.26.rest_7_) | copy-start | bytes 811012
  267.9 10.3 %copy-start.12 = (bf16[1056,128]{1,0:T(8,128)(2,1)}, bf16[1056,128]{1,0:T(8,128)(2,1)S(1)}, u32[]{:S(2)}) copy-start(bf16[1056,128]{1,0:T(8,128)(2,1)S(1)} %collective-permute-done.25.rest_6_) | copy-start | bytes 811012
  267.9 10.3 %collective-permute-start.27 = (bf16[1056,128]{1,0:T(8,128)(2,1)S(1)}, bf16[1056,128]{1,0:T(8,128)(2,1)S(1)}, u32[]{:S(2)}, u32[]{:S(2)}) collective-permute-start(bf16[1056,128]{1,0:T(8,128)(2,1)S(1)} %collective-permute-done.25.rest_6_), channel_id=1, source_target_pairs={{0,1},{1,2},{2,3},{3,4},{4,5},{5,6},{6,7},{7,0},{8,9},{9,10},{10,1... | collective-permute-start | bytes 811016 | tf_op jit(solution)/shard_map/ppermute | solution.py:365
  269.8 15.7 %collective-permute-start.28 = (bf16[256,128]{1,0:T(8,128)(2,1)S(1)}, bf16[256,128]{1,0:T(8,128)(2,1)S(1)}, u32[]{:S(2)}, u32[]{:S(2)}) collective-permute-start(bf16[256,128]{1,0:T(8,128)(2,1)S(1)} %slice.14), channel_id=1, source_target_pairs={{0,8},{1,9},{2,10},{3,11},{4,12},{5,13},{6,14},{7,15},{8,0},{9,1},... | collective-permute-start | bytes 196616 | tf_op jit(solution)/shard_map/ppermute | solution.py:364
  278.1 0.7 copy-start.13
  285.5 0.6 copy-start.29
Sparse Core Ops, SparseCore 0:
  20.6 47.7 reduce-scatter.3
  113.9 47.3 reduce-scatter.5
  208.4 44.8 reduce-scatter.7

commit v5 on v3

--- a/solution.py
+++ b/solution.py
@@ -187,41 +187,22 @@
         shape(ITEM_TILES * TILE, BF16),
         [SMEM, VMEM, VMEM],
         flops=2 * ITEM_TILES * USER_ROWS * TILE * K,
-        moved=3 << 20,
+        moved=40 << 20,
     )(me, users, dense)
-
-
-def fetched(pieces, top, held, sems):
-    rows = held.shape[1]
-    copies = [
-        pltpu.make_async_copy(piece.at[pl.ds(top, rows)], held.at[i], sems.at[i])
-        for i, piece in enumerate(pieces)
-    ]
-    for copy in copies:
-        copy.start()
-    return copies
-
-
-def fetch_scratch(rows):
-    count = len(DISTANCES)
-    return [pltpu.VMEM((count, rows, K), BF16), pltpu.SemaphoreType.DMA((count,))]
 
 
 def user_body(s, states, me_ref, counts_ref, dense_ref, rows_ref, *rest):
     state_refs, pieces = rest[:states], rest[states : states + len(DISTANCES)]
-    *outs, held, sems = rest[states + len(DISTANCES) :]
-    outs = outs[-3:] if s + 1 == STEPS else outs[-2:]
-    copies = fetched(pieces, 0, held, sems)
+    outs = rest[-3:] if s + 1 == STEPS else rest[-2:]
     fac, first, second = loaded(state_refs)
     users = fac.astype(BF16)
     total = jnp.zeros((USER_ROWS, K), F32)
     upper = lax.broadcasted_iota(jnp.int32, (USER_ROWS, TILE), 0) < TILE
     me = me_ref[0]
-    for i, distance in enumerate(DISTANCES):
-        copies[i].wait()
-        place = (me % RING + distance + RING) % RING
+    for piece, distance in zip(pieces, DISTANCES):
+        place = (me % RING + distance * me_ref[1] + RING) % RING
         for swap in range(2):
-            rows = held[i, swap * ITEM_ROWS : (swap + 1) * ITEM_ROWS]
+            rows = piece[swap * ITEM_ROWS : (swap + 1) * ITEM_ROWS]
             predicted = lax.dot_general(
                 users, rows, (((1,), (1,)), ((), ())), preferred_element_type=F32
             )
@@ -253,8 +234,7 @@
     return kernel_call(
         functools.partial(user_body, s, len(state)),
         outs,
-        [SMEM, SMEM] + [VMEM] * (2 + len(state)) + [ANY] * (len(pieces) + len(later)),
-        scratch=fetch_scratch(2 * ITEM_ROWS),
+        [SMEM, SMEM] + [VMEM] * (2 + len(state) + len(pieces)) + [ANY] * len(later),
         flops=4 * ITEM_TILES * USER_ROWS * TILE * K,
         moved=5 << 20,
     )(me, counts, dense, rows, *state, *pieces, *later)
@@ -262,17 +242,15 @@
 
 def item_body(s, states, me_ref, own_ref, other_ref, *rest):
     state_refs, pieces = rest[:states], rest[states : states + len(DISTANCES)]
-    *outs, held, sems = rest[states + len(DISTANCES) :]
-    copies = fetched(pieces, 2 * ITEM_ROWS, held, sems)
+    outs = rest[states + len(DISTANCES) :]
     lane = lax.broadcasted_iota(jnp.int32, (COUNT_ROWS, K), 1)
     weighted = [jnp.zeros((K, K), F32) for _ in range(2)]
-    for i, copy in enumerate(copies):
-        copy.wait()
+    for piece in pieces:
         for swap in range(2):
-            top = swap * PART
-            counts = held[i, top + USER_ROWS : top + PART].astype(F32)
+            top = 2 * ITEM_ROWS + swap * PART
+            counts = piece[top + USER_ROWS : top + PART].astype(F32)
             for u in range(USER_TILES):
-                users = held[i, top + u * TILE : top + (u + 1) * TILE]
+                users = piece[top + u * TILE : top + (u + 1) * TILE]
                 gram = lax.dot_general(
                     users, users, (((0,), (0,)), ((), ())), preferred_element_type=F32
                 )
@@ -305,8 +283,7 @@
     return kernel_call(
         functools.partial(item_body, s, len(state)),
         outs,
-        [SMEM] + [VMEM] * (2 + len(state)) + [ANY] * len(pieces),
-        scratch=fetch_scratch(2 * PART),
+        [SMEM] + [VMEM] * (2 + len(state) + len(pieces)),
         flops=2 * 32 * TILE * K * K,
         moved=4 << 20,
     )(me, own, other, *state, *pieces)
@@ -329,13 +306,22 @@
     tile_counts,
 ):
     strata = lax.axis_size("blk")
-    forward = [(z * RING + y, z * RING + (y + 1) % RING) for z in range(2) for y in range(RING)]
-    backward = [(target, source) for source, target in forward]
+    members = 2 * RING
+
+    def ring_route(step):
+        return [
+            (b * members + n, b * members + n // RING * RING + (n + (-step if b % 2 else step)) % RING)
+            for b in range(strata)
+            for n in range(members)
+        ]
+
+    forward, backward = ring_route(1), ring_route(-1)
     across = [(n, (n + RING) % (2 * RING)) for n in range(2 * RING)]
     rings = [[z * RING + y for y in range(RING)] for z in range(2)]
 
     earlier = [(b, (b - 1) % strata) for b in range(strata)]
-    me = lax.axis_index("narrow").reshape(1).astype(jnp.int32)
+    way = 1 - 2 * (lax.axis_index("blk") % 2)
+    me = jnp.stack([lax.axis_index("narrow"), way]).astype(jnp.int32)
     users_at, items_at = user_tiles.reshape(-1), item_tiles.reshape(-1)
     live = tile_counts.reshape(-1)
     first, rows, counts = opening(users_at, items_at, live, user_factors, item_factors)
@@ -354,16 +340,16 @@
         pieces = [load]
         up = down = load
         for step in range(3):
-            up = lax.ppermute(up, "narrow", forward)
-            down = lax.ppermute(down, "narrow", backward)
+            up = lax.ppermute(up, ("blk", "narrow"), forward)
+            down = lax.ppermute(down, ("blk", "narrow"), backward)
             pieces += [up, down]
             if step == 1 and s + 1 < STEPS:
                 dense_next = dense_ratings(s + 1, users_at, items_at, live, ratings, pieces[1])
                 up = after(up, dense_next)
-            if step == (1 if s > 0 else 2):
+            if step == 2:
                 ready = after(partial[ITEM_ROWS:], up, down)
                 other = lax.ppermute(ready, "narrow", across)
-        pieces.append(lax.ppermute(after(up, other) if s > 0 else up, "narrow", forward))
+        pieces.append(lax.ppermute(after(up, ready), ("blk", "narrow"), forward))
         item_state = item_step(s, me, partial, other, item_state, pieces)
         if s + 1 < STEPS:
             moved = lax.ppermute(item_state[0], "blk", earlier)

time: 289 us -> 290 us (level)
  starting transfers between devices: 114 us -> 124 us
  Pallas kernels: 35.1 us -> 28.5 us
    reduce_scatter x3, waiting for transfers between devices: 6.51 us -> 0.06 us  [per_device(): lax.psum_scatter(rating_part(me, first, dense), 'narrow', scatter_dimensi...]
    pallas_call x3, Pallas kernels: 14.9 us -> 9.03 us  [user_step(): kernel_call(functools.partial(user_body, s, len(state)), outs, [SMEM, SME...]
    ppermute x3, starting transfers between devices: 20.1 us -> 25 us  [per_device(): other = lax.ppermute(ready, 'narrow', across)]
    ppermute x3, starting transfers between devices: 21.7 us -> 25.8 us  [per_device(): load = packed(first, lax.ppermute(first, 'narrow', across))]
    ppermute x3, waiting for transfers between devices: 3.14 us -> 7.15 us  [per_device(): other = lax.ppermute(ready, 'narrow', across)]
    unnamed x118 -> x128, local copies, waits for them, and re-layouts: 39.6 us -> 36.8 us
  transfers between devices with their start and end apart: 32 -> 32, of which waited for: 19 -> 18; matrix products, arithmetic and copies ran while one was open for 1% -> 1% of each run, Pallas kernels for 4% -> 4%
where the time goes in v5:
time: 290 us; the launch traced here: 286 us
  starting transfers between devices  124 us (43%)
  waiting for transfers between devices  77.5 us (27%)
  local copies, waits for them, and re-layouts  39.7 us (14%)
  Pallas kernels  28.5 us (10%)
  between operations  14.5 us (5%)
    ppermute x9, starting transfers between devices, per_device(): down = lax.ppermute(down, ('blk', 'narrow'), backward)  37.8 us
    unnamed x128, local copies, waits for them, and re-layouts  36.8 us
    ppermute x9, waiting for transfers between devices, per_device(): down = lax.ppermute(down, ('blk', 'narrow'), backward)  25.9 us
    ppermute x9, waiting for transfers between devices, per_device(): up = lax.ppermute(up, ('blk', 'narrow'), forward)  25.8 us
    ppermute x3, starting transfers between devices, per_device(): load = packed(first, lax.ppermute(first, 'narrow', across))  25.8 us
    ppermute x3, starting transfers between devices, per_device(): other = lax.ppermute(ready, 'narrow', across)  25 us
    ppermute x9, starting transfers between devices, per_device(): up = lax.ppermute(up, ('blk', 'narrow'), forward)  22.6 us
    ppermute x3, waiting for transfers between devices, per_device(): load = packed(first, lax.ppermute(first, 'narrow', across))  17.8 us
  transfers between devices with their start and end apart: 32, of which 18 were waited for; matrix products, arithmetic and copies ran while one was open for 1% of the time, Pallas kernels for 4%

profile of v5, /device:TPU:6, one launch (start us, length us, event | category | flops | bytes accessed | tf_op | source)
XLA Modules:
  0.0 285.9 jit_solution(5140702108015325599)
XLA Ops:
  11.3 2.9 shard_map.145
  14.8 2.0 copy-done
  16.8 1.4 shard_map.146.dense_ref
  18.2 1.3 shard_map.149
  19.6 1.4 copy-done.8
  22.0 11.0 %collective-permute-start = (bf16[528,128]{1,0:T(8,128)(2,1)}, bf16[528,128]{1,0:T(8,128)(2,1)S(1)}, u32[]{:S(2)}, u32[]{:S(2)}) collective-permute-start(bf16[528,128]{1,0:T(8,128)(2,1)} %copy-done.28), channel_id=1, source_target_pairs={{0,8},{1,9},{2,10},{3,11},{4,12},{5,13},{6,14},{7,15},{8,0},{9,1},... | collective-permute-start | bytes 405512 | tf_op jit(solution)/shard_map/ppermute | solution.py:332
  33.0 4.1 %collective-permute-done.other = bf16[528,128]{1,0:T(8,128)(2,1)S(1)} collective-permute-done((bf16[528,128]{1,0:T(8,128)(2,1)}, bf16[528,128]{1,0:T(8,128)(2,1)S(1)}, u32[]{:S(2)}, u32[]{:S(2)}) %collective-permute-start) | collective-permute-done | bytes 135200 | tf_op jit(solution)/shard_map/ppermute | solution.py:332
  38.0 3.5 %collective-permute-start.1 = (bf16[1056,128]{1,0:T(8,128)(2,1)S(1)}, bf16[1056,128]{1,0:T(8,128)(2,1)S(1)}, u32[]{:S(2)}, u32[]{:S(2)}) collective-permute-start(bf16[1056,128]{1,0:T(8,128)(2,1)S(1)} %shard_map.147.rest_3_), channel_id=1, source_target_pairs={{0,1},{1,2},{2,3},{3,4},{4,5},{5,6},{6,7},{7,0},{8,9},{9,10},{10,1... | collective-permute-start | bytes 811016 | tf_op jit(solution)/shard_map/ppermute | solution.py:343
  41.5 3.5 %collective-permute-start.2 = (bf16[1056,128]{1,0:T(8,128)(2,1)S(1)}, bf16[1056,128]{1,0:T(8,128)(2,1)S(1)}, u32[]{:S(2)}, u32[]{:S(2)}) collective-permute-start(bf16[1056,128]{1,0:T(8,128)(2,1)S(1)} %shard_map.147.rest_3_), channel_id=1, source_target_pairs={{0,7},{1,0},{2,1},{3,2},{4,3},{5,4},{6,5},{7,6},{8,15},{9,8},{10,9... | collective-permute-start | bytes 811016 | tf_op jit(solution)/shard_map/ppermute | solution.py:344
  45.8 6.1 %collective-permute-done.1.rest_0_.rest_4_ = bf16[1056,128]{1,0:T(8,128)(2,1)S(1)} collective-permute-done((bf16[1056,128]{1,0:T(8,128)(2,1)S(1)}, bf16[1056,128]{1,0:T(8,128)(2,1)S(1)}, u32[]{:S(2)}, u32[]{:S(2)}) %collective-permute-start.1) | collective-permute-done | bytes 270368 | tf_op jit(solution)/shard_map/ppermute | solution.py:343
  51.9 1.9 collective-permute-start.3
  53.8 8.0 %collective-permute-start.4 = (bf16[1056,128]{1,0:T(8,128)(2,1)S(1)}, bf16[1056,128]{1,0:T(8,128)(2,1)}, u32[]{:S(2)}, u32[]{:S(2)}) collective-permute-start(bf16[1056,128]{1,0:T(8,128)(2,1)S(1)} %collective-permute-done.2.rest_5_), channel_id=1, source_target_pairs={{0,7},{1,0},{2,1},{3,2},{4,3},{5,4},{6,5},{7,6},{8,15},{9,8},{10,9... | collective-permute-start | bytes 811016 | tf_op jit(solution)/shard_map/ppermute | solution.py:344
  63.8 1.7 shard_map.148.dense_ref
  65.5 1.3 copy-done.2
  66.8 2.6 collective-permute-done.3.rest_6_
  69.4 3.0 %collective-permute-start.6 = (bf16[1056,128]{1,0:T(8,128)(2,1)}, bf16[1056,128]{1,0:T(8,128)(2,1)}, u32[]{:S(2)}, u32[]{:S(2)}) collective-permute-start(bf16[1056,128]{1,0:T(8,128)(2,1)} %collective-permute-done.4.rest_7_), channel_id=1, source_target_pairs={{0,7},{1,0},{2,1},{3,2},{4,3},{5,4},{6,5},{7,6},{8,15},{9,8},{10,9... | collective-permute-start | bytes 811016 | tf_op jit(solution)/shard_map/ppermute | solution.py:344
  72.4 2.8 collective-permute-start.5
  75.3 1.0 slice.12
  76.3 4.0 %collective-permute-done.6.rest_9_ = bf16[1056,128]{1,0:T(8,128)(2,1)} collective-permute-done((bf16[1056,128]{1,0:T(8,128)(2,1)}, bf16[1056,128]{1,0:T(8,128)(2,1)}, u32[]{:S(2)}, u32[]{:S(2)}) %collective-permute-start.6) | collective-permute-done | bytes 270368 | tf_op jit(solution)/shard_map/ppermute | solution.py:344
  80.3 2.0 collective-permute-done.5.rest_8_
  82.3 1.9 collective-permute-start.7
  84.2 8.7 %collective-permute-start.8 = (bf16[256,128]{1,0:T(8,128)(2,1)S(1)}, bf16[256,128]{1,0:T(8,128)(2,1)S(1)}, u32[]{:S(2)}, u32[]{:S(2)}) collective-permute-start(bf16[256,128]{1,0:T(8,128)(2,1)S(1)} %slice.12), channel_id=1, source_target_pairs={{0,8},{1,9},{2,10},{3,11},{4,12},{5,13},{6,14},{7,15},{8,0},{9,1},... | collective-permute-start | bytes 196616 | tf_op jit(solution)/shard_map/ppermute | solution.py:351
  93.0 2.9 collective-permute-done.8.other_ref
  102.3 2.3 shard_map.150.rest_11_
  104.6 4.2 %collective-permute-start.9 = (f32[768,128]{1,0:T(8,128)S(1)}, f32[768,128]{1,0:T(8,128)S(1)}, u32[]{:S(2)}, u32[]{:S(2)}) collective-permute-start(f32[768,128]{1,0:T(8,128)S(1)} %shard_map.150.rest_11_), channel_id=1, source_target_pairs={{0,496},{16,0},{32,16},{48,32},{64,48},{80,64},{96,80},{112,96},{1... | collective-permute-start | bytes 1179656 | tf_op jit(solution)/shard_map/ppermute | solution.py:355
  110.4 2.9 shard_map.151
  114.8 1.3 shard_map.155
  117.9 7.3 %collective-permute-start.10 = (bf16[528,128]{1,0:T(8,128)(2,1)}, bf16[528,128]{1,0:T(8,128)(2,1)S(1)}, u32[]{:S(2)}, u32[]{:S(2)}) collective-permute-start(bf16[528,128]{1,0:T(8,128)(2,1)} %copy-done.26), channel_id=1, source_target_pairs={{0,8},{1,9},{2,10},{3,11},{4,12},{5,13},{6,14},{7,15},{8,0},{9,1},... | collective-permute-start | bytes 405512 | tf_op jit(solution)/shard_map/ppermute | solution.py:332
  125.2 6.1 %collective-permute-done.10.other = bf16[528,128]{1,0:T(8,128)(2,1)S(1)} collective-permute-done((bf16[528,128]{1,0:T(8,128)(2,1)}, bf16[528,128]{1,0:T(8,128)(2,1)S(1)}, u32[]{:S(2)}, u32[]{:S(2)}) %collective-permute-start.10) | collective-permute-done | bytes 135200 | tf_op jit(solution)/shard_map/ppermute | solution.py:332
  132.3 1.9 collective-permute-start.11
  134.2 5.1 %collective-permute-start.12 = (bf16[1056,128]{1,0:T(8,128)(2,1)S(1)}, bf16[1056,128]{1,0:T(8,128)(2,1)S(1)}, u32[]{:S(2)}, u32[]{:S(2)}) collective-permute-start(bf16[1056,128]{1,0:T(8,128)(2,1)S(1)} %shard_map.153.rest_1_), channel_id=1, source_target_pairs={{0,7},{1,0},{2,1},{3,2},{4,3},{5,4},{6,5},{7,6},{8,15},{9,8},{10,9... | collective-permute-start | bytes 811016 | tf_op jit(solution)/shard_map/ppermute | solution.py:344
  140.0 7.0 %collective-permute-done.11.rest_0_.rest_2_ = bf16[1056,128]{1,0:T(8,128)(2,1)S(1)} collective-permute-done((bf16[1056,128]{1,0:T(8,128)(2,1)S(1)}, bf16[1056,128]{1,0:T(8,128)(2,1)S(1)}, u32[]{:S(2)}, u32[]{:S(2)}) %collective-permute-start.11) | collective-permute-done | bytes 270368 | tf_op jit(solution)/shard_map/ppermute | solution.py:343
  147.0 1.9 collective-permute-start.13
  149.0 5.1 %collective-permute-start.14 = (bf16[1056,128]{1,0:T(8,128)(2,1)S(1)}, bf16[1056,128]{1,0:T(8,128)(2,1)}, u32[]{:S(2)}, u32[]{:S(2)}) collective-permute-start(bf16[1056,128]{1,0:T(8,128)(2,1)S(1)} %collective-permute-done.12.rest_3_), channel_id=1, source_target_pairs={{0,7},{1,0},{2,1},{3,2},{4,3},{5,4},{6,5},{7,6},{8,15},{9,8},{10,9... | collective-permute-start | bytes 811016 | tf_op jit(solution)/shard_map/ppermute | solution.py:344
  156.1 1.3 shard_map.154.dense_ref
  157.4 1.4 copy-done.5
  158.8 3.3 %collective-permute-done.13.rest_4_ = bf16[1056,128]{1,0:T(8,128)(2,1)} collective-permute-done((bf16[1056,128]{1,0:T(8,128)(2,1)S(1)}, bf16[1056,128]{1,0:T(8,128)(2,1)}, u32[]{:S(2)}, u32[]{:S(2)}) %collective-permute-start.13) | collective-permute-done | bytes 270368 | tf_op jit(solution)/shard_map/ppermute | solution.py:343
  162.1 2.9 collective-permute-start.16
  165.0 3.0 %collective-permute-start.15 = (bf16[1056,128]{1,0:T(8,128)(2,1)}, bf16[1056,128]{1,0:T(8,128)(2,1)S(1)}, u32[]{:S(2)}, u32[]{:S(2)}) collective-permute-start(bf16[1056,128]{1,0:T(8,128)(2,1)} %collective-permute-done.13.rest_4_), channel_id=1, source_target_pairs={{0,1},{1,2},{2,3},{3,4},{4,5},{5,6},{6,7},{7,0},{8,9},{9,10},{10,1... | collective-permute-start | bytes 811016 | tf_op jit(solution)/shard_map/ppermute | solution.py:343
  168.9 4.1 %collective-permute-done.16.rest_7_ = bf16[1056,128]{1,0:T(8,128)(2,1)S(1)} collective-permute-done((bf16[1056,128]{1,0:T(8,128)(2,1)}, bf16[1056,128]{1,0:T(8,128)(2,1)S(1)}, u32[]{:S(2)}, u32[]{:S(2)}) %collective-permute-start.16) | collective-permute-done | bytes 270368 | tf_op jit(solution)/shard_map/ppermute | solution.py:344
  172.9 1.9 collective-permute-done.15.rest_6_
  174.8 1.9 collective-permute-start.17
  176.7 8.2 %collective-permute-start.18 = (bf16[256,128]{1,0:T(8,128)(2,1)S(1)}, bf16[256,128]{1,0:T(8,128)(2,1)S(1)}, u32[]{:S(2)}, u32[]{:S(2)}) collective-permute-start(bf16[256,128]{1,0:T(8,128)(2,1)S(1)} %slice.13), channel_id=1, source_target_pairs={{0,8},{1,9},{2,10},{3,11},{4,12},{5,13},{6,14},{7,15},{8,0},{9,1},... | collective-permute-start | bytes 196616 | tf_op jit(solution)/shard_map/ppermute | solution.py:351
  184.9 4.3 %collective-permute-done.18.other_ref = bf16[256,128]{1,0:T(8,128)(2,1)S(1)} collective-permute-done((bf16[256,128]{1,0:T(8,128)(2,1)S(1)}, bf16[256,128]{1,0:T(8,128)(2,1)S(1)}, u32[]{:S(2)}, u32[]{:S(2)}) %collective-permute-start.18) | collective-permute-done | bytes 65568 | tf_op jit(solution)/shard_map/ppermute | solution.py:351
  194.0 2.1 shard_map.156.rest_9_
  196.1 2.0 collective-permute-start.19
  200.7 2.7 shard_map.157
  204.2 2.3 shard_map.160
  206.5 7.5 %collective-permute-start.20 = (bf16[528,128]{1,0:T(8,128)(2,1)S(1)}, bf16[528,128]{1,0:T(8,128)(2,1)S(1)}, u32[]{:S(2)}, u32[]{:S(2)}) collective-permute-start(bf16[528,128]{1,0:T(8,128)(2,1)S(1)} %shard_map.158.own.users_ref), channel_id=1, source_target_pairs={{0,8},{1,9},{2,10},{3,11},{4,12},{5,13},{6,14},{7,15},{8,0},{9,1},... | collective-permute-start | bytes 405512 | tf_op jit(solution)/shard_map/ppermute | solution.py:332
  214.0 7.6 %collective-permute-done.20.other = bf16[528,128]{1,0:T(8,128)(2,1)S(1)} collective-permute-done((bf16[528,128]{1,0:T(8,128)(2,1)S(1)}, bf16[528,128]{1,0:T(8,128)(2,1)S(1)}, u32[]{:S(2)}, u32[]{:S(2)}) %collective-permute-start.20) | collective-permute-done | bytes 135200 | tf_op jit(solution)/shard_map/ppermute | solution.py:332
  221.6 2.8 collective-permute-start.22
  224.4 3.1 %collective-permute-start.21 = (bf16[1056,128]{1,0:T(8,128)(2,1)S(1)}, bf16[1056,128]{1,0:T(8,128)(2,1)S(1)}, u32[]{:S(2)}, u32[]{:S(2)}) collective-permute-start(bf16[1056,128]{1,0:T(8,128)(2,1)S(1)} %shard_map.159.rest_1_), channel_id=1, source_target_pairs={{0,1},{1,2},{2,3},{3,4},{4,5},{5,6},{6,7},{7,0},{8,9},{9,10},{10,1... | collective-permute-start | bytes 811016 | tf_op jit(solution)/shard_map/ppermute | solution.py:343
  227.5 7.3 %collective-permute-done.22.rest_3_ = bf16[1056,128]{1,0:T(8,128)(2,1)S(1)} collective-permute-done((bf16[1056,128]{1,0:T(8,128)(2,1)S(1)}, bf16[1056,128]{1,0:T(8,128)(2,1)S(1)}, u32[]{:S(2)}, u32[]{:S(2)}) %collective-permute-start.22) | collective-permute-done | bytes 270368 | tf_op jit(solution)/shard_map/ppermute | solution.py:344
  234.8 3.4 %collective-permute-start.24 = (bf16[1056,128]{1,0:T(8,128)(2,1)S(1)}, bf16[1056,128]{1,0:T(8,128)(2,1)}, u32[]{:S(2)}, u32[]{:S(2)}) collective-permute-start(bf16[1056,128]{1,0:T(8,128)(2,1)S(1)} %collective-permute-done.22.rest_3_), channel_id=1, source_target_pairs={{0,7},{1,0},{2,1},{3,2},{4,3},{5,4},{6,5},{7,6},{8,15},{9,8},{10,9... | collective-permute-start | bytes 811016 | tf_op jit(solution)/shard_map/ppermute | solution.py:344
  238.3 2.4 collective-permute-start.23
  240.7 6.4 %collective-permute-done.24.rest_5_ = bf16[1056,128]{1,0:T(8,128)(2,1)} collective-permute-done((bf16[1056,128]{1,0:T(8,128)(2,1)S(1)}, bf16[1056,128]{1,0:T(8,128)(2,1)}, u32[]{:S(2)}, u32[]{:S(2)}) %collective-permute-start.24) | collective-permute-done | bytes 270368 | tf_op jit(solution)/shard_map/ppermute | solution.py:344
  247.1 4.0 %collective-permute-start.26 = (bf16[1056,128]{1,0:T(8,128)(2,1)}, bf16[1056,128]{1,0:T(8,128)(2,1)}, u32[]{:S(2)}, u32[]{:S(2)}) collective-permute-start(bf16[1056,128]{1,0:T(8,128)(2,1)} %collective-permute-done.24.rest_5_), channel_id=1, source_target_pairs={{0,7},{1,0},{2,1},{3,2},{4,3},{5,4},{6,5},{7,6},{8,15},{9,8},{10,9... | collective-permute-start | bytes 811016 | tf_op jit(solution)/shard_map/ppermute | solution.py:344
  251.1 2.0 collective-permute-start.25
  254.0 4.1 %collective-permute-done.26.rest_7_ = bf16[1056,128]{1,0:T(8,128)(2,1)} collective-permute-done((bf16[1056,128]{1,0:T(8,128)(2,1)}, bf16[1056,128]{1,0:T(8,128)(2,1)}, u32[]{:S(2)}, u32[]{:S(2)}) %collective-permute-start.26) | collective-permute-done | bytes 270368 | tf_op jit(solution)/shard_map/ppermute | solution.py:344
  258.1 2.9 %collective-permute-done.25.rest_6_ = bf16[1056,128]{1,0:T(8,128)(2,1)} collective-permute-done((bf16[1056,128]{1,0:T(8,128)(2,1)}, bf16[1056,128]{1,0:T(8,128)(2,1)}, u32[]{:S(2)}, u32[]{:S(2)}) %collective-permute-start.25) | collective-permute-done | bytes 270368 | tf_op jit(solution)/shard_map/ppermute | solution.py:343
  261.0 2.9 collective-permute-start.27
  263.8 8.1 %collective-permute-start.28 = (bf16[256,128]{1,0:T(8,128)(2,1)S(1)}, bf16[256,128]{1,0:T(8,128)(2,1)S(1)}, u32[]{:S(2)}, u32[]{:S(2)}) collective-permute-start(bf16[256,128]{1,0:T(8,128)(2,1)S(1)} %slice.14), channel_id=1, source_target_pairs={{0,8},{1,9},{2,10},{3,11},{4,12},{5,13},{6,14},{7,15},{8,0},{9,1},... | collective-permute-start | bytes 196616 | tf_op jit(solution)/shard_map/ppermute | solution.py:351
  272.9 3.5 %shard_map.161 = (f32[256,128]{1,0:T(8,128)}, f32[256,128]{1,0:T(8,128)}, f32[256,128]{1,0:T(8,128)}) custom-call(s32[2]{0:T(128)S(1)} %pad_add_fusion.me_ref, f32[192]{0:T(256)S(1)} %copy-done.60, bf16[8192,128]{1,0:T(8,128)(2,1)S(1)} %copy-done.7, bf16[48,128]{1,0:T(8,128)(2,1)S(1)} %get-tuple-element.29.rows_ref, f32[768,128]{1,0:T(8,128)S(1)} %copy-done.43, ...), custom_call_target="tpu_custom_call" | custom-call | flops 536870912 | bytes 5242880 | tf_op jit(solution)/shard_map/pallas_call | solution.py:234
  276.4 2.9 %shard_map.162 = (f32[256,128]{1,0:T(8,128)}, f32[256,128]{1,0:T(8,128)}, f32[256,128]{1,0:T(8,128)}) custom-call(s32[2]{0:T(128)S(1)} %pad_add_fusion.me_ref, bf16[512,128]{1,0:T(8,128)(2,1)S(1)} %copy-done.44, bf16[256,128]{1,0:T(8,128)(2,1)S(1)} %collective-permute-done.28.other_ref, f32[768,128]{1,0:T(8,128)S(1)} %collective-permute-done.19.state.rest_0_, ...), custom_call_target="tpu_custom_call" | custom-call | flops 134217728 | bytes 4194304 | tf_op jit(solution)/shard_map/pallas_call | solution.py:283
  (157 shorter events, 35.2 us)
Async XLA Ops:
  7.2 68.1 %reduce-scatter.4.cloned.1.call-start = ((), (), s32[]{:S(2)}) async-start(), calls=%async_computation.3 | async-start | bytes 1179648 | tf_op jit(solution)/shard_map/reduce_scatter | solution.py:333
  8.0 6.8 %copy-start.51 = (s32[108]{0:T(128)}, s32[108]{0:T(128)S(1)}, u32[]{:S(2)}) copy-start(s32[108]{0:T(128)S(1)} %reshape.21.users_at) | copy-start | bytes 1300
  8.8 6.0 %copy-start.54 = (s32[108]{0:T(128)}, s32[108]{0:T(128)S(1)}, u32[]{:S(2)}) copy-start(s32[108]{0:T(128)S(1)} %reshape.22.items_at) | copy-start | bytes 1300
  14.8 3.4 %copy-start.28 = (bf16[528,128]{1,0:T(8,128)(2,1)}, bf16[528,128]{1,0:T(8,128)(2,1)S(1)}, u32[]{:S(2)}) copy-start(bf16[528,128]{1,0:T(8,128)(2,1)S(1)} %get-tuple-element.28.rest_0_.own.users_ref) | copy-start | bytes 405508
  14.8 2.1 copy-start
  18.2 43.6 %copy-start.1 = (bf16[1,1,3,36,128,128]{5,4,3,2,1,0:T(8,128)(2,1)S(1)}, bf16[1,1,3,36,128,128]{5,4,3,2,1,0:T(8,128)(2,1)}, u32[]{:S(2)}) copy-start(bf16[1,1,3,36,128,128]{5,4,3,2,1,0:T(8,128)(2,1)} %ratings.5) | copy-start | bytes 10616836
  19.6 1.4 copy-start.8
  20.9 1.0 copy-start.11
  21.9 146.1 %reduce-scatter.6.cloned.1.call-start = ((), (), s32[]{:S(2)}) async-start(), calls=%async_computation.4 | async-start | bytes 1179648 | tf_op jit(solution)/shard_map/reduce_scatter | solution.py:333
  22.0 15.1 %collective-permute-start = (bf16[528,128]{1,0:T(8,128)(2,1)}, bf16[528,128]{1,0:T(8,128)(2,1)S(1)}, u32[]{:S(2)}, u32[]{:S(2)}) collective-permute-start(bf16[528,128]{1,0:T(8,128)(2,1)} %copy-done.28), channel_id=1, source_target_pairs={{0,8},{1,9},{2,10},{3,11},{4,12},{5,13},{6,14},{7,15},{8,0},{9,1},... | collective-permute-start | bytes 405512 | tf_op jit(solution)/shard_map/ppermute | solution.py:332
  38.0 13.9 %collective-permute-start.1 = (bf16[1056,128]{1,0:T(8,128)(2,1)S(1)}, bf16[1056,128]{1,0:T(8,128)(2,1)S(1)}, u32[]{:S(2)}, u32[]{:S(2)}) collective-permute-start(bf16[1056,128]{1,0:T(8,128)(2,1)S(1)} %shard_map.147.rest_3_), channel_id=1, source_target_pairs={{0,1},{1,2},{2,3},{3,4},{4,5},{5,6},{6,7},{7,0},{8,9},{9,10},{10,1... | collective-permute-start | bytes 811016 | tf_op jit(solution)/shard_map/ppermute | solution.py:343
  41.5 12.3 %collective-permute-start.2 = (bf16[1056,128]{1,0:T(8,128)(2,1)S(1)}, bf16[1056,128]{1,0:T(8,128)(2,1)S(1)}, u32[]{:S(2)}, u32[]{:S(2)}) collective-permute-start(bf16[1056,128]{1,0:T(8,128)(2,1)S(1)} %shard_map.147.rest_3_), channel_id=1, source_target_pairs={{0,7},{1,0},{2,1},{3,2},{4,3},{5,4},{6,5},{7,6},{8,15},{9,8},{10,9... | collective-permute-start | bytes 811016 | tf_op jit(solution)/shard_map/ppermute | solution.py:344
  51.9 13.6 %copy-start.15 = (bf16[1056,128]{1,0:T(8,128)(2,1)}, bf16[1056,128]{1,0:T(8,128)(2,1)S(1)}, u32[]{:S(2)}) copy-start(bf16[1056,128]{1,0:T(8,128)(2,1)S(1)} %collective-permute-done.1.rest_0_.rest_4_) | copy-start | bytes 811012
  51.9 17.5 %collective-permute-start.3 = (bf16[1056,128]{1,0:T(8,128)(2,1)S(1)}, bf16[1056,128]{1,0:T(8,128)(2,1)}, u32[]{:S(2)}, u32[]{:S(2)}) collective-permute-start(bf16[1056,128]{1,0:T(8,128)(2,1)S(1)} %collective-permute-done.1.rest_0_.rest_4_), channel_id=1, source_target_pairs={{0,1},{1,2},{2,3},{3,4},{4,5},{5,6},{6,7},{7,0},{8,9},{9,10},{10,1... | collective-permute-start | bytes 811016 | tf_op jit(solution)/shard_map/ppermute | solution.py:343
  53.8 11.7 %copy-start.33 = (bf16[1056,128]{1,0:T(8,128)(2,1)}, bf16[1056,128]{1,0:T(8,128)(2,1)S(1)}, u32[]{:S(2)}) copy-start(bf16[1056,128]{1,0:T(8,128)(2,1)S(1)} %collective-permute-done.2.rest_5_) | copy-start | bytes 811012
  53.8 15.6 %collective-permute-start.4 = (bf16[1056,128]{1,0:T(8,128)(2,1)S(1)}, bf16[1056,128]{1,0:T(8,128)(2,1)}, u32[]{:S(2)}, u32[]{:S(2)}) collective-permute-start(bf16[1056,128]{1,0:T(8,128)(2,1)S(1)} %collective-permute-done.2.rest_5_), channel_id=1, source_target_pairs={{0,7},{1,0},{2,1},{3,2},{4,3},{5,4},{6,5},{7,6},{8,15},{9,8},{10,9... | collective-permute-start | bytes 811016 | tf_op jit(solution)/shard_map/ppermute | solution.py:344
  65.5 1.3 copy-start.2
  69.4 10.9 %collective-permute-start.6 = (bf16[1056,128]{1,0:T(8,128)(2,1)}, bf16[1056,128]{1,0:T(8,128)(2,1)}, u32[]{:S(2)}, u32[]{:S(2)}) collective-permute-start(bf16[1056,128]{1,0:T(8,128)(2,1)} %collective-permute-done.4.rest_7_), channel_id=1, source_target_pairs={{0,7},{1,0},{2,1},{3,2},{4,3},{5,4},{6,5},{7,6},{8,15},{9,8},{10,9... | collective-permute-start | bytes 811016 | tf_op jit(solution)/shard_map/ppermute | solution.py:344
  72.4 9.9 %collective-permute-start.5 = (bf16[1056,128]{1,0:T(8,128)(2,1)}, bf16[1056,128]{1,0:T(8,128)(2,1)}, u32[]{:S(2)}, u32[]{:S(2)}) collective-permute-start(bf16[1056,128]{1,0:T(8,128)(2,1)} %collective-permute-done.3.rest_6_), channel_id=1, source_target_pairs={{0,1},{1,2},{2,3},{3,4},{4,5},{5,6},{6,7},{7,0},{8,9},{9,10},{10,1... | collective-permute-start | bytes 811016 | tf_op jit(solution)/shard_map/ppermute | solution.py:343
  75.3 33.5 %copy-start.9 = (bf16[8192,128]{1,0:T(8,128)(2,1)S(1)}, bf16[8192,128]{1,0:T(8,128)(2,1)}, u32[]{:S(2)}) copy-start(bf16[8192,128]{1,0:T(8,128)(2,1)} %copy-done.8) | copy-start | bytes 6291460
  82.3 13.5 %collective-permute-start.7 = (bf16[1056,128]{1,0:T(8,128)(2,1)}, bf16[1056,128]{1,0:T(8,128)(2,1)S(1)}, u32[]{:S(2)}, u32[]{:S(2)}) collective-permute-start(bf16[1056,128]{1,0:T(8,128)(2,1)} %collective-permute-done.5.rest_8_), channel_id=1, source_target_pairs={{0,1},{1,2},{2,3},{3,4},{4,5},{5,6},{6,7},{7,0},{8,9},{9,10},{10,1... | collective-permute-start | bytes 811016 | tf_op jit(solution)/shard_map/ppermute | solution.py:352
  84.2 11.6 %collective-permute-start.8 = (bf16[256,128]{1,0:T(8,128)(2,1)S(1)}, bf16[256,128]{1,0:T(8,128)(2,1)S(1)}, u32[]{:S(2)}, u32[]{:S(2)}) collective-permute-start(bf16[256,128]{1,0:T(8,128)(2,1)S(1)} %slice.12), channel_id=1, source_target_pairs={{0,8},{1,9},{2,10},{3,11},{4,12},{5,13},{6,14},{7,15},{8,0},{9,1},... | collective-permute-start | bytes 196616 | tf_op jit(solution)/shard_map/ppermute | solution.py:351
  95.8 1.0 copy-start.16
  102.3 6.5 %copy-start.17 = (bf16[1056,128]{1,0:T(8,128)(2,1)S(1)}, bf16[1056,128]{1,0:T(8,128)(2,1)}, u32[]{:S(2)}) copy-start(bf16[1056,128]{1,0:T(8,128)(2,1)} %copy-done.15) | copy-start | bytes 811012
  102.3 6.5 %copy-start.23 = (bf16[1056,128]{1,0:T(8,128)(2,1)S(1)}, bf16[1056,128]{1,0:T(8,128)(2,1)}, u32[]{:S(2)}) copy-start(bf16[1056,128]{1,0:T(8,128)(2,1)} %copy-done.21) | copy-start | bytes 811012
  102.3 6.5 %copy-start.35 = (bf16[1056,128]{1,0:T(8,128)(2,1)S(1)}, bf16[1056,128]{1,0:T(8,128)(2,1)}, u32[]{:S(2)}) copy-start(bf16[1056,128]{1,0:T(8,128)(2,1)} %copy-done.33) | copy-start | bytes 811012
  102.3 6.5 %copy-start.37 = (f32[256,128]{1,0:T(8,128)S(1)}, f32[256,128]{1,0:T(8,128)}, u32[]{:S(2)}) copy-start(f32[256,128]{1,0:T(8,128)} %rest_0_.3) | copy-start | bytes 393220
  102.3 6.5 %copy-start.47 = (f32[256,128]{1,0:T(8,128)S(1)}, f32[256,128]{1,0:T(8,128)}, u32[]{:S(2)}) copy-start(f32[256,128]{1,0:T(8,128)} %rest_1_.3) | copy-start | bytes 393220
  104.6 9.4 %collective-permute-start.9 = (f32[768,128]{1,0:T(8,128)S(1)}, f32[768,128]{1,0:T(8,128)S(1)}, u32[]{:S(2)}, u32[]{:S(2)}) collective-permute-start(f32[768,128]{1,0:T(8,128)S(1)} %shard_map.150.rest_11_), channel_id=1, source_target_pairs={{0,496},{16,0},{32,16},{48,32},{64,48},{80,64},{96,80},{112,96},{1... | collective-permute-start | bytes 1179656 | tf_op jit(solution)/shard_map/ppermute | solution.py:355
  110.4 4.4 %copy-start.3 = (bf16[8192,128]{1,0:T(8,128)(2,1)S(1)}, bf16[8192,128]{1,0:T(8,128)(2,1)}, u32[]{:S(2)}) copy-start(bf16[8192,128]{1,0:T(8,128)(2,1)} %copy-done.2) | copy-start | bytes 6291460
  116.2 1.0 copy-start.10
  117.8 135.3 %reduce-scatter.8.cloned.1.call-start = ((), (), s32[]{:S(2)}) async-start(), calls=%async_computation.5 | async-start | bytes 1179648 | tf_op jit(solution)/shard_map/reduce_scatter | solution.py:333
  117.9 13.5 %collective-permute-start.10 = (bf16[528,128]{1,0:T(8,128)(2,1)}, bf16[528,128]{1,0:T(8,128)(2,1)S(1)}, u32[]{:S(2)}, u32[]{:S(2)}) collective-permute-start(bf16[528,128]{1,0:T(8,128)(2,1)} %copy-done.26), channel_id=1, source_target_pairs={{0,8},{1,9},{2,10},{3,11},{4,12},{5,13},{6,14},{7,15},{8,0},{9,1},... | collective-permute-start | bytes 405512 | tf_op jit(solution)/shard_map/ppermute | solution.py:332
  132.3 14.7 %collective-permute-start.11 = (bf16[1056,128]{1,0:T(8,128)(2,1)S(1)}, bf16[1056,128]{1,0:T(8,128)(2,1)S(1)}, u32[]{:S(2)}, u32[]{:S(2)}) collective-permute-start(bf16[1056,128]{1,0:T(8,128)(2,1)S(1)} %shard_map.153.rest_1_), channel_id=1, source_target_pairs={{0,1},{1,2},{2,3},{3,4},{4,5},{5,6},{6,7},{7,0},{8,9},{9,10},{10,1... | collective-permute-start | bytes 811016 | tf_op jit(solution)/shard_map/ppermute | solution.py:343
  134.2 14.7 %collective-permute-start.12 = (bf16[1056,128]{1,0:T(8,128)(2,1)S(1)}, bf16[1056,128]{1,0:T(8,128)(2,1)S(1)}, u32[]{:S(2)}, u32[]{:S(2)}) collective-permute-start(bf16[1056,128]{1,0:T(8,128)(2,1)S(1)} %shard_map.153.rest_1_), channel_id=1, source_target_pairs={{0,7},{1,0},{2,1},{3,2},{4,3},{5,4},{6,5},{7,6},{8,15},{9,8},{10,9... | collective-permute-start | bytes 811016 | tf_op jit(solution)/shard_map/ppermute | solution.py:344
  147.0 10.4 %copy-start.12 = (bf16[1056,128]{1,0:T(8,128)(2,1)}, bf16[1056,128]{1,0:T(8,128)(2,1)S(1)}, u32[]{:S(2)}) copy-start(bf16[1056,128]{1,0:T(8,128)(2,1)S(1)} %collective-permute-done.11.rest_0_.rest_2_) | copy-start | bytes 811012
  147.0 15.1 %collective-permute-start.13 = (bf16[1056,128]{1,0:T(8,128)(2,1)S(1)}, bf16[1056,128]{1,0:T(8,128)(2,1)}, u32[]{:S(2)}, u32[]{:S(2)}) collective-permute-start(bf16[1056,128]{1,0:T(8,128)(2,1)S(1)} %collective-permute-done.11.rest_0_.rest_2_), channel_id=1, source_target_pairs={{0,1},{1,2},{2,3},{3,4},{4,5},{5,6},{6,7},{7,0},{8,9},{9,10},{10,1... | collective-permute-start | bytes 811016 | tf_op jit(solution)/shard_map/ppermute | solution.py:343
  149.0 8.5 %copy-start.30 = (bf16[1056,128]{1,0:T(8,128)(2,1)}, bf16[1056,128]{1,0:T(8,128)(2,1)S(1)}, u32[]{:S(2)}) copy-start(bf16[1056,128]{1,0:T(8,128)(2,1)S(1)} %collective-permute-done.12.rest_3_) | copy-start | bytes 811012
  149.0 13.2 %collective-permute-start.14 = (bf16[1056,128]{1,0:T(8,128)(2,1)S(1)}, bf16[1056,128]{1,0:T(8,128)(2,1)}, u32[]{:S(2)}, u32[]{:S(2)}) collective-permute-start(bf16[1056,128]{1,0:T(8,128)(2,1)S(1)} %collective-permute-done.12.rest_3_), channel_id=1, source_target_pairs={{0,7},{1,0},{2,1},{3,2},{4,3},{5,4},{6,5},{7,6},{8,15},{9,8},{10,9... | collective-permute-start | bytes 811016 | tf_op jit(solution)/shard_map/ppermute | solution.py:344
  157.4 1.4 copy-start.5
  158.8 39.3 %copy-start.4 = (bf16[8192,128]{1,0:T(8,128)(2,1)S(1)}, bf16[8192,128]{1,0:T(8,128)(2,1)}, u32[]{:S(2)}) copy-start(bf16[8192,128]{1,0:T(8,128)(2,1)} %copy-done.2) | copy-start | bytes 6291460
  162.1 10.8 %collective-permute-start.16 = (bf16[1056,128]{1,0:T(8,128)(2,1)}, bf16[1056,128]{1,0:T(8,128)(2,1)S(1)}, u32[]{:S(2)}, u32[]{:S(2)}) collective-permute-start(bf16[1056,128]{1,0:T(8,128)(2,1)} %collective-permute-done.14.rest_5_), channel_id=1, source_target_pairs={{0,7},{1,0},{2,1},{3,2},{4,3},{5,4},{6,5},{7,6},{8,15},{9,8},{10,9... | collective-permute-start | bytes 811016 | tf_op jit(solution)/shard_map/ppermute | solution.py:344
  165.0 9.8 %collective-permute-start.15 = (bf16[1056,128]{1,0:T(8,128)(2,1)}, bf16[1056,128]{1,0:T(8,128)(2,1)S(1)}, u32[]{:S(2)}, u32[]{:S(2)}) collective-permute-start(bf16[1056,128]{1,0:T(8,128)(2,1)} %collective-permute-done.13.rest_4_), channel_id=1, source_target_pairs={{0,1},{1,2},{2,3},{3,4},{4,5},{5,6},{6,7},{7,0},{8,9},{9,10},{10,1... | collective-permute-start | bytes 811016 | tf_op jit(solution)/shard_map/ppermute | solution.py:343
  174.8 14.4 %collective-permute-start.17 = (bf16[1056,128]{1,0:T(8,128)(2,1)S(1)}, bf16[1056,128]{1,0:T(8,128)(2,1)S(1)}, u32[]{:S(2)}, u32[]{:S(2)}) collective-permute-start(bf16[1056,128]{1,0:T(8,128)(2,1)S(1)} %collective-permute-done.15.rest_6_), channel_id=1, source_target_pairs={{0,1},{1,2},{2,3},{3,4},{4,5},{5,6},{6,7},{7,0},{8,9},{9,10},{10,1... | collective-permute-start | bytes 811016 | tf_op jit(solution)/shard_map/ppermute | solution.py:352
  176.7 12.5 %collective-permute-start.18 = (bf16[256,128]{1,0:T(8,128)(2,1)S(1)}, bf16[256,128]{1,0:T(8,128)(2,1)S(1)}, u32[]{:S(2)}, u32[]{:S(2)}) collective-permute-start(bf16[256,128]{1,0:T(8,128)(2,1)S(1)} %slice.13), channel_id=1, source_target_pairs={{0,8},{1,9},{2,10},{3,11},{4,12},{5,13},{6,14},{7,15},{8,0},{9,1},... | collective-permute-start | bytes 196616 | tf_op jit(solution)/shard_map/ppermute | solution.py:351
  191.1 1.0 copy-start.25
  194.0 4.1 %copy-start.14 = (bf16[1056,128]{1,0:T(8,128)(2,1)S(1)}, bf16[1056,128]{1,0:T(8,128)(2,1)}, u32[]{:S(2)}) copy-start(bf16[1056,128]{1,0:T(8,128)(2,1)} %copy-done.12) | copy-start | bytes 811012
  194.0 4.1 %copy-start.32 = (bf16[1056,128]{1,0:T(8,128)(2,1)S(1)}, bf16[1056,128]{1,0:T(8,128)(2,1)}, u32[]{:S(2)}) copy-start(bf16[1056,128]{1,0:T(8,128)(2,1)} %copy-done.30) | copy-start | bytes 811012
  196.1 8.1 %collective-permute-start.19 = (f32[768,128]{1,0:T(8,128)S(1)}, f32[768,128]{1,0:T(8,128)S(1)}, u32[]{:S(2)}, u32[]{:S(2)}) collective-permute-start(f32[768,128]{1,0:T(8,128)S(1)} %shard_map.156.rest_9_), channel_id=1, source_target_pairs={{0,496},{16,0},{32,16},{48,32},{64,48},{80,64},{96,80},{112,96},{1... | collective-permute-start | bytes 1179656 | tf_op jit(solution)/shard_map/ppermute | solution.py:355
  199.1 1.0 copy-start.41
  200.7 3.5 %copy-start.6 = (bf16[8192,128]{1,0:T(8,128)(2,1)S(1)}, bf16[8192,128]{1,0:T(8,128)(2,1)}, u32[]{:S(2)}) copy-start(bf16[8192,128]{1,0:T(8,128)(2,1)} %copy-done.5) | copy-start | bytes 6291460
  204.2 67.7 %copy-start.7 = (bf16[8192,128]{1,0:T(8,128)(2,1)S(1)}, bf16[8192,128]{1,0:T(8,128)(2,1)}, u32[]{:S(2)}) copy-start(bf16[8192,128]{1,0:T(8,128)(2,1)} %copy-done.5) | copy-start | bytes 6291460
  204.2 67.7 %copy-start.60 = (f32[192]{0:T(256)S(1)}, f32[192]{0:T(256)}, u32[]{:S(2)}) copy-start(f32[192]{0:T(256)} %copy-done.57) | copy-start | bytes 2308
  206.5 15.0 %collective-permute-start.20 = (bf16[528,128]{1,0:T(8,128)(2,1)S(1)}, bf16[528,128]{1,0:T(8,128)(2,1)S(1)}, u32[]{:S(2)}, u32[]{:S(2)}) collective-permute-start(bf16[528,128]{1,0:T(8,128)(2,1)S(1)} %shard_map.158.own.users_ref), channel_id=1, source_target_pairs={{0,8},{1,9},{2,10},{3,11},{4,12},{5,13},{6,14},{7,15},{8,0},{9,1},... | collective-permute-start | bytes 405512 | tf_op jit(solution)/shard_map/ppermute | solution.py:332
  221.6 13.2 %collective-permute-start.22 = (bf16[1056,128]{1,0:T(8,128)(2,1)S(1)}, bf16[1056,128]{1,0:T(8,128)(2,1)S(1)}, u32[]{:S(2)}, u32[]{:S(2)}) collective-permute-start(bf16[1056,128]{1,0:T(8,128)(2,1)S(1)} %shard_map.159.rest_1_), channel_id=1, source_target_pairs={{0,7},{1,0},{2,1},{3,2},{4,3},{5,4},{6,5},{7,6},{8,15},{9,8},{10,9... | collective-permute-start | bytes 811016 | tf_op jit(solution)/shard_map/ppermute | solution.py:344
  224.4 13.9 %collective-permute-start.21 = (bf16[1056,128]{1,0:T(8,128)(2,1)S(1)}, bf16[1056,128]{1,0:T(8,128)(2,1)S(1)}, u32[]{:S(2)}, u32[]{:S(2)}) collective-permute-start(bf16[1056,128]{1,0:T(8,128)(2,1)S(1)} %shard_map.159.rest_1_), channel_id=1, source_target_pairs={{0,1},{1,2},{2,3},{3,4},{4,5},{5,6},{6,7},{7,0},{8,9},{9,10},{10,1... | collective-permute-start | bytes 811016 | tf_op jit(solution)/shard_map/ppermute | solution.py:343
  234.8 12.3 %collective-permute-start.24 = (bf16[1056,128]{1,0:T(8,128)(2,1)S(1)}, bf16[1056,128]{1,0:T(8,128)(2,1)}, u32[]{:S(2)}, u32[]{:S(2)}) collective-permute-start(bf16[1056,128]{1,0:T(8,128)(2,1)S(1)} %collective-permute-done.22.rest_3_), channel_id=1, source_target_pairs={{0,7},{1,0},{2,1},{3,2},{4,3},{5,4},{6,5},{7,6},{8,15},{9,8},{10,9... | collective-permute-start | bytes 811016 | tf_op jit(solution)/shard_map/ppermute | solution.py:344
  238.3 12.8 %collective-permute-start.23 = (bf16[1056,128]{1,0:T(8,128)(2,1)S(1)}, bf16[1056,128]{1,0:T(8,128)(2,1)}, u32[]{:S(2)}, u32[]{:S(2)}) collective-permute-start(bf16[1056,128]{1,0:T(8,128)(2,1)S(1)} %collective-permute-done.21.rest_2_), channel_id=1, source_target_pairs={{0,1},{1,2},{2,3},{3,4},{4,5},{5,6},{6,7},{7,0},{8,9},{9,10},{10,1... | collective-permute-start | bytes 811016 | tf_op jit(solution)/shard_map/ppermute | solution.py:343
  247.1 11.0 %collective-permute-start.26 = (bf16[1056,128]{1,0:T(8,128)(2,1)}, bf16[1056,128]{1,0:T(8,128)(2,1)}, u32[]{:S(2)}, u32[]{:S(2)}) collective-permute-start(bf16[1056,128]{1,0:T(8,128)(2,1)} %collective-permute-done.24.rest_5_), channel_id=1, source_target_pairs={{0,7},{1,0},{2,1},{3,2},{4,3},{5,4},{6,5},{7,6},{8,15},{9,8},{10,9... | collective-permute-start | bytes 811016 | tf_op jit(solution)/shard_map/ppermute | solution.py:344
  251.1 9.9 %collective-permute-start.25 = (bf16[1056,128]{1,0:T(8,128)(2,1)}, bf16[1056,128]{1,0:T(8,128)(2,1)}, u32[]{:S(2)}, u32[]{:S(2)}) collective-permute-start(bf16[1056,128]{1,0:T(8,128)(2,1)} %collective-permute-done.23.rest_4_), channel_id=1, source_target_pairs={{0,1},{1,2},{2,3},{3,4},{4,5},{5,6},{6,7},{7,0},{8,9},{9,10},{10,1... | collective-permute-start | bytes 811016 | tf_op jit(solution)/shard_map/ppermute | solution.py:343
  261.0 11.0 %collective-permute-start.27 = (bf16[1056,128]{1,0:T(8,128)(2,1)}, bf16[1056,128]{1,0:T(8,128)(2,1)S(1)}, u32[]{:S(2)}, u32[]{:S(2)}) collective-permute-start(bf16[1056,128]{1,0:T(8,128)(2,1)} %collective-permute-done.25.rest_6_), channel_id=1, source_target_pairs={{0,1},{1,2},{2,3},{3,4},{4,5},{5,6},{6,7},{7,0},{8,9},{9,10},{10,1... | collective-permute-start | bytes 811016 | tf_op jit(solution)/shard_map/ppermute | solution.py:352
  263.8 12.6 %collective-permute-start.28 = (bf16[256,128]{1,0:T(8,128)(2,1)S(1)}, bf16[256,128]{1,0:T(8,128)(2,1)S(1)}, u32[]{:S(2)}, u32[]{:S(2)}) collective-permute-start(bf16[256,128]{1,0:T(8,128)(2,1)S(1)} %slice.14), channel_id=1, source_target_pairs={{0,8},{1,9},{2,10},{3,11},{4,12},{5,13},{6,14},{7,15},{8,0},{9,1},... | collective-permute-start | bytes 196616 | tf_op jit(solution)/shard_map/ppermute | solution.py:351
  271.9 1.0 copy-start.43
  272.9 3.5 %copy-start.44 = (bf16[512,128]{1,0:T(8,128)(2,1)S(1)}, bf16[512,128]{1,0:T(8,128)(2,1)}, u32[]{:S(2)}) copy-start(bf16[512,128]{1,0:T(8,128)(2,1)} %reduce-scatter.8.cloned.1.call-done.own_ref) | copy-start | bytes 393220
  (32 other events, 25.6 us)
Sparse Core Ops, SparseCore 0:
  22.1 48.1 reduce-scatter.3
  117.9 45.8 reduce-scatter.5
  206.7 43.3 reduce-scatter.7

commit v6 on v5

--- a/solution.py
+++ b/solution.py
@@ -124,15 +124,17 @@
     return kernel_call(joined_body, shape(PART + ITEM_ROWS, BF16), [VMEM, VMEM])(part, state)
 
 
-def packed_body(own, other, out):
-    out[:ITEM_ROWS] = own[PART:]
-    out[ITEM_ROWS : 2 * ITEM_ROWS] = other[PART:]
-    out[2 * ITEM_ROWS : 2 * ITEM_ROWS + PART] = own[:PART]
-    out[2 * ITEM_ROWS + PART :] = other[:PART]
-
-
-def packed(own, other):
-    return kernel_call(packed_body, shape(2 * (ITEM_ROWS + PART), BF16), [VMEM, VMEM])(own, other)
+def packed_body(me_ref, both, out):
+    plane = me_ref[0] // RING
+    for swap in range(2):
+        top = pl.multiple_of((1 - plane if swap else plane) * (PART + ITEM_ROWS), 16)
+        out[swap * ITEM_ROWS : (swap + 1) * ITEM_ROWS] = both[pl.ds(top + PART, ITEM_ROWS)]
+        users = 2 * ITEM_ROWS + swap * PART
+        out[users : users + PART] = both[pl.ds(top, PART)]
+
+
+def packed(me, both):
+    return kernel_call(packed_body, shape(2 * (ITEM_ROWS + PART), BF16), [SMEM, VMEM])(me, both)
 
 
 def dense_body(s, users_at, items_at, live, ratings, *rest):
@@ -240,7 +242,7 @@
     )(me, counts, dense, rows, *state, *pieces, *later)
 
 
-def item_body(s, states, me_ref, own_ref, other_ref, *rest):
+def item_body(s, states, me_ref, sums_ref, *rest):
     state_refs, pieces = rest[:states], rest[states : states + len(DISTANCES)]
     outs = rest[states + len(DISTANCES) :]
     lane = lax.broadcasted_iota(jnp.int32, (COUNT_ROWS, K), 1)
@@ -269,24 +271,28 @@
             jnp.dot(mine, high, preferred_element_type=F32)
             + jnp.dot(mine, low, preferred_element_type=F32)
         )
+    plane = me_ref[0] // RING
+    mine_at = pl.multiple_of(plane * 2 * ITEM_ROWS, ITEM_ROWS)
+    other_at = pl.multiple_of((1 - plane) * 2 * ITEM_ROWS + ITEM_ROWS, ITEM_ROWS)
     total = jnp.concatenate(parts, axis=0) - (
-        own_ref[:ITEM_ROWS].astype(F32) + other_ref[...].astype(F32)
+        sums_ref[pl.ds(mine_at, ITEM_ROWS)].astype(F32)
+        + sums_ref[pl.ds(other_at, ITEM_ROWS)].astype(F32)
     )
     grad = GRAD_SCALE * total + DECAY_REG * fac
     fac, first, second = adam_update(fac, first, second, grad)
     stored(outs, (fac, first, second))
 
 
-def item_step(s, me, own, other, state, pieces):
+def item_step(s, me, sums, state, pieces):
     last = s + 1 == STEPS
     outs = [shape(ITEM_ROWS)] * 3 if last else [shape(3 * ITEM_ROWS)]
     return kernel_call(
         functools.partial(item_body, s, len(state)),
         outs,
-        [SMEM] + [VMEM] * (2 + len(state) + len(pieces)),
+        [SMEM] + [VMEM] * (1 + len(state) + len(pieces)),
         flops=2 * 32 * TILE * K * K,
         moved=4 << 20,
-    )(me, own, other, *state, *pieces)
+    )(me, sums, *state, *pieces)
 
 
 def after(value, *others):
@@ -316,7 +322,11 @@
         ]
 
     forward, backward = ring_route(1), ring_route(-1)
-    across = [(n, (n + RING) % (2 * RING)) for n in range(2 * RING)]
+    facing = [[y, y + RING] for y in range(RING)]
+
+    def both_planes(rows):
+        return lax.all_gather(rows, "narrow", axis=0, tiled=True, axis_index_groups=facing)
+
     rings = [[z * RING + y for y in range(RING)] for z in range(2)]
 
     earlier = [(b, (b - 1) % strata) for b in range(strata)]
@@ -329,7 +339,7 @@
     user_state = (user_factors, user_m, user_v)
     item_state = (item_factors, item_m, item_v)
     for s in range(STEPS):
-        load = packed(first, lax.ppermute(first, "narrow", across))
+        load = packed(me, both_planes(first))
         partial = lax.psum_scatter(
             rating_part(me, first, dense),
             "narrow",
@@ -347,10 +357,9 @@
                 dense_next = dense_ratings(s + 1, users_at, items_at, live, ratings, pieces[1])
                 up = after(up, dense_next)
             if step == 2:
-                ready = after(partial[ITEM_ROWS:], up, down)
-                other = lax.ppermute(ready, "narrow", across)
-        pieces.append(lax.ppermute(after(up, ready), ("blk", "narrow"), forward))
-        item_state = item_step(s, me, partial, other, item_state, pieces)
+                sums = both_planes(after(partial, up, down))
+        pieces.append(lax.ppermute(up, ("blk", "narrow"), forward))
+        item_state = item_step(s, me, sums, item_state, pieces)
         if s + 1 < STEPS:
             moved = lax.ppermute(item_state[0], "blk", earlier)
             part, *user_state = user_step(

time: 290 us -> 301 us (1.038)
  blocking collectives: 0 us -> 75.8 us
  starting transfers between devices: 124 us -> 83.2 us
  waiting for transfers between devices: 77.5 us -> 44.6 us
  local copies, waits for them, and re-layouts: 39.7 us -> 52.5 us
    all_gather x0 -> x6, blocking collectives: none -> 75.8 us  [both_planes(): lax.all_gather(rows, 'narrow', axis=0, tiled=True, axis_index_groups=facing)]
    ppermute x9 -> x3, starting transfers between devices: 57.5 us -> 5.73 us  [per_device(): pieces.append(lax.ppermute(up, ('blk', 'narrow'), forward))]
    ppermute x9, waiting for transfers between devices: 25.9 us -> 0.97 us  [per_device(): down = lax.ppermute(down, ('blk', 'narrow'), backward)]
    ppermute x9 -> x3, waiting for transfers between devices: 25 us -> 7.63 us  [per_device(): pieces.append(lax.ppermute(up, ('blk', 'narrow'), forward))]
    unnamed x128 -> x168, local copies, waits for them, and re-layouts: 36.8 us -> 52.3 us
    ppermute x9, starting transfers between devices: 37.8 us -> 51.2 us  [per_device(): down = lax.ppermute(down, ('blk', 'narrow'), backward)]
    ppermute x9, waiting for transfers between devices: 25.8 us -> 35.9 us  [per_device(): up = lax.ppermute(up, ('blk', 'narrow'), forward)]
  transfers between devices with their start and end apart: 32 -> 26, of which waited for: 18 -> 14; matrix products, arithmetic and copies ran while one was open for 1% -> 0% of each run, Pallas kernels for 4% -> 4%
where the time goes in v6:
time: 301 us; the launch traced here: 299 us
  starting transfers between devices  83.2 us (28%)
  blocking collectives  75.8 us (25%)
  local copies, waits for them, and re-layouts  52.5 us (17%)
  waiting for transfers between devices  44.6 us (15%)
  Pallas kernels  26.9 us (9%)
  between operations  14.5 us (5%)
    all_gather x6, blocking collectives, both_planes(): lax.all_gather(rows, 'narrow', axis=0, tiled=True, axis_index_groups=facing)  75.8 us
    unnamed x168, local copies, waits for them, and re-layouts  52.3 us
    ppermute x9, starting transfers between devices, per_device(): down = lax.ppermute(down, ('blk', 'narrow'), backward)  51.2 us
    ppermute x9, waiting for transfers between devices, per_device(): up = lax.ppermute(up, ('blk', 'narrow'), forward)  35.9 us
    ppermute x9, starting transfers between devices, per_device(): up = lax.ppermute(up, ('blk', 'narrow'), forward)  22.2 us
    ppermute x3, waiting for transfers between devices, per_device(): pieces.append(lax.ppermute(up, ('blk', 'narrow'), forward))  7.63 us
    pallas_call x3, Pallas kernels, user_step(): kernel_call(functools.partial(user_body, s, len(state)), outs, [SMEM, SME...  7.54 us
  transfers between devices with their start and end apart: 26, of which 14 were waited for; matrix products, arithmetic and copies ran while one was open for 0% of the time, Pallas kernels for 4%

profile of v6, /device:TPU:6, one launch (start us, length us, event | category | flops | bytes accessed | tf_op | source)
XLA Modules:
  0.0 298.9 jit_solution(11965458944352125180)
XLA Ops:
  11.3 2.6 shard_map.145
  14.6 2.0 copy-done
  16.6 1.3 shard_map.146.dense_ref
  18.0 1.3 shard_map.149
  19.3 1.3 copy-done.8
  20.6 1.0 copy-done.11
  21.7 13.8 %all_gather.18.both = bf16[1056,128]{1,0:T(8,128)(2,1)S(1)} all-gather(bf16[528,128]{1,0:T(8,128)(2,1)} %copy-done.27), channel_id=1, replica_groups={{0,8},{1,9},{2,10},{3,11},{4,12},{5,13},{6,14},{7,15},{16,24},{17,25},{..., dimensions={0}, use_global_device_ids=true | all-gather | bytes 405504 | tf_op jit(solution)/shard_map/all_gather | solution.py:328
  36.0 3.6 %collective-permute-start = (bf16[1056,128]{1,0:T(8,128)(2,1)S(1)}, bf16[1056,128]{1,0:T(8,128)(2,1)S(1)}, u32[]{:S(2)}, u32[]{:S(2)}) collective-permute-start(bf16[1056,128]{1,0:T(8,128)(2,1)S(1)} %shard_map.147.rest_3_), channel_id=1, source_target_pairs={{0,1},{1,2},{2,3},{3,4},{4,5},{5,6},{6,7},{7,0},{8,9},{9,10},{10,1... | collective-permute-start | bytes 811016 | tf_op jit(solution)/shard_map/ppermute | solution.py:353
  39.6 4.3 %collective-permute-start.1 = (bf16[1056,128]{1,0:T(8,128)(2,1)S(1)}, bf16[1056,128]{1,0:T(8,128)(2,1)S(1)}, u32[]{:S(2)}, u32[]{:S(2)}) collective-permute-start(bf16[1056,128]{1,0:T(8,128)(2,1)S(1)} %shard_map.147.rest_3_), channel_id=1, source_target_pairs={{0,7},{1,0},{2,1},{3,2},{4,3},{5,4},{6,5},{7,6},{8,15},{9,8},{10,9... | collective-permute-start | bytes 811016 | tf_op jit(solution)/shard_map/ppermute | solution.py:354
  44.7 4.1 %collective-permute-done.rest_0_.rest_4_ = bf16[1056,128]{1,0:T(8,128)(2,1)S(1)} collective-permute-done((bf16[1056,128]{1,0:T(8,128)(2,1)S(1)}, bf16[1056,128]{1,0:T(8,128)(2,1)S(1)}, u32[]{:S(2)}, u32[]{:S(2)}) %collective-permute-start) | collective-permute-done | bytes 270368 | tf_op jit(solution)/shard_map/ppermute | solution.py:353
  48.8 4.3 %collective-permute-start.2 = (bf16[1056,128]{1,0:T(8,128)(2,1)S(1)}, bf16[1056,128]{1,0:T(8,128)(2,1)S(1)}, u32[]{:S(2)}, u32[]{:S(2)}) collective-permute-start(bf16[1056,128]{1,0:T(8,128)(2,1)S(1)} %collective-permute-done.rest_0_.rest_4_), channel_id=1, source_target_pairs={{0,1},{1,2},{2,3},{3,4},{4,5},{5,6},{6,7},{7,0},{8,9},{9,10},{10,1... | collective-permute-start | bytes 811016 | tf_op jit(solution)/shard_map/ppermute | solution.py:353
  53.2 5.0 %collective-permute-start.3 = (bf16[1056,128]{1,0:T(8,128)(2,1)S(1)}, bf16[1056,128]{1,0:T(8,128)(2,1)S(1)}, u32[]{:S(2)}, u32[]{:S(2)}) collective-permute-start(bf16[1056,128]{1,0:T(8,128)(2,1)S(1)} %collective-permute-done.1.rest_5_), channel_id=1, source_target_pairs={{0,7},{1,0},{2,1},{3,2},{4,3},{5,4},{6,5},{7,6},{8,15},{9,8},{10,9... | collective-permute-start | bytes 811016 | tf_op jit(solution)/shard_map/ppermute | solution.py:354
  60.2 1.5 shard_map.148.dense_ref
  61.7 1.3 copy-done.2
  63.0 3.8 %collective-permute-done.2.rest_6_ = bf16[1056,128]{1,0:T(8,128)(2,1)S(1)} collective-permute-done((bf16[1056,128]{1,0:T(8,128)(2,1)S(1)}, bf16[1056,128]{1,0:T(8,128)(2,1)S(1)}, u32[]{:S(2)}, u32[]{:S(2)}) %collective-permute-start.2) | collective-permute-done | bytes 270368 | tf_op jit(solution)/shard_map/ppermute | solution.py:353
  66.8 1.9 collective-permute-start.4
  69.4 5.1 %collective-permute-start.5 = (bf16[1056,128]{1,0:T(8,128)(2,1)S(1)}, bf16[1056,128]{1,0:T(8,128)(2,1)S(1)}, u32[]{:S(2)}, u32[]{:S(2)}) collective-permute-start(bf16[1056,128]{1,0:T(8,128)(2,1)S(1)} %collective-permute-done.3.rest_7_), channel_id=1, source_target_pairs={{0,7},{1,0},{2,1},{3,2},{4,3},{5,4},{6,5},{7,6},{8,15},{9,8},{10,9... | collective-permute-start | bytes 811016 | tf_op jit(solution)/shard_map/ppermute | solution.py:354
  75.3 3.2 %collective-permute-done.4.rest_8_ = bf16[1056,128]{1,0:T(8,128)(2,1)} collective-permute-done((bf16[1056,128]{1,0:T(8,128)(2,1)S(1)}, bf16[1056,128]{1,0:T(8,128)(2,1)}, u32[]{:S(2)}, u32[]{:S(2)}) %collective-permute-start.4) | collective-permute-done | bytes 270368 | tf_op jit(solution)/shard_map/ppermute | solution.py:353
  78.5 1.9 collective-permute-start.6
  81.2 14.0 %all_gather.19.sums_ref = bf16[1024,128]{1,0:T(8,128)(2,1)S(1)} all-gather(bf16[512,128]{1,0:T(8,128)(2,1)} %reduce-scatter.4.cloned.1.call-done), channel_id=1, replica_groups={{0,8},{1,9},{2,10},{3,11},{4,12},{5,13},{6,14},{7,15},{16,24},{17,25},{..., dimensions={0}, use_global_device_ids=true | all-gather | bytes 393216 | tf_op jit(solution)/shard_map/all_gather | solution.py:328
  95.2 1.0 copy-done.16
  103.7 2.1 shard_map.150.rest_11_
  105.8 1.9 collective-permute-start.7
  111.3 2.7 shard_map.151
  115.5 1.3 shard_map.155
  116.8 1.0 copy-done.10
  118.5 13.7 %all_gather.20.both = bf16[1056,128]{1,0:T(8,128)(2,1)S(1)} all-gather(bf16[528,128]{1,0:T(8,128)(2,1)} %copy-done.26), channel_id=1, replica_groups={{0,8},{1,9},{2,10},{3,11},{4,12},{5,13},{6,14},{7,15},{16,24},{17,25},{..., dimensions={0}, use_global_device_ids=true | all-gather | bytes 405504 | tf_op jit(solution)/shard_map/all_gather | solution.py:328
  132.8 1.9 collective-permute-start.8
  134.7 5.7 %collective-permute-start.9 = (bf16[1056,128]{1,0:T(8,128)(2,1)S(1)}, bf16[1056,128]{1,0:T(8,128)(2,1)S(1)}, u32[]{:S(2)}, u32[]{:S(2)}) collective-permute-start(bf16[1056,128]{1,0:T(8,128)(2,1)S(1)} %shard_map.153.rest_1_), channel_id=1, source_target_pairs={{0,7},{1,0},{2,1},{3,2},{4,3},{5,4},{6,5},{7,6},{8,15},{9,8},{10,9... | collective-permute-start | bytes 811016 | tf_op jit(solution)/shard_map/ppermute | solution.py:354
  141.1 4.0 %collective-permute-done.8.rest_0_.rest_2_ = bf16[1056,128]{1,0:T(8,128)(2,1)S(1)} collective-permute-done((bf16[1056,128]{1,0:T(8,128)(2,1)S(1)}, bf16[1056,128]{1,0:T(8,128)(2,1)S(1)}, u32[]{:S(2)}, u32[]{:S(2)}) %collective-permute-start.8) | collective-permute-done | bytes 270368 | tf_op jit(solution)/shard_map/ppermute | solution.py:353
  145.2 1.9 collective-permute-start.10
  147.6 7.4 %collective-permute-start.11 = (bf16[1056,128]{1,0:T(8,128)(2,1)S(1)}, bf16[1056,128]{1,0:T(8,128)(2,1)S(1)}, u32[]{:S(2)}, u32[]{:S(2)}) collective-permute-start(bf16[1056,128]{1,0:T(8,128)(2,1)S(1)} %collective-permute-done.9.rest_3_), channel_id=1, source_target_pairs={{0,7},{1,0},{2,1},{3,2},{4,3},{5,4},{6,5},{7,6},{8,15},{9,8},{10,9... | collective-permute-start | bytes 811016 | tf_op jit(solution)/shard_map/ppermute | solution.py:354
  156.9 1.3 shard_map.154.dense_ref
  158.3 1.3 copy-done.5
  159.6 2.1 collective-permute-done.10.rest_4_
  161.7 1.9 collective-permute-start.12
  164.3 5.1 %collective-permute-start.13 = (bf16[1056,128]{1,0:T(8,128)(2,1)S(1)}, bf16[1056,128]{1,0:T(8,128)(2,1)S(1)}, u32[]{:S(2)}, u32[]{:S(2)}) collective-permute-start(bf16[1056,128]{1,0:T(8,128)(2,1)S(1)} %collective-permute-done.11.rest_5_), channel_id=1, source_target_pairs={{0,7},{1,0},{2,1},{3,2},{4,3},{5,4},{6,5},{7,6},{8,15},{9,8},{10,9... | collective-permute-start | bytes 811016 | tf_op jit(solution)/shard_map/ppermute | solution.py:354
  170.2 3.2 %collective-permute-done.12.rest_6_ = bf16[1056,128]{1,0:T(8,128)(2,1)S(1)} collective-permute-done((bf16[1056,128]{1,0:T(8,128)(2,1)S(1)}, bf16[1056,128]{1,0:T(8,128)(2,1)S(1)}, u32[]{:S(2)}, u32[]{:S(2)}) %collective-permute-start.12) | collective-permute-done | bytes 270368 | tf_op jit(solution)/shard_map/ppermute | solution.py:353
  173.4 1.9 collective-permute-start.14
  175.6 11.3 %all_gather.21.sums_ref = bf16[1024,128]{1,0:T(8,128)(2,1)S(1)} all-gather(bf16[512,128]{1,0:T(8,128)(2,1)} %reduce-scatter.6.cloned.1.call-done), channel_id=1, replica_groups={{0,8},{1,9},{2,10},{3,11},{4,12},{5,13},{6,14},{7,15},{16,24},{17,25},{..., dimensions={0}, use_global_device_ids=true | all-gather | bytes 393216 | tf_op jit(solution)/shard_map/all_gather | solution.py:328
  186.9 1.0 copy-done.13
  188.8 1.0 copy-done.25
  192.6 1.5 shard_map.156.rest_9_
  194.2 1.9 collective-permute-start.15
  197.1 1.0 copy-done.64
  198.8 2.1 shard_map.157
  201.7 2.3 shard_map.161
  204.0 13.3 %all_gather.22.both = bf16[1056,128]{1,0:T(8,128)(2,1)S(1)} all-gather(bf16[528,128]{1,0:T(8,128)(2,1)S(1)} %shard_map.158.users_ref), channel_id=1, replica_groups={{0,8},{1,9},{2,10},{3,11},{4,12},{5,13},{6,14},{7,15},{16,24},{17,25},{..., dimensions={0}, use_global_device_ids=true | all-gather | bytes 405504 | tf_op jit(solution)/shard_map/all_gather | solution.py:328
  217.8 1.9 collective-permute-start.16
  219.8 5.3 %collective-permute-start.17 = (bf16[1056,128]{1,0:T(8,128)(2,1)S(1)}, bf16[1056,128]{1,0:T(8,128)(2,1)S(1)}, u32[]{:S(2)}, u32[]{:S(2)}) collective-permute-start(bf16[1056,128]{1,0:T(8,128)(2,1)S(1)} %shard_map.159.rest_1_), channel_id=1, source_target_pairs={{0,7},{1,0},{2,1},{3,2},{4,3},{5,4},{6,5},{7,6},{8,15},{9,8},{10,9... | collective-permute-start | bytes 811016 | tf_op jit(solution)/shard_map/ppermute | solution.py:354
  225.0 4.3 %collective-permute-done.16.rest_2_ = bf16[1056,128]{1,0:T(8,128)(2,1)S(1)} collective-permute-done((bf16[1056,128]{1,0:T(8,128)(2,1)S(1)}, bf16[1056,128]{1,0:T(8,128)(2,1)S(1)}, u32[]{:S(2)}, u32[]{:S(2)}) %collective-permute-start.16) | collective-permute-done | bytes 270368 | tf_op jit(solution)/shard_map/ppermute | solution.py:353
  229.4 2.8 collective-permute-start.18
  232.3 8.2 %collective-permute-start.19 = (bf16[1056,128]{1,0:T(8,128)(2,1)S(1)}, bf16[1056,128]{1,0:T(8,128)(2,1)S(1)}, u32[]{:S(2)}, u32[]{:S(2)}) collective-permute-start(bf16[1056,128]{1,0:T(8,128)(2,1)S(1)} %collective-permute-done.17.rest_3_), channel_id=1, source_target_pairs={{0,7},{1,0},{2,1},{3,2},{4,3},{5,4},{6,5},{7,6},{8,15},{9,8},{10,9... | collective-permute-start | bytes 811016 | tf_op jit(solution)/shard_map/ppermute | solution.py:354
  240.5 6.6 %collective-permute-done.18.rest_4_ = bf16[1056,128]{1,0:T(8,128)(2,1)S(1)} collective-permute-done((bf16[1056,128]{1,0:T(8,128)(2,1)S(1)}, bf16[1056,128]{1,0:T(8,128)(2,1)S(1)}, u32[]{:S(2)}, u32[]{:S(2)}) %collective-permute-start.18) | collective-permute-done | bytes 270368 | tf_op jit(solution)/shard_map/ppermute | solution.py:353
  247.1 1.9 collective-permute-start.20
  249.0 5.1 %collective-permute-start.21 = (bf16[1056,128]{1,0:T(8,128)(2,1)S(1)}, bf16[1056,128]{1,0:T(8,128)(2,1)S(1)}, u32[]{:S(2)}, u32[]{:S(2)}) collective-permute-start(bf16[1056,128]{1,0:T(8,128)(2,1)S(1)} %collective-permute-done.19.rest_5_), channel_id=1, source_target_pairs={{0,7},{1,0},{2,1},{3,2},{4,3},{5,4},{6,5},{7,6},{8,15},{9,8},{10,9... | collective-permute-start | bytes 811016 | tf_op jit(solution)/shard_map/ppermute | solution.py:354
  254.2 4.6 %collective-permute-done.20.rest_6_ = bf16[1056,128]{1,0:T(8,128)(2,1)S(1)} collective-permute-done((bf16[1056,128]{1,0:T(8,128)(2,1)S(1)}, bf16[1056,128]{1,0:T(8,128)(2,1)S(1)}, u32[]{:S(2)}, u32[]{:S(2)}) %collective-permute-start.20) | collective-permute-done | bytes 270368 | tf_op jit(solution)/shard_map/ppermute | solution.py:353
  258.8 1.9 collective-permute-start.22
  260.7 7.6 %collective-permute-done.22.rest_8_ = bf16[1056,128]{1,0:T(8,128)(2,1)S(1)} collective-permute-done((bf16[1056,128]{1,0:T(8,128)(2,1)S(1)}, bf16[1056,128]{1,0:T(8,128)(2,1)S(1)}, u32[]{:S(2)}, u32[]{:S(2)}) %collective-permute-start.22) | collective-permute-done | bytes 270368 | tf_op jit(solution)/shard_map/ppermute | solution.py:361
  268.3 1.0 copy-done.66
  269.3 2.8 shard_map.160
  275.6 9.8 %all_gather.23.sums_ref = bf16[1024,128]{1,0:T(8,128)(2,1)S(1)} all-gather(bf16[512,128]{1,0:T(8,128)(2,1)} %reduce-scatter.8.cloned.1.call-done), channel_id=1, replica_groups={{0,8},{1,9},{2,10},{3,11},{4,12},{5,13},{6,14},{7,15},{16,24},{17,25},{..., dimensions={0}, use_global_device_ids=true | all-gather | bytes 393216 | tf_op jit(solution)/shard_map/all_gather | solution.py:328
  285.4 1.0 copy-done.29
  290.1 2.3 shard_map.162
  (188 shorter events, 43.1 us)
Async XLA Ops:
  7.2 74.0 %reduce-scatter.4.cloned.1.call-start = ((), (), s32[]{:S(2)}) async-start(), calls=%async_computation.3 | async-start | bytes 1179648 | tf_op jit(solution)/shard_map/reduce_scatter | solution.py:343
  8.0 6.5 %copy-start.71 = (s32[108]{0:T(128)}, s32[108]{0:T(128)S(1)}, u32[]{:S(2)}) copy-start(s32[108]{0:T(128)S(1)} %reshape.21.users_at) | copy-start | bytes 1300
  8.8 5.8 %copy-start.74 = (s32[108]{0:T(128)}, s32[108]{0:T(128)S(1)}, u32[]{:S(2)}) copy-start(s32[108]{0:T(128)S(1)} %reshape.22.items_at) | copy-start | bytes 1300
  14.6 3.4 %copy-start.27 = (bf16[528,128]{1,0:T(8,128)(2,1)}, bf16[528,128]{1,0:T(8,128)(2,1)S(1)}, u32[]{:S(2)}) copy-start(bf16[528,128]{1,0:T(8,128)(2,1)S(1)} %get-tuple-element.25.rest_0_.users_ref) | copy-start | bytes 405508
  14.6 2.1 copy-start
  18.0 40.2 %copy-start.1 = (bf16[1,1,3,36,128,128]{5,4,3,2,1,0:T(8,128)(2,1)S(1)}, bf16[1,1,3,36,128,128]{5,4,3,2,1,0:T(8,128)(2,1)}, u32[]{:S(2)}) copy-start(bf16[1,1,3,36,128,128]{5,4,3,2,1,0:T(8,128)(2,1)} %ratings.5) | copy-start | bytes 10616836
  19.3 1.3 copy-start.8
  20.6 1.0 copy-start.11
  21.6 154.0 %reduce-scatter.6.cloned.1.call-start = ((), (), s32[]{:S(2)}) async-start(), calls=%async_computation.4 | async-start | bytes 1179648 | tf_op jit(solution)/shard_map/reduce_scatter | solution.py:343
  36.0 12.8 %collective-permute-start = (bf16[1056,128]{1,0:T(8,128)(2,1)S(1)}, bf16[1056,128]{1,0:T(8,128)(2,1)S(1)}, u32[]{:S(2)}, u32[]{:S(2)}) collective-permute-start(bf16[1056,128]{1,0:T(8,128)(2,1)S(1)} %shard_map.147.rest_3_), channel_id=1, source_target_pairs={{0,1},{1,2},{2,3},{3,4},{4,5},{5,6},{6,7},{7,0},{8,9},{9,10},{10,1... | collective-permute-start | bytes 811016 | tf_op jit(solution)/shard_map/ppermute | solution.py:353
  39.6 13.5 %collective-permute-start.1 = (bf16[1056,128]{1,0:T(8,128)(2,1)S(1)}, bf16[1056,128]{1,0:T(8,128)(2,1)S(1)}, u32[]{:S(2)}, u32[]{:S(2)}) collective-permute-start(bf16[1056,128]{1,0:T(8,128)(2,1)S(1)} %shard_map.147.rest_3_), channel_id=1, source_target_pairs={{0,7},{1,0},{2,1},{3,2},{4,3},{5,4},{6,5},{7,6},{8,15},{9,8},{10,9... | collective-permute-start | bytes 811016 | tf_op jit(solution)/shard_map/ppermute | solution.py:354
  48.8 12.8 %copy-start.15 = (bf16[1056,128]{1,0:T(8,128)(2,1)}, bf16[1056,128]{1,0:T(8,128)(2,1)S(1)}, u32[]{:S(2)}) copy-start(bf16[1056,128]{1,0:T(8,128)(2,1)S(1)} %collective-permute-done.rest_0_.rest_4_) | copy-start | bytes 811012
  48.8 17.9 %collective-permute-start.2 = (bf16[1056,128]{1,0:T(8,128)(2,1)S(1)}, bf16[1056,128]{1,0:T(8,128)(2,1)S(1)}, u32[]{:S(2)}, u32[]{:S(2)}) collective-permute-start(bf16[1056,128]{1,0:T(8,128)(2,1)S(1)} %collective-permute-done.rest_0_.rest_4_), channel_id=1, source_target_pairs={{0,1},{1,2},{2,3},{3,4},{4,5},{5,6},{6,7},{7,0},{8,9},{9,10},{10,1... | collective-permute-start | bytes 811016 | tf_op jit(solution)/shard_map/ppermute | solution.py:353
  53.2 8.5 %copy-start.41 = (bf16[1056,128]{1,0:T(8,128)(2,1)}, bf16[1056,128]{1,0:T(8,128)(2,1)S(1)}, u32[]{:S(2)}) copy-start(bf16[1056,128]{1,0:T(8,128)(2,1)S(1)} %collective-permute-done.1.rest_5_) | copy-start | bytes 811012
  53.2 16.2 %collective-permute-start.3 = (bf16[1056,128]{1,0:T(8,128)(2,1)S(1)}, bf16[1056,128]{1,0:T(8,128)(2,1)S(1)}, u32[]{:S(2)}, u32[]{:S(2)}) collective-permute-start(bf16[1056,128]{1,0:T(8,128)(2,1)S(1)} %collective-permute-done.1.rest_5_), channel_id=1, source_target_pairs={{0,7},{1,0},{2,1},{3,2},{4,3},{5,4},{6,5},{7,6},{8,15},{9,8},{10,9... | collective-permute-start | bytes 811016 | tf_op jit(solution)/shard_map/ppermute | solution.py:354
  61.7 1.3 copy-start.2
  66.8 11.7 %collective-permute-start.4 = (bf16[1056,128]{1,0:T(8,128)(2,1)S(1)}, bf16[1056,128]{1,0:T(8,128)(2,1)}, u32[]{:S(2)}, u32[]{:S(2)}) collective-permute-start(bf16[1056,128]{1,0:T(8,128)(2,1)S(1)} %collective-permute-done.2.rest_6_), channel_id=1, source_target_pairs={{0,1},{1,2},{2,3},{3,4},{4,5},{5,6},{6,7},{7,0},{8,9},{9,10},{10,1... | collective-permute-start | bytes 811016 | tf_op jit(solution)/shard_map/ppermute | solution.py:353
  69.4 11.1 %collective-permute-start.5 = (bf16[1056,128]{1,0:T(8,128)(2,1)S(1)}, bf16[1056,128]{1,0:T(8,128)(2,1)S(1)}, u32[]{:S(2)}, u32[]{:S(2)}) collective-permute-start(bf16[1056,128]{1,0:T(8,128)(2,1)S(1)} %collective-permute-done.3.rest_7_), channel_id=1, source_target_pairs={{0,7},{1,0},{2,1},{3,2},{4,3},{5,4},{6,5},{7,6},{8,15},{9,8},{10,9... | collective-permute-start | bytes 811016 | tf_op jit(solution)/shard_map/ppermute | solution.py:354
  78.5 16.7 %collective-permute-start.6 = (bf16[1056,128]{1,0:T(8,128)(2,1)}, bf16[1056,128]{1,0:T(8,128)(2,1)}, u32[]{:S(2)}, u32[]{:S(2)}) collective-permute-start(bf16[1056,128]{1,0:T(8,128)(2,1)} %collective-permute-done.4.rest_8_), channel_id=1, source_target_pairs={{0,1},{1,2},{2,3},{3,4},{4,5},{5,6},{6,7},{7,0},{8,9},{9,10},{10,1... | collective-permute-start | bytes 811016 | tf_op jit(solution)/shard_map/ppermute | solution.py:361
  81.2 26.6 %copy-start.9 = (bf16[8192,128]{1,0:T(8,128)(2,1)S(1)}, bf16[8192,128]{1,0:T(8,128)(2,1)}, u32[]{:S(2)}) copy-start(bf16[8192,128]{1,0:T(8,128)(2,1)} %copy-done.8) | copy-start | bytes 6291460
  95.2 1.0 copy-start.16
  103.7 4.1 %copy-start.17 = (bf16[1056,128]{1,0:T(8,128)(2,1)S(1)}, bf16[1056,128]{1,0:T(8,128)(2,1)}, u32[]{:S(2)}) copy-start(bf16[1056,128]{1,0:T(8,128)(2,1)} %copy-done.15) | copy-start | bytes 811012
  103.7 4.1 %copy-start.23 = (bf16[1056,128]{1,0:T(8,128)(2,1)S(1)}, bf16[1056,128]{1,0:T(8,128)(2,1)}, u32[]{:S(2)}) copy-start(bf16[1056,128]{1,0:T(8,128)(2,1)} %copy-done.21) | copy-start | bytes 811012
  103.7 4.1 %copy-start.43 = (bf16[1056,128]{1,0:T(8,128)(2,1)S(1)}, bf16[1056,128]{1,0:T(8,128)(2,1)}, u32[]{:S(2)}) copy-start(bf16[1056,128]{1,0:T(8,128)(2,1)} %copy-done.41) | copy-start | bytes 811012
  103.7 4.1 %copy-start.49 = (bf16[1056,128]{1,0:T(8,128)(2,1)S(1)}, bf16[1056,128]{1,0:T(8,128)(2,1)}, u32[]{:S(2)}) copy-start(bf16[1056,128]{1,0:T(8,128)(2,1)} %copy-done.47) | copy-start | bytes 811012
  103.7 4.1 %copy-start.55 = (bf16[1056,128]{1,0:T(8,128)(2,1)S(1)}, bf16[1056,128]{1,0:T(8,128)(2,1)}, u32[]{:S(2)}) copy-start(bf16[1056,128]{1,0:T(8,128)(2,1)} %copy-done.53) | copy-start | bytes 811012
  103.7 4.1 %copy-start.60 = (f32[256,128]{1,0:T(8,128)S(1)}, f32[256,128]{1,0:T(8,128)}, u32[]{:S(2)}) copy-start(f32[256,128]{1,0:T(8,128)} %rest_0_.3) | copy-start | bytes 393220
  105.8 8.2 %collective-permute-start.7 = (f32[768,128]{1,0:T(8,128)S(1)}, f32[768,128]{1,0:T(8,128)S(1)}, u32[]{:S(2)}, u32[]{:S(2)}) collective-permute-start(f32[768,128]{1,0:T(8,128)S(1)} %shard_map.150.rest_11_), channel_id=1, source_target_pairs={{0,496},{16,0},{32,16},{48,32},{64,48},{80,64},{96,80},{112,96},{1... | collective-permute-start | bytes 1179656 | tf_op jit(solution)/shard_map/ppermute | solution.py:364
  107.8 1.0 copy-start.58
  111.3 4.2 %copy-start.3 = (bf16[8192,128]{1,0:T(8,128)(2,1)S(1)}, bf16[8192,128]{1,0:T(8,128)(2,1)}, u32[]{:S(2)}) copy-start(bf16[8192,128]{1,0:T(8,128)(2,1)} %copy-done.2) | copy-start | bytes 6291460
  116.8 1.0 copy-start.10
  118.5 157.2 %reduce-scatter.8.cloned.1.call-start = ((), (), s32[]{:S(2)}) async-start(), calls=%async_computation.5 | async-start | bytes 1179648 | tf_op jit(solution)/shard_map/reduce_scatter | solution.py:343
  132.8 12.4 %collective-permute-start.8 = (bf16[1056,128]{1,0:T(8,128)(2,1)S(1)}, bf16[1056,128]{1,0:T(8,128)(2,1)S(1)}, u32[]{:S(2)}, u32[]{:S(2)}) collective-permute-start(bf16[1056,128]{1,0:T(8,128)(2,1)S(1)} %shard_map.153.rest_1_), channel_id=1, source_target_pairs={{0,1},{1,2},{2,3},{3,4},{4,5},{5,6},{6,7},{7,0},{8,9},{9,10},{10,1... | collective-permute-start | bytes 811016 | tf_op jit(solution)/shard_map/ppermute | solution.py:353
  134.7 12.9 %collective-permute-start.9 = (bf16[1056,128]{1,0:T(8,128)(2,1)S(1)}, bf16[1056,128]{1,0:T(8,128)(2,1)S(1)}, u32[]{:S(2)}, u32[]{:S(2)}) collective-permute-start(bf16[1056,128]{1,0:T(8,128)(2,1)S(1)} %shard_map.153.rest_1_), channel_id=1, source_target_pairs={{0,7},{1,0},{2,1},{3,2},{4,3},{5,4},{6,5},{7,6},{8,15},{9,8},{10,9... | collective-permute-start | bytes 811016 | tf_op jit(solution)/shard_map/ppermute | solution.py:354
  145.2 13.1 %copy-start.12 = (bf16[1056,128]{1,0:T(8,128)(2,1)}, bf16[1056,128]{1,0:T(8,128)(2,1)S(1)}, u32[]{:S(2)}) copy-start(bf16[1056,128]{1,0:T(8,128)(2,1)S(1)} %collective-permute-done.8.rest_0_.rest_2_) | copy-start | bytes 811012
  145.2 16.5 %collective-permute-start.10 = (bf16[1056,128]{1,0:T(8,128)(2,1)S(1)}, bf16[1056,128]{1,0:T(8,128)(2,1)S(1)}, u32[]{:S(2)}, u32[]{:S(2)}) collective-permute-start(bf16[1056,128]{1,0:T(8,128)(2,1)S(1)} %collective-permute-done.8.rest_0_.rest_2_), channel_id=1, source_target_pairs={{0,1},{1,2},{2,3},{3,4},{4,5},{5,6},{6,7},{7,0},{8,9},{9,10},{10,1... | collective-permute-start | bytes 811016 | tf_op jit(solution)/shard_map/ppermute | solution.py:353
  147.6 10.7 %copy-start.38 = (bf16[1056,128]{1,0:T(8,128)(2,1)}, bf16[1056,128]{1,0:T(8,128)(2,1)S(1)}, u32[]{:S(2)}) copy-start(bf16[1056,128]{1,0:T(8,128)(2,1)S(1)} %collective-permute-done.9.rest_3_) | copy-start | bytes 811012
  147.6 16.7 %collective-permute-start.11 = (bf16[1056,128]{1,0:T(8,128)(2,1)S(1)}, bf16[1056,128]{1,0:T(8,128)(2,1)S(1)}, u32[]{:S(2)}, u32[]{:S(2)}) collective-permute-start(bf16[1056,128]{1,0:T(8,128)(2,1)S(1)} %collective-permute-done.9.rest_3_), channel_id=1, source_target_pairs={{0,7},{1,0},{2,1},{3,2},{4,3},{5,4},{6,5},{7,6},{8,15},{9,8},{10,9... | collective-permute-start | bytes 811016 | tf_op jit(solution)/shard_map/ppermute | solution.py:354
  158.3 1.3 copy-start.5
  159.6 36.5 %copy-start.4 = (bf16[8192,128]{1,0:T(8,128)(2,1)S(1)}, bf16[8192,128]{1,0:T(8,128)(2,1)}, u32[]{:S(2)}) copy-start(bf16[8192,128]{1,0:T(8,128)(2,1)} %copy-done.2) | copy-start | bytes 6291460
  161.7 11.7 %collective-permute-start.12 = (bf16[1056,128]{1,0:T(8,128)(2,1)S(1)}, bf16[1056,128]{1,0:T(8,128)(2,1)S(1)}, u32[]{:S(2)}, u32[]{:S(2)}) collective-permute-start(bf16[1056,128]{1,0:T(8,128)(2,1)S(1)} %collective-permute-done.10.rest_4_), channel_id=1, source_target_pairs={{0,1},{1,2},{2,3},{3,4},{4,5},{5,6},{6,7},{7,0},{8,9},{9,10},{10,1... | collective-permute-start | bytes 811016 | tf_op jit(solution)/shard_map/ppermute | solution.py:353
  164.3 11.3 %collective-permute-start.13 = (bf16[1056,128]{1,0:T(8,128)(2,1)S(1)}, bf16[1056,128]{1,0:T(8,128)(2,1)S(1)}, u32[]{:S(2)}, u32[]{:S(2)}) collective-permute-start(bf16[1056,128]{1,0:T(8,128)(2,1)S(1)} %collective-permute-done.11.rest_5_), channel_id=1, source_target_pairs={{0,7},{1,0},{2,1},{3,2},{4,3},{5,4},{6,5},{7,6},{8,15},{9,8},{10,9... | collective-permute-start | bytes 811016 | tf_op jit(solution)/shard_map/ppermute | solution.py:354
  173.4 13.5 %collective-permute-start.14 = (bf16[1056,128]{1,0:T(8,128)(2,1)S(1)}, bf16[1056,128]{1,0:T(8,128)(2,1)S(1)}, u32[]{:S(2)}, u32[]{:S(2)}) collective-permute-start(bf16[1056,128]{1,0:T(8,128)(2,1)S(1)} %collective-permute-done.12.rest_6_), channel_id=1, source_target_pairs={{0,1},{1,2},{2,3},{3,4},{4,5},{5,6},{6,7},{7,0},{8,9},{9,10},{10,1... | collective-permute-start | bytes 811016 | tf_op jit(solution)/shard_map/ppermute | solution.py:361
  186.9 1.0 copy-start.13
  188.8 1.0 copy-start.25
  192.6 3.5 %copy-start.14 = (bf16[1056,128]{1,0:T(8,128)(2,1)S(1)}, bf16[1056,128]{1,0:T(8,128)(2,1)}, u32[]{:S(2)}) copy-start(bf16[1056,128]{1,0:T(8,128)(2,1)} %copy-done.12) | copy-start | bytes 811012
  192.6 3.5 %copy-start.40 = (bf16[1056,128]{1,0:T(8,128)(2,1)S(1)}, bf16[1056,128]{1,0:T(8,128)(2,1)}, u32[]{:S(2)}) copy-start(bf16[1056,128]{1,0:T(8,128)(2,1)} %copy-done.38) | copy-start | bytes 811012
  192.6 3.5 %copy-start.46 = (bf16[1056,128]{1,0:T(8,128)(2,1)S(1)}, bf16[1056,128]{1,0:T(8,128)(2,1)}, u32[]{:S(2)}) copy-start(bf16[1056,128]{1,0:T(8,128)(2,1)} %copy-done.44) | copy-start | bytes 811012
  192.6 3.5 %copy-start.52 = (bf16[1056,128]{1,0:T(8,128)(2,1)S(1)}, bf16[1056,128]{1,0:T(8,128)(2,1)}, u32[]{:S(2)}) copy-start(bf16[1056,128]{1,0:T(8,128)(2,1)} %copy-done.50) | copy-start | bytes 811012
  194.2 7.4 %collective-permute-start.15 = (f32[768,128]{1,0:T(8,128)S(1)}, f32[768,128]{1,0:T(8,128)S(1)}, u32[]{:S(2)}, u32[]{:S(2)}) collective-permute-start(f32[768,128]{1,0:T(8,128)S(1)} %shard_map.156.rest_9_), channel_id=1, source_target_pairs={{0,496},{16,0},{32,16},{48,32},{64,48},{80,64},{96,80},{112,96},{1... | collective-permute-start | bytes 1179656 | tf_op jit(solution)/shard_map/ppermute | solution.py:364
  196.2 1.0 copy-start.20
  197.1 1.0 copy-start.64
  198.8 2.8 copy-start.6
  201.6 66.7 %copy-start.7 = (bf16[8192,128]{1,0:T(8,128)(2,1)S(1)}, bf16[8192,128]{1,0:T(8,128)(2,1)}, u32[]{:S(2)}) copy-start(bf16[8192,128]{1,0:T(8,128)(2,1)} %copy-done.5) | copy-start | bytes 6291460
  201.6 66.7 %copy-start.80 = (f32[192]{0:T(256)S(1)}, f32[192]{0:T(256)}, u32[]{:S(2)}) copy-start(f32[192]{0:T(256)} %copy-done.77) | copy-start | bytes 2308
  217.8 11.5 %collective-permute-start.16 = (bf16[1056,128]{1,0:T(8,128)(2,1)S(1)}, bf16[1056,128]{1,0:T(8,128)(2,1)S(1)}, u32[]{:S(2)}, u32[]{:S(2)}) collective-permute-start(bf16[1056,128]{1,0:T(8,128)(2,1)S(1)} %shard_map.159.rest_1_), channel_id=1, source_target_pairs={{0,1},{1,2},{2,3},{3,4},{4,5},{5,6},{6,7},{7,0},{8,9},{9,10},{10,1... | collective-permute-start | bytes 811016 | tf_op jit(solution)/shard_map/ppermute | solution.py:353
  219.8 12.5 %collective-permute-start.17 = (bf16[1056,128]{1,0:T(8,128)(2,1)S(1)}, bf16[1056,128]{1,0:T(8,128)(2,1)S(1)}, u32[]{:S(2)}, u32[]{:S(2)}) collective-permute-start(bf16[1056,128]{1,0:T(8,128)(2,1)S(1)} %shard_map.159.rest_1_), channel_id=1, source_target_pairs={{0,7},{1,0},{2,1},{3,2},{4,3},{5,4},{6,5},{7,6},{8,15},{9,8},{10,9... | collective-permute-start | bytes 811016 | tf_op jit(solution)/shard_map/ppermute | solution.py:354
  229.4 17.7 %collective-permute-start.18 = (bf16[1056,128]{1,0:T(8,128)(2,1)S(1)}, bf16[1056,128]{1,0:T(8,128)(2,1)S(1)}, u32[]{:S(2)}, u32[]{:S(2)}) collective-permute-start(bf16[1056,128]{1,0:T(8,128)(2,1)S(1)} %collective-permute-done.16.rest_2_), channel_id=1, source_target_pairs={{0,1},{1,2},{2,3},{3,4},{4,5},{5,6},{6,7},{7,0},{8,9},{9,10},{10,1... | collective-permute-start | bytes 811016 | tf_op jit(solution)/shard_map/ppermute | solution.py:353
  232.3 16.7 %collective-permute-start.19 = (bf16[1056,128]{1,0:T(8,128)(2,1)S(1)}, bf16[1056,128]{1,0:T(8,128)(2,1)S(1)}, u32[]{:S(2)}, u32[]{:S(2)}) collective-permute-start(bf16[1056,128]{1,0:T(8,128)(2,1)S(1)} %collective-permute-done.17.rest_3_), channel_id=1, source_target_pairs={{0,7},{1,0},{2,1},{3,2},{4,3},{5,4},{6,5},{7,6},{8,15},{9,8},{10,9... | collective-permute-start | bytes 811016 | tf_op jit(solution)/shard_map/ppermute | solution.py:354
  247.1 11.7 %collective-permute-start.20 = (bf16[1056,128]{1,0:T(8,128)(2,1)S(1)}, bf16[1056,128]{1,0:T(8,128)(2,1)S(1)}, u32[]{:S(2)}, u32[]{:S(2)}) collective-permute-start(bf16[1056,128]{1,0:T(8,128)(2,1)S(1)} %collective-permute-done.18.rest_4_), channel_id=1, source_target_pairs={{0,1},{1,2},{2,3},{3,4},{4,5},{5,6},{6,7},{7,0},{8,9},{9,10},{10,1... | collective-permute-start | bytes 811016 | tf_op jit(solution)/shard_map/ppermute | solution.py:353
  249.0 11.7 %collective-permute-start.21 = (bf16[1056,128]{1,0:T(8,128)(2,1)S(1)}, bf16[1056,128]{1,0:T(8,128)(2,1)S(1)}, u32[]{:S(2)}, u32[]{:S(2)}) collective-permute-start(bf16[1056,128]{1,0:T(8,128)(2,1)S(1)} %collective-permute-done.19.rest_5_), channel_id=1, source_target_pairs={{0,7},{1,0},{2,1},{3,2},{4,3},{5,4},{6,5},{7,6},{8,15},{9,8},{10,9... | collective-permute-start | bytes 811016 | tf_op jit(solution)/shard_map/ppermute | solution.py:354
  258.8 9.6 %collective-permute-start.22 = (bf16[1056,128]{1,0:T(8,128)(2,1)S(1)}, bf16[1056,128]{1,0:T(8,128)(2,1)S(1)}, u32[]{:S(2)}, u32[]{:S(2)}) collective-permute-start(bf16[1056,128]{1,0:T(8,128)(2,1)S(1)} %collective-permute-done.20.rest_6_), channel_id=1, source_target_pairs={{0,1},{1,2},{2,3},{3,4},{4,5},{5,6},{6,7},{7,0},{8,9},{9,10},{10,1... | collective-permute-start | bytes 811016 | tf_op jit(solution)/shard_map/ppermute | solution.py:361
  268.3 1.0 copy-start.66
  285.4 1.0 copy-start.29
  (46 other events, 36.7 us)
Sparse Core Ops, SparseCore 0:
  21.7 49.2 reduce-scatter.3
  118.6 42.7 reduce-scatter.5
  204.1 42.8 reduce-scatter.7

commit v7 on v1

v7 whole, which is shorter than its diff:
```python
import functools

import jax
import jax.numpy as jnp
from jax import lax
from jax.experimental import pallas as pl
from jax.experimental.pallas import tpu as pltpu
from jax.sharding import PartitionSpec as P

K = 128
TILE = 128
MAXT = 36
STEPS = 3
USER_ROWS = 256
ITEM_ROWS = 256
USER_TILES = 2
ITEM_TILES = 32
PAIRS = USER_TILES * ITEM_TILES


LEARN_RATE = 0.01
BETA_ONE = 0.8
BETA_TWO = 0.95
ADAM_EPS = 1e-08
DECAY_REG = 0.05
GRAD_SCALE = 0.03125

VMEM = pl.BlockSpec(memory_space=pltpu.VMEM)
SMEM = pl.BlockSpec(memory_space=pltpu.SMEM)
ANY = pl.BlockSpec(memory_space=pl.ANY)
F32 = jnp.float32
BF16 = jnp.bfloat16


def shape(rows, dtype=F32):
    return jax.ShapeDtypeStruct((rows, K), dtype)


def adam_update(param, first, second, grad):
    first = BETA_ONE * first + (1.0 - BETA_ONE) * grad
    second = BETA_TWO * second + (1.0 - BETA_TWO) * grad * grad
    return (param - LEARN_RATE * first / (jnp.sqrt(second) + ADAM_EPS), first, second)


def kernel_call(body, outs, in_specs, out_specs=None, scratch=(), flops=0, moved=1 << 20):
    return pl.pallas_call(
        body,
        out_shape=outs,
        in_specs=in_specs,
        out_specs=out_specs or jax.tree.map(lambda _: VMEM, outs),
        scratch_shapes=list(scratch),
        cost_estimate=pl.CostEstimate(flops=flops, bytes_accessed=moved, transcendentals=0),
        compiler_params=pltpu.CompilerParams(vmem_limit_bytes=40 << 20),
    )


def shifted(block, axis, distance):
    devices = range(lax.axis_size(axis))
    route = [((i - distance) % len(devices), i) for i in devices]
    return lax.ppermute(block, axis, route)


def gathered(rows):
    members = lax.axis_size("narrow")
    copies = jnp.broadcast_to(rows[None], (members,) + rows.shape)
    return lax.all_to_all(copies, "narrow", 0, 0).reshape(members * rows.shape[0], K)


def summed(partial):
    members = lax.axis_size("narrow")
    parts = partial.reshape(members, partial.shape[0] // members, K)
    arrived = lax.all_to_all(parts, "narrow", 0, 0)
    return jnp.sum(arrived.astype(jnp.float32), axis=0)


def dense_body(s, users_at, items_at, live, ratings, *rest):
    out_ref, total, tiles, sem = rest[-4:]
    fetch = pltpu.make_async_copy(ratings.at[0, 0, s], tiles, sem)
    fetch.start()
    total[...] = jnp.zeros_like(total)
    fetch.wait()

    def add(t, carry):
        slot = items_at[s * MAXT + t] * USER_TILES + users_at[s * MAXT + t]
        row = pl.multiple_of(slot * TILE, TILE)
        total[pl.ds(row, TILE), :] += tiles[t].astype(F32)
        return carry

    lax.fori_loop(0, live[s], add, 0)
    out_ref[...] = total[...].astype(BF16)


def dense_ratings(s, users_at, items_at, live, ratings, *later):
    rows = ITEM_TILES * USER_ROWS
    return kernel_call(
        functools.partial(dense_body, s),
        shape(rows, BF16),
        [SMEM, SMEM, SMEM, ANY] + [ANY] * len(later),
        scratch=[
            pltpu.VMEM((rows, TILE), F32),
            pltpu.VMEM((MAXT, TILE, TILE), BF16),
            pltpu.SemaphoreType.DMA,
        ],
        moved=10 << 20,
    )(users_at, items_at, live, ratings, *later)


def tile_body(counts_ref, dense_ref, items_ref, fac_ref, first_ref, second_ref, *outs):
    part_out, fac_out, first_out, second_out = outs
    fac = fac_ref[...]
    users = fac.astype(BF16)
    total = jnp.zeros((USER_ROWS, K), F32)
    upper = lax.broadcasted_iota(jnp.int32, (USER_ROWS, TILE), 0) < TILE
    for k in range(ITEM_TILES // 2):
        rows = items_ref[2 * k * TILE : 2 * (k + 1) * TILE]
        predicted = lax.dot_general(
            users, rows, (((1,), (1,)), ((), ())), preferred_element_type=F32
        )
        errors = []
        for h in range(2):
            tile = 2 * k + h
            many = jnp.where(upper, counts_ref[tile], counts_ref[ITEM_TILES + tile])
            ratings = dense_ref[tile * USER_ROWS : (tile + 1) * USER_ROWS].astype(F32)
            errors.append((predicted[:, h * TILE : (h + 1) * TILE] * many - ratings).astype(BF16))
        error = jnp.concatenate(errors, axis=1)
        total += jnp.dot(error, rows, preferred_element_type=F32)
        part = lax.dot_general(error, users, (((0,), (0,)), ((), ())), preferred_element_type=F32)
        part_out[2 * k * TILE : 2 * (k + 1) * TILE] = part.astype(BF16)
    grad = GRAD_SCALE * total + DECAY_REG * fac
    fac, first, second = adam_update(fac, first_ref[...], second_ref[...], grad)
    fac_out[...] = fac
    first_out[...] = first
    second_out[...] = second


def tile_step(counts, dense, items, state):
    return kernel_call(
        tile_body,
        [shape(ITEM_TILES * TILE, BF16)] + [shape(USER_ROWS)] * 3,
        [SMEM] + [VMEM] * (2 + len(state)),
        flops=6 * ITEM_TILES * USER_ROWS * TILE * K,
        moved=6 << 20,
    )(counts, dense, items, *state)


def per_device(
    user_factors,
    user_m,
    user_v,
    item_factors,
    item_m,
    item_v,
    ratings,
    user_tiles,
    item_tiles,
    tile_counts,
):
    item_fac, item_first, item_second = (item_factors, item_m, item_v)
    user_state = (user_factors, user_m, user_v)
    users_at, items_at = user_tiles.reshape(-1), item_tiles.reshape(-1)
    live = tile_counts.reshape(-1)
    pair = (user_tiles * ITEM_TILES + item_tiles)[0, 0]
    alive = jnp.arange(MAXT)[None, :] < live[:, None]
    named = (pair[:, :, None] == jnp.arange(PAIRS)) & alive[:, :, None]
    counts = jnp.sum(named.astype(F32), axis=1)
    for s in range(STEPS):
        current_rows = gathered(item_fac.astype(BF16))
        dense = dense_ratings(s, users_at, items_at, live, ratings)
        item_part, *user_state = tile_step(counts[s], dense, current_rows, user_state)
        item_total = summed(item_part)
        item_fac, item_first, item_second = adam_update(
            item_fac, item_first, item_second, GRAD_SCALE * item_total + DECAY_REG * item_fac
        )
        if s + 1 < STEPS:
            item_fac, item_first, item_second = shifted(
                (item_fac, item_first, item_second), "blk", -1
            )
    return (*user_state, item_fac, item_first, item_second)


def solution(mesh):
    return jax.shard_map(
        per_device,
        mesh=mesh,
        in_specs=(
            P(("blk", "narrow"), None),
            P(("blk", "narrow"), None),
            P(("blk", "narrow"), None),
            P(("blk", "narrow"), None),
            P(("blk", "narrow"), None),
            P(("blk", "narrow"), None),
            P("blk", "narrow", None, None, None, None),
            P("blk", "narrow", None, None),
            P("blk", "narrow", None, None),
            P("blk", "narrow", None),
        ),
        out_specs=(
            P(("blk", "narrow"), None),
            P(("blk", "narrow"), None),
            P(("blk", "narrow"), None),
            P(("blk", "narrow"), None),
            P(("blk", "narrow"), None),
            P(("blk", "narrow"), None),
        ),
        check_vma=False,
    )
```

time: 290 us -> 290 us (level)
  Pallas kernels: 0 us -> 18.8 us
  matrix products: 17.4 us -> 0 us
  waiting for transfers between devices: 131 us -> 146 us
  local copies, waits for them, and re-layouts: 29.1 us -> 23.1 us
  other arithmetic: 12.2 us -> 6.22 us
    pallas_call x0 -> x6, Pallas kernels: none -> 18.8 us  [the longest x3 14.2 us: tile_step(): kernel_call(tile_body, [shape(ITEM_TILES * TILE, BF16)] + [shape(USER_ROW...]
    dot_general x15 -> x0, matrix products: 17.4 us -> none  [the longest x3 6.66 us: slot_terms(): jnp.einsum('tak,tbk->tab', user_rows, item_rows, preferred_element_type=j...]
    all_to_all x3, waiting for transfers between devices: 78.4 us -> 86.7 us  [gathered(): lax.all_to_all(copies, 'narrow', 0, 0).reshape(members * rows.shape[0], K)]
    gather x6 -> x0, local copies, waits for them, and re-layouts: 7.09 us -> none  [the longest x3 4.77 us: slot_terms(): item_rows = item_bf.reshape(item_tiles_all, TILE, K)[item_idx]]
    unnamed x80 -> x71, local copies, waits for them, and re-layouts: 12.1 us -> 18.8 us
    all_to_all x2, waiting for transfers between devices: 47.9 us -> 54.3 us  [summed(): arrived = lax.all_to_all(parts, 'narrow', 0, 0)]
    convert_element_type x9 -> x3, other arithmetic: 5.53 us -> 0.95 us  [per_device(): current_rows = gathered(item_fac.astype(BF16))]
    convert_element_type x3 -> x0, local copies, waits for them, and re-layouts: 4.21 us -> none  [per_device(): item_total = summed(dense_part.astype(jnp.bfloat16))]
  transfers between devices with their start and end apart: 11 -> 11, of which waited for: 7 -> 7; matrix products, arithmetic and copies ran while one was open for 7% -> 1% of each run, Pallas kernels for 0% -> 2%
where the time goes in v7:
time: 290 us; the launch traced here: 289 us
  waiting for transfers between devices  146 us (50%)
  starting transfers between devices  56.3 us (19%)
  blocking collectives  37.8 us (13%)
  local copies, waits for them, and re-layouts  23.1 us (8%)
  Pallas kernels  18.8 us (6%)
  other arithmetic  6.22 us (2%)
    all_to_all x3, waiting for transfers between devices, gathered(): lax.all_to_all(copies, 'narrow', 0, 0).reshape(members * rows.shape[0], K)  86.7 us
    all_to_all x2, waiting for transfers between devices, summed(): arrived = lax.all_to_all(parts, 'narrow', 0, 0)  54.3 us
    all_to_all x1, blocking collectives, summed(): arrived = lax.all_to_all(parts, 'narrow', 0, 0)  37.8 us
    all_to_all x3, starting transfers between devices, gathered(): lax.all_to_all(copies, 'narrow', 0, 0).reshape(members * rows.shape[0], K)  27 us
    unnamed x71, local copies, waits for them, and re-layouts  18.8 us
    all_to_all x2, starting transfers between devices, summed(): arrived = lax.all_to_all(parts, 'narrow', 0, 0)  17.6 us
    pallas_call x3, Pallas kernels, tile_step(): kernel_call(tile_body, [shape(ITEM_TILES * TILE, BF16)] + [shape(USER_ROW...  14.2 us
    ppermute x6, starting transfers between devices, shifted(): return lax.ppermute(block, axis, route)  11.6 us
  transfers between devices with their start and end apart: 11, of which 7 were waited for; matrix products, arithmetic and copies ran while one was open for 1% of the time, Pallas kernels for 2%

profile of v7, /device:TPU:6, one launch (start us, length us, event | category | flops | bytes accessed | tf_op | source)
XLA Modules:
  0.0 289.3 jit_solution(15114637597785458182)
XLA Ops:
  0.7 0.9 convert_element_type.22
  1.6 1.2 broadcast_in_dim.6
  2.8 15.6 %all-to-all-start = ((bf16[16,256,128]{2,1,0:T(8,128)(2,1)}), bf16[16,256,128]{2,1,0:T(8,128)(2,1)S(1)}, u32[]{:S(2)}, u32[]{:S(2)}) async-start(bf16[16,256,128]{2,1,0:T(8,128)(2,1)} %broadcast_in_dim.6), calls=%async_computation | async-start | bytes 2097152 | tf_op jit(solution)/shard_map/all_to_all | solution.py:66
  18.5 0.1 reshape.65.users_at
  18.6 0.1 reshape.66.items_at
  18.7 2.0 copy-done
  20.7 1.3 shard_map.146.dense_ref
  22.0 0.1 iota_compare_fusion.1
  22.1 0.1 convert_reduce_fusion.3
  22.2 0.5 slice_bitcast_fusion
  22.7 27.1 %all-to-all-done = bf16[16,256,128]{2,1,0:T(8,128)(2,1)S(1)} async-done(((bf16[16,256,128]{2,1,0:T(8,128)(2,1)}), bf16[16,256,128]{2,1,0:T(8,128)(2,1)S(1)}, u32[]{:S(2)}, u32[]{:S(2)}) %all-to-all-start) | async-done | bytes 1048608 | tf_op jit(solution)/shard_map/all_to_all | solution.py:66
  49.8 0.0 copy-start.24
  49.8 0.6 copy-done.24
  50.5 3.9 %shard_map.147 = (bf16[4096,128]{1,0:T(8,128)(2,1)S(1)}, f32[256,128]{1,0:T(8,128)S(1)}, f32[256,128]{1,0:T(8,128)S(1)}, f32[256,128]{1,0:T(8,128)S(1)}) custom-call(f32[64]{0:T(128)S(1)} %copy-done.24, bf16[8192,128]{1,0:T(8,128)(2,1)S(1)} %shard_map.146.dense_ref, bf16[4096,128]{1,0:T(8,128)(2,1)S(1)} %bitcast.16, f32[256,128]{1,0:T(8,128)S(1)} %copy-done.7, ...), custom_call_target="tpu_custom_call" | custom-call | flops 805306368 | bytes 6291456 | tf_op jit(solution)/shard_map/pallas_call | solution.py:137
  54.4 0.0 copy-start.16
  54.4 0.0 copy-start.20
  54.4 0.0 copy-start.25
  54.4 37.8 %all_to_all.30 = bf16[16,256,128]{2,1,0:T(8,128)(2,1)S(1)} all-to-all(bf16[16,256,128]{2,1,0:T(8,128)(2,1)S(1)} %bitcast.18), channel_id=1, replica_groups=mesh['blk'=32,'narrow'=16] {'narrow'}, dimensions={0} | all-to-all | bytes 2097152 | tf_op jit(solution)/shard_map/all_to_all | solution.py:72
  92.3 0.1 convert_reduce_fusion.2
  92.4 0.0 copy-start.1
  92.4 0.8 divide_subtract_fusion.2
  93.2 2.1 collective-permute-start
  95.3 2.5 collective-permute-done
  97.8 0.7 copy-done.28
  98.5 1.2 broadcast_in_dim.7
  99.7 4.7 %all-to-all-start.2 = ((bf16[16,256,128]{2,1,0:T(8,128)(2,1)}), bf16[16,256,128]{2,1,0:T(8,128)(2,1)}, u32[]{:S(2)}, u32[]{:S(2)}) async-start(bf16[16,256,128]{2,1,0:T(8,128)(2,1)} %broadcast_in_dim.7), calls=%async_computation.2 | async-start | bytes 2097152 | tf_op jit(solution)/shard_map/all_to_all | solution.py:66
  104.4 1.7 shard_map.148.dense_ref
  106.1 1.3 copy-done.4
  107.4 31.1 %all-to-all-done.2 = bf16[16,256,128]{2,1,0:T(8,128)(2,1)} async-done(((bf16[16,256,128]{2,1,0:T(8,128)(2,1)}), bf16[16,256,128]{2,1,0:T(8,128)(2,1)}, u32[]{:S(2)}, u32[]{:S(2)}) %all-to-all-start.2) | async-done | bytes 1048608 | tf_op jit(solution)/shard_map/all_to_all | solution.py:66
  138.5 1.6 copy-done.5
  140.1 0.9 copy-done.17
  141.0 0.9 copy-done.19
  141.9 0.9 copy-done.21
  142.8 0.6 copy-done.23
  143.4 4.6 %shard_map.149 = (bf16[4096,128]{1,0:T(8,128)(2,1)S(1)}, f32[256,128]{1,0:T(8,128)S(1)}, f32[256,128]{1,0:T(8,128)S(1)}, f32[256,128]{1,0:T(8,128)S(1)}) custom-call(f32[64]{0:T(128)S(1)} %copy-done.23, bf16[8192,128]{1,0:T(8,128)(2,1)S(1)} %copy-done.5, bf16[4096,128]{1,0:T(8,128)(2,1)} %bitcast.6.items_ref, f32[256,128]{1,0:T(8,128)S(1)} %copy-done.17, ...), custom_call_target="tpu_custom_call" | custom-call | flops 805306368 | bytes 6291456 | tf_op jit(solution)/shard_map/pallas_call | solution.py:137
  148.0 1.0 copy-done.6
  149.0 0.7 copy-done.10
  149.7 0.7 copy-done.12
  150.3 0.7 copy-done.14
  151.0 12.4 %all-to-all-start.3 = ((bf16[16,256,128]{2,1,0:T(8,128)(2,1)}), bf16[16,256,128]{2,1,0:T(8,128)(2,1)}, u32[]{:S(2)}, u32[]{:S(2)}) async-start(bf16[16,256,128]{2,1,0:T(8,128)(2,1)} %bitcast.17), calls=%async_computation.3 | async-start | bytes 2097152 | tf_op jit(solution)/shard_map/all_to_all | solution.py:72
  163.3 1.9 collective-permute-start.1
  165.3 1.9 collective-permute-start.2
  167.2 27.4 %all-to-all-done.3 = bf16[16,256,128]{2,1,0:T(8,128)(2,1)} async-done(((bf16[16,256,128]{2,1,0:T(8,128)(2,1)}), bf16[16,256,128]{2,1,0:T(8,128)(2,1)}, u32[]{:S(2)}, u32[]{:S(2)}) %all-to-all-start.3) | async-done | bytes 1048608 | tf_op jit(solution)/shard_map/all_to_all | solution.py:72
  194.6 1.4 convert_reduce_fusion.1
  196.0 1.8 divide_subtract_fusion.1
  197.8 1.9 collective-permute-start.3
  199.7 2.5 collective-permute-done.3
  202.2 0.7 copy-done.26
  202.9 1.2 broadcast_in_dim.8
  204.1 6.7 %all-to-all-start.4 = ((bf16[16,256,128]{2,1,0:T(8,128)(2,1)}), bf16[16,256,128]{2,1,0:T(8,128)(2,1)}, u32[]{:S(2)}, u32[]{:S(2)}) async-start(bf16[16,256,128]{2,1,0:T(8,128)(2,1)} %broadcast_in_dim.8), calls=%async_computation.4 | async-start | bytes 2097152 | tf_op jit(solution)/shard_map/all_to_all | solution.py:66
  210.8 1.5 shard_map.145.dense_ref
  212.3 1.3 copy-done.2
  213.6 28.5 %all-to-all-done.4 = bf16[16,256,128]{2,1,0:T(8,128)(2,1)} async-done(((bf16[16,256,128]{2,1,0:T(8,128)(2,1)}), bf16[16,256,128]{2,1,0:T(8,128)(2,1)}, u32[]{:S(2)}, u32[]{:S(2)}) %all-to-all-start.4) | async-done | bytes 1048608 | tf_op jit(solution)/shard_map/all_to_all | solution.py:66
  242.2 1.6 copy-done.3
  243.7 0.9 copy-done.11
  244.6 0.9 copy-done.13
  245.6 0.9 copy-done.15
  246.5 5.7 %shard_map.150 = (bf16[4096,128]{1,0:T(8,128)(2,1)}, f32[256,128]{1,0:T(8,128)}, f32[256,128]{1,0:T(8,128)}, f32[256,128]{1,0:T(8,128)}) custom-call(f32[64]{0:T(128)S(1)} %get-tuple-element.41.counts_ref, bf16[8192,128]{1,0:T(8,128)(2,1)S(1)} %copy-done.3, bf16[4096,128]{1,0:T(8,128)(2,1)} %bitcast.8.items_ref, f32[256,128]{1,0:T(8,128)S(1)} %copy-done.11, ...), custom_call_target="tpu_custom_call" | custom-call | flops 805306368 | bytes 6291456 | tf_op jit(solution)/shard_map/pallas_call | solution.py:137
  252.2 5.3 %all-to-all-start.5 = ((bf16[16,256,128]{2,1,0:T(8,128)(2,1)}), bf16[16,256,128]{2,1,0:T(8,128)(2,1)S(1)}, u32[]{:S(2)}, u32[]{:S(2)}) async-start(bf16[16,256,128]{2,1,0:T(8,128)(2,1)} %bitcast.9), calls=%async_computation.5 | async-start | bytes 2097152 | tf_op jit(solution)/shard_map/all_to_all | solution.py:72
  257.5 1.9 collective-permute-start.4
  259.4 1.9 collective-permute-start.5
  261.3 27.0 %all-to-all-done.5 = bf16[16,256,128]{2,1,0:T(8,128)(2,1)S(1)} async-done(((bf16[16,256,128]{2,1,0:T(8,128)(2,1)}), bf16[16,256,128]{2,1,0:T(8,128)(2,1)S(1)}, u32[]{:S(2)}, u32[]{:S(2)}) %all-to-all-start.5) | async-done | bytes 1048608 | tf_op jit(solution)/shard_map/all_to_all | solution.py:72
  288.3 0.1 convert_reduce_fusion
  288.5 0.8 divide_subtract_fusion
  (54 shorter events, 0.1 us)
Async XLA Ops:
  0.6 17.8 %copy-start.34 = (s32[1,1,3,36]{3,1,2,0:T(1,128)S(1)}, s32[1,1,3,36]{3,1,2,0:T(1,128)}, u32[]{:S(2)}) copy-start(s32[1,1,3,36]{3,1,2,0:T(1,128)} %param.17) | copy-start | bytes 1300
  0.6 17.8 %copy-start.33 = (s32[1,1,3,36]{3,1,2,0:T(1,128)S(1)}, s32[1,1,3,36]{3,1,2,0:T(1,128)}, u32[]{:S(2)}) copy-start(s32[1,1,3,36]{3,1,2,0:T(1,128)} %param.18) | copy-start | bytes 1300
  0.7 18.0 %copy-start.22 = (s32[1,1,3]{2,1,0:T(1,128)S(1)}, s32[1,1,3]{2,1,0:T(1,128)}, u32[]{:S(2)}) copy-start(s32[1,1,3]{2,1,0:T(1,128)} %param.19) | copy-start | bytes 40
  2.8 47.0 %all-to-all-start = ((bf16[16,256,128]{2,1,0:T(8,128)(2,1)}), bf16[16,256,128]{2,1,0:T(8,128)(2,1)S(1)}, u32[]{:S(2)}, u32[]{:S(2)}) async-start(bf16[16,256,128]{2,1,0:T(8,128)(2,1)} %broadcast_in_dim.6), calls=%async_computation | async-start | bytes 2097152 | tf_op jit(solution)/shard_map/all_to_all | solution.py:66
  18.7 2.0 copy-start
  20.7 29.1 %copy-start.7 = (f32[256,128]{1,0:T(8,128)S(1)}, f32[256,128]{1,0:T(8,128)}, u32[]{:S(2)}) copy-start(f32[256,128]{1,0:T(8,128)} %fac_ref.1) | copy-start | bytes 393220
  20.7 29.1 %copy-start.8 = (f32[256,128]{1,0:T(8,128)S(1)}, f32[256,128]{1,0:T(8,128)}, u32[]{:S(2)}) copy-start(f32[256,128]{1,0:T(8,128)} %first_ref.1) | copy-start | bytes 393220
  20.7 29.1 %copy-start.9 = (f32[256,128]{1,0:T(8,128)S(1)}, f32[256,128]{1,0:T(8,128)}, u32[]{:S(2)}) copy-start(f32[256,128]{1,0:T(8,128)} %second_ref.1) | copy-start | bytes 393220
  49.8 0.7 copy-start.24
  54.4 38.9 %copy-start.16 = (f32[256,128]{1,0:T(8,128)}, f32[256,128]{1,0:T(8,128)S(1)}, u32[]{:S(2)}) copy-start(f32[256,128]{1,0:T(8,128)S(1)} %get-tuple-element.19.fac_ref) | copy-start | bytes 393220
  54.4 38.8 %copy-start.18 = (f32[256,128]{1,0:T(8,128)}, f32[256,128]{1,0:T(8,128)S(1)}, u32[]{:S(2)}) copy-start(f32[256,128]{1,0:T(8,128)S(1)} %get-tuple-element.20.first_ref) | copy-start | bytes 393220
  54.4 38.8 %copy-start.20 = (f32[256,128]{1,0:T(8,128)}, f32[256,128]{1,0:T(8,128)S(1)}, u32[]{:S(2)}) copy-start(f32[256,128]{1,0:T(8,128)S(1)} %get-tuple-element.21.second_ref) | copy-start | bytes 393220
  54.4 38.0 %copy-start.25 = (f32[256,128]{1,0:T(8,128)S(1)}, f32[256,128]{1,0:T(8,128)}, u32[]{:S(2)}) copy-start(f32[256,128]{1,0:T(8,128)} %param.13) | copy-start | bytes 393220
  54.4 38.0 %copy-start.29 = (f32[256,128]{1,0:T(8,128)S(1)}, f32[256,128]{1,0:T(8,128)}, u32[]{:S(2)}) copy-start(f32[256,128]{1,0:T(8,128)} %param.14) | copy-start | bytes 393220
  54.4 38.0 %copy-start.30 = (f32[256,128]{1,0:T(8,128)S(1)}, f32[256,128]{1,0:T(8,128)}, u32[]{:S(2)}) copy-start(f32[256,128]{1,0:T(8,128)} %param.15) | copy-start | bytes 393220
  92.4 11.9 %copy-start.1 = (bf16[1,1,3,36,128,128]{5,4,3,2,1,0:T(8,128)(2,1)S(1)}, bf16[1,1,3,36,128,128]{5,4,3,2,1,0:T(8,128)(2,1)}, u32[]{:S(2)}) copy-start(bf16[1,1,3,36,128,128]{5,4,3,2,1,0:T(8,128)(2,1)} %ratings.5) | copy-start | bytes 10616836
  93.2 4.6 %collective-permute-start = (f32[256,128]{1,0:T(8,128)S(1)}, f32[256,128]{1,0:T(8,128)S(1)}, u32[]{:S(2)}, u32[]{:S(2)}) collective-permute-start(f32[256,128]{1,0:T(8,128)S(1)} %get-tuple-element.36), channel_id=1, source_target_pairs={{16,0},{32,16},{48,32},{64,48},{80,64},{96,80},{112,96},{128,112},... | collective-permute-start | bytes 393224 | tf_op jit(solution)/shard_map/ppermute | solution.py:60
  97.8 0.7 copy-start.28
  99.7 38.9 %all-to-all-start.2 = ((bf16[16,256,128]{2,1,0:T(8,128)(2,1)}), bf16[16,256,128]{2,1,0:T(8,128)(2,1)}, u32[]{:S(2)}, u32[]{:S(2)}) async-start(bf16[16,256,128]{2,1,0:T(8,128)(2,1)} %broadcast_in_dim.7), calls=%async_computation.2 | async-start | bytes 2097152 | tf_op jit(solution)/shard_map/all_to_all | solution.py:66
  106.1 1.4 copy-start.4
  138.5 1.6 copy-start.5
  140.1 0.9 copy-start.17
  141.0 0.9 copy-start.19
  141.9 0.9 copy-start.21
  142.8 0.6 copy-start.23
  148.0 1.0 copy-start.6
  149.0 0.7 copy-start.10
  149.7 0.7 copy-start.12
  150.3 0.7 copy-start.14
  151.0 43.6 %all-to-all-start.3 = ((bf16[16,256,128]{2,1,0:T(8,128)(2,1)}), bf16[16,256,128]{2,1,0:T(8,128)(2,1)}, u32[]{:S(2)}, u32[]{:S(2)}) async-start(bf16[16,256,128]{2,1,0:T(8,128)(2,1)} %bitcast.17), calls=%async_computation.3 | async-start | bytes 2097152 | tf_op jit(solution)/shard_map/all_to_all | solution.py:72
  163.3 32.6 %collective-permute-start.1 = (f32[256,128]{1,0:T(8,128)}, f32[256,128]{1,0:T(8,128)}, u32[]{:S(2)}, u32[]{:S(2)}) collective-permute-start(f32[256,128]{1,0:T(8,128)} %get-tuple-element.37), channel_id=1, source_target_pairs={{16,0},{32,16},{48,32},{64,48},{80,64},{96,80},{112,96},{128,112},... | collective-permute-start | bytes 393224 | tf_op jit(solution)/shard_map/ppermute | solution.py:60
  165.3 30.7 %collective-permute-start.2 = (f32[256,128]{1,0:T(8,128)}, f32[256,128]{1,0:T(8,128)}, u32[]{:S(2)}, u32[]{:S(2)}) collective-permute-start(f32[256,128]{1,0:T(8,128)} %get-tuple-element.38), channel_id=1, source_target_pairs={{16,0},{32,16},{48,32},{64,48},{80,64},{96,80},{112,96},{128,112},... | collective-permute-start | bytes 393224 | tf_op jit(solution)/shard_map/ppermute | solution.py:60
  197.8 4.4 %collective-permute-start.3 = (f32[256,128]{1,0:T(8,128)S(1)}, f32[256,128]{1,0:T(8,128)S(1)}, u32[]{:S(2)}, u32[]{:S(2)}) collective-permute-start(f32[256,128]{1,0:T(8,128)S(1)} %get-tuple-element.33), channel_id=1, source_target_pairs={{16,0},{32,16},{48,32},{64,48},{80,64},{96,80},{112,96},{128,112},... | collective-permute-start | bytes 393224 | tf_op jit(solution)/shard_map/ppermute | solution.py:60
  202.2 0.7 copy-start.26
  204.1 38.1 %all-to-all-start.4 = ((bf16[16,256,128]{2,1,0:T(8,128)(2,1)}), bf16[16,256,128]{2,1,0:T(8,128)(2,1)}, u32[]{:S(2)}, u32[]{:S(2)}) async-start(bf16[16,256,128]{2,1,0:T(8,128)(2,1)} %broadcast_in_dim.8), calls=%async_computation.4 | async-start | bytes 2097152 | tf_op jit(solution)/shard_map/all_to_all | solution.py:66
  212.3 1.4 copy-start.2
  242.1 1.6 copy-start.3
  243.7 0.9 copy-start.11
  244.6 0.9 copy-start.13
  245.5 0.9 copy-start.15
  246.5 11.0 %copy-start.32 = (f32[256,128]{1,0:T(8,128)S(1)}, f32[256,128]{1,0:T(8,128)}, u32[]{:S(2)}) copy-start(f32[256,128]{1,0:T(8,128)} %get-tuple-element.34) | copy-start | bytes 393220
  246.5 12.9 %copy-start.31 = (f32[256,128]{1,0:T(8,128)S(1)}, f32[256,128]{1,0:T(8,128)}, u32[]{:S(2)}) copy-start(f32[256,128]{1,0:T(8,128)} %get-tuple-element.35) | copy-start | bytes 393220
  252.2 36.3 %copy-start.27 = (f32[256,128]{1,0:T(8,128)S(1)}, f32[256,128]{1,0:T(8,128)}, u32[]{:S(2)}) copy-start(f32[256,128]{1,0:T(8,128)} %copy-done.26) | copy-start | bytes 393220
  252.2 36.1 %all-to-all-start.5 = ((bf16[16,256,128]{2,1,0:T(8,128)(2,1)}), bf16[16,256,128]{2,1,0:T(8,128)(2,1)S(1)}, u32[]{:S(2)}, u32[]{:S(2)}) async-start(bf16[16,256,128]{2,1,0:T(8,128)(2,1)} %bitcast.9), calls=%async_computation.5 | async-start | bytes 2097152 | tf_op jit(solution)/shard_map/all_to_all | solution.py:72
  257.5 31.0 %collective-permute-start.4 = (f32[256,128]{1,0:T(8,128)S(1)}, f32[256,128]{1,0:T(8,128)S(1)}, u32[]{:S(2)}, u32[]{:S(2)}) collective-permute-start(f32[256,128]{1,0:T(8,128)S(1)} %copy-done.32), channel_id=1, source_target_pairs={{16,0},{32,16},{48,32},{64,48},{80,64},{96,80},{112,96},{128,112},... | collective-permute-start | bytes 393224 | tf_op jit(solution)/shard_map/ppermute | solution.py:60
  259.4 29.0 %collective-permute-start.5 = (f32[256,128]{1,0:T(8,128)S(1)}, f32[256,128]{1,0:T(8,128)S(1)}, u32[]{:S(2)}, u32[]{:S(2)}) collective-permute-start(f32[256,128]{1,0:T(8,128)S(1)} %copy-done.31), channel_id=1, source_target_pairs={{16,0},{32,16},{48,32},{64,48},{80,64},{96,80},{112,96},{128,112},... | collective-permute-start | bytes 393224 | tf_op jit(solution)/shard_map/ppermute | solution.py:60
